TPU v7x, 32 devices: a whole 2x2x4 slice. The times are simulated.
32 devices in a mesh: rows: 8 (over y, x, core), sub: 4 (over z).
Axes of the slice: x: 2, y: 2, z: 4, core: 2. Of those that a mesh axis runs over, the one named last changes fastest.
Arguments:
- right_sides: float32 [32768, 512], P(('rows', 'sub')), may hold values from -6 to 6
- bases_u: float32 [4, 32768, 256], P(None, ('rows', 'sub')), may hold values from -0.375 to 0.375
- bases_v: float32 [4, 32768, 256], P(None, ('rows', 'sub')), may hold values from -0.046875 to 0.046875
- couple_first: float32 [512, 512], P(('rows', 'sub')), may hold values from -0.25 to 0.25
- couple_second: float32 [1024, 512], P(('rows', 'sub')), may hold values from -0.25 to 0.25
- couple_third: float32 [2048, 512], P(('rows', 'sub')), may hold values from -0.25 to 0.25
- couple_fourth: float32 [4096, 512], P(('rows', 'sub')), may hold values from -0.25 to 0.25
Outputs:
- solved: float32 [32768, 512], P(('rows', 'sub'))
All inputs are finite; a program needn't handle non-finite values.
Results may differ from a plain program's by a relative error of at most 0.00013.
Values sent between devices are 32-bit elements; how exact they have to be, the bound alone decides.
No kernel may reach another device: no remote copies, remote signals or barrier semaphores. Data moves between devices by JAX's collectives and lax.ppermute only.
A program may use at most 64 MiB of HBM per device.

v0:
```python
import jax
import jax.numpy as jnp
from jax import lax
from jax.sharding import PartitionSpec as P

HIGHEST = lax.Precision.HIGHEST


def partner_2(x, axis, bit):
    return lax.ppermute(x, axis, [(i, i ^ 1 << bit) for i in range(lax.axis_size(axis))])


def contract(left, right):
    return lax.dot_general(
        left, right, (((0,), (0,)), ((), ())), precision=HIGHEST, preferred_element_type=jnp.float32
    )


def multiply(left, right):
    return jnp.dot(left, right, precision=HIGHEST, preferred_element_type=jnp.float32)


def partner_share(value, digit_place, sub_bits):
    if digit_place < sub_bits:
        return partner_2(value, "sub", digit_place)
    return partner_2(value, "rows", digit_place - sub_bits)


def partner_widen(value, digit_place, sub_bits):
    if digit_place < sub_bits:
        return partner_2(value, "sub", digit_place)
    return partner_2(value, "rows", digit_place - sub_bits)


def partner_coef(value, digit_place, sub_bits):
    if digit_place < sub_bits:
        return partner_2(value, "sub", digit_place)
    return partner_2(value, "rows", digit_place - sub_bits)


def my_digit(position, digit_place):
    return position // 2**digit_place % 2


def pair_of(own_sums, sibling, position, digit_place):
    lower_half = my_digit(position, digit_place) == 0
    return jnp.where(
        lower_half, jnp.concatenate([own_sums, sibling], 0), jnp.concatenate([sibling, own_sums], 0)
    )


def spread_coef(own_rows, position, child_bits, sub_bits):
    gathered = own_rows
    for digit_place in range(child_bits):
        partner = partner_coef(gathered, digit_place, sub_bits)
        lower_half = my_digit(position, digit_place) == 0
        gathered = jnp.where(
            lower_half,
            jnp.concatenate([gathered, partner], 0),
            jnp.concatenate([partner, gathered], 0),
        )
    return gathered


def local(right_sides, bases_u, bases_v, couple_first, couple_second, couple_third, couple_fourth):
    couples = (couple_first, couple_second, couple_third, couple_fourth)
    levels = bases_u.shape[0]
    sides = right_sides.shape[1]
    sub_bits = lax.axis_size("sub").bit_length() - 1
    total_bits = sub_bits + lax.axis_size("rows").bit_length() - 1
    position = lax.axis_index("rows") * lax.axis_size("sub") + lax.axis_index("sub")
    twos = (sides & -sides).bit_length() - 1
    whole_couples = []
    for depth_index in range(levels):
        child_bits = total_bits - depth_index - 1
        whole_couples.append(spread_coef(couples[depth_index], position, child_bits, sub_bits))
    solved = right_sides
    for depth_index in range(levels):
        child_bits = total_bits - depth_index - 1
        halvings = min(child_bits, twos)
        partial_value = contract(bases_v[depth_index], solved)
        for digit_place in range(halvings):
            width = partial_value.shape[1] // 2
            lower_half = my_digit(position, digit_place) == 0
            first = partial_value[:, :width]
            second = partial_value[:, width:]
            keep = jnp.where(lower_half, first, second)
            outgoing = jnp.where(lower_half, second, first)
            partial_value = keep + partner_share(outgoing, digit_place, sub_bits)
        sibling = partner_share(partial_value, child_bits, sub_bits)
        paired = pair_of(partial_value, sibling, position, child_bits)
        share = multiply(whole_couples[depth_index], paired)
        for digit_place in reversed(range(halvings)):
            partner = partner_widen(share, digit_place, sub_bits)
            lower_half = my_digit(position, digit_place) == 0
            share = jnp.where(
                lower_half,
                jnp.concatenate([share, partner], 1),
                jnp.concatenate([partner, share], 1),
            )
        solved = solved - multiply(bases_u[depth_index], share)
    return solved


def solution(mesh):
    placed = (
        P(("rows", "sub"), None),
        P(None, ("rows", "sub"), None),
        P(None, ("rows", "sub"), None),
        P(("rows", "sub"), None),
        P(("rows", "sub"), None),
        P(("rows", "sub"), None),
        P(("rows", "sub"), None),
    )
    return jax.shard_map(
        local, mesh=mesh, in_specs=placed, out_specs=P(("rows", "sub"), None), check_vma=False
    )
```

profile of v0, /device:TPU:0, one launch (start us, length us, event | category | flops | bytes accessed | tf_op | source)
XLA Modules:
  0.0 198.2 jit_solution(14430030261590698818)
XLA Ops:
  0.0 3.9 %fusion.7 = f32[256,512]{1,0:T(8,128)S(1)} fusion(f32[1024,512]{1,0:T(8,128)} %param.7, f32[4,1024,256]{2,1,0:T(8,128)} %param.9), kind=kOutput, calls=%fused_computation.14 | convolution fusion | flops 1610612736 | bytes 3670016 | tf_op jit(solution)/shard_map/dot_general | solution.py:14
  3.9 3.1 %collective-permute-start.4 = (f32[256,256]{1,0:T(8,128)S(1)}, f32[256,256]{1,0:T(8,128)S(1)}, u32[]{:S(2)}, u32[]{:S(2)}) collective-permute-start(f32[256,256]{1,0:T(8,128)S(1)} %slice_select_fusion.3), channel_id=1, source_target_pairs={{0,1},{1,0},{2,3},{3,2},{4,5},{5,4},{6,7},{7,6},{8,9},{9,8},{10,11... | collective-permute-start | bytes 786440 | tf_op jit(solution)/shard_map/ppermute | solution.py:10
  7.1 6.6 %collective-permute-done.4 = f32[256,256]{1,0:T(8,128)S(1)} collective-permute-done((f32[256,256]{1,0:T(8,128)S(1)}, f32[256,256]{1,0:T(8,128)S(1)}, u32[]{:S(2)}, u32[]{:S(2)}) %collective-permute-start.4) | collective-permute-done | bytes 262176 | tf_op jit(solution)/shard_map/ppermute | solution.py:10
  13.7 2.8 %collective-permute-start.5 = (f32[256,128]{1,0:T(8,128)S(1)}, f32[256,128]{1,0:T(8,128)S(1)}, u32[]{:S(2)}, u32[]{:S(2)}) collective-permute-start(f32[256,128]{1,0:T(8,128)S(1)} %slice_select_fusion.9), channel_id=1, source_target_pairs={{0,2},{1,3},{2,0},{3,1},{4,6},{5,7},{6,4},{7,5},{8,10},{9,11},{10,... | collective-permute-start | bytes 393224 | tf_op jit(solution)/shard_map/ppermute | solution.py:10
  16.8 7.1 %collective-permute-done.5 = f32[256,128]{1,0:T(8,128)S(1)} collective-permute-done((f32[256,128]{1,0:T(8,128)S(1)}, f32[256,128]{1,0:T(8,128)S(1)}, u32[]{:S(2)}, u32[]{:S(2)}) %collective-permute-start.5) | collective-permute-done | bytes 131104 | tf_op jit(solution)/shard_map/ppermute | solution.py:10
  25.7 1.4 collective-permute-start.7
  27.9 4.2 %collective-permute-done.7 = f32[256,32]{1,0:T(8,128)S(1)} collective-permute-done((f32[256,32]{1,0:T(8,128)S(1)}, f32[256,32]{1,0:T(8,128)S(1)}, u32[]{:S(2)}, u32[]{:S(2)}) %collective-permute-start.7) | collective-permute-done | bytes 32800 | tf_op jit(solution)/shard_map/ppermute | solution.py:10
  32.2 1.4 collective-permute-start.8
  33.7 3.5 %collective-permute-done.8 = f32[256,32]{1,0:T(8,128)S(1)} collective-permute-done((f32[256,32]{1,0:T(8,128)S(1)}, f32[256,32]{1,0:T(8,128)S(1)}, u32[]{:S(2)}, u32[]{:S(2)}) %collective-permute-start.8) | collective-permute-done | bytes 32800 | tf_op jit(solution)/shard_map/ppermute | solution.py:10
  37.9 1.4 collective-permute-start.9
  39.3 2.6 %collective-permute-done.9 = f32[256,32]{0,1:T(8,128)S(1)} collective-permute-done((f32[256,32]{0,1:T(8,128)S(1)}, f32[256,32]{0,1:T(8,128)S(1)}, u32[]{:S(2)}, u32[]{:S(2)}) %collective-permute-start.9) | collective-permute-done | bytes 32800 | tf_op jit(solution)/shard_map/ppermute | solution.py:10
  42.0 1.2 collective-permute-done.10
  43.3 9.3 %collective-permute-done.11 = f32[256,128]{0,1:T(8,128)S(1)} collective-permute-done((f32[256,128]{0,1:T(8,128)S(1)}, f32[256,128]{0,1:T(8,128)S(1)}, u32[]{:S(2)}, u32[]{:S(2)}) %collective-permute-start.11) | collective-permute-done | bytes 131104 | tf_op jit(solution)/shard_map/ppermute | solution.py:10
  52.6 2.1 %copy.18 = f32[1024,512]{0,1:T(8,128)S(1)} copy(f32[1024,512]{1,0:T(8,128)} %param.7) | data formatting | bytes 4194304 | tf_op args[0]
  54.8 5.8 %collective-permute-done.12 = f32[256,256]{0,1:T(8,128)S(1)} collective-permute-done((f32[256,256]{0,1:T(8,128)S(1)}, f32[256,256]{0,1:T(8,128)S(1)}, u32[]{:S(2)}, u32[]{:S(2)}) %collective-permute-start.12) | collective-permute-done | bytes 262176 | tf_op jit(solution)/shard_map/ppermute | solution.py:10
  60.6 3.2 %bitcast_subtract_fusion.3 = f32[1024,512]{0,1:T(8,128)S(1)} fusion(f32[1024,512]{0,1:T(8,128)S(1)} %copy.18, f32[4,1024,256]{2,1,0:T(8,128)} %param.8, f32[256,256]{0,1:T(8,128)S(1)} %collective-permute-done.12, f32[256,256]{0,1:T(8,128)S(1)} %maximum_select_fusion.19, pred[]{:T(512)S(6)} %eq.79), kind=kOutput, calls=%fused_computation.3 | convolution fusion | flops 1611530240 | bytes 5767169 | tf_op jit(solution)/shard_map/dot_general | solution.py:20
  63.9 2.1 %convolution_bitcast_fusion.2 = f32[256,512]{1,0:T(8,128)S(1)} fusion(f32[1024,512]{0,1:T(8,128)S(1)} %bitcast_subtract_fusion.3, f32[4,1024,256]{2,1,0:T(8,128)S(1)} %copy-done), kind=kOutput, calls=%fused_computation.6 | convolution fusion | flops 1610612736 | bytes 3670016 | tf_op jit(solution)/shard_map/dot_general | solution.py:14
  66.4 1.7 collective-permute-start.13
  68.1 5.8 %collective-permute-done.16 = f32[256,256]{1,0:T(8,128)S(1)} collective-permute-done((f32[256,256]{1,0:T(8,128)S(1)}, f32[256,256]{1,0:T(8,128)S(1)}, u32[]{:S(2)}, u32[]{:S(2)}) %collective-permute-start.16) | collective-permute-done | bytes 262176 | tf_op jit(solution)/shard_map/ppermute | solution.py:10
  74.0 1.0 collective-permute-start.17
  75.0 2.1 %collective-permute-start.14 = (f32[64,512]{1,0:T(8,128)S(1)}, f32[64,512]{1,0:T(8,128)S(1)}, u32[]{:S(2)}, u32[]{:S(2)}) collective-permute-start(f32[64,512]{1,0:T(8,128)S(1)} %maximum_select_fusion.30), channel_id=1, source_target_pairs={{0,2},{1,3},{2,0},{3,1},{4,6},{5,7},{6,4},{7,5},{8,10},{9,11},{10,... | collective-permute-start | bytes 393224 | tf_op jit(solution)/shard_map/ppermute | solution.py:10
  77.1 7.1 %collective-permute-done.17 = f32[256,128]{1,0:T(8,128)S(1)} collective-permute-done((f32[256,128]{1,0:T(8,128)S(1)}, f32[256,128]{1,0:T(8,128)S(1)}, u32[]{:S(2)}, u32[]{:S(2)}) %collective-permute-start.17) | collective-permute-done | bytes 131104 | tf_op jit(solution)/shard_map/ppermute | solution.py:10
  84.4 1.6 collective-permute-done.14
  86.3 1.0 collective-permute-start.19
  87.7 4.6 %collective-permute-done.19 = f32[256,64]{1,0:T(8,128)S(1)} collective-permute-done((f32[256,64]{1,0:T(8,128)S(1)}, f32[256,64]{1,0:T(8,128)S(1)}, u32[]{:S(2)}, u32[]{:S(2)}) %collective-permute-start.19) | collective-permute-done | bytes 65568 | tf_op jit(solution)/shard_map/ppermute | solution.py:10
  92.9 1.2 collective-permute-done.20
  94.2 8.7 %collective-permute-done.21 = f32[256,128]{0,1:T(8,128)S(1)} collective-permute-done((f32[256,128]{0,1:T(8,128)S(1)}, f32[256,128]{0,1:T(8,128)S(1)}, u32[]{:S(2)}, u32[]{:S(2)}) %collective-permute-start.21) | collective-permute-done | bytes 131104 | tf_op jit(solution)/shard_map/ppermute | solution.py:10
  103.0 8.2 %collective-permute-done.22 = f32[256,256]{0,1:T(8,128)S(1)} collective-permute-done((f32[256,256]{0,1:T(8,128)S(1)}, f32[256,256]{0,1:T(8,128)S(1)}, u32[]{:S(2)}, u32[]{:S(2)}) %collective-permute-start.22) | collective-permute-done | bytes 262176 | tf_op jit(solution)/shard_map/ppermute | solution.py:10
  111.3 1.9 bitcast_subtract_fusion.2
  113.2 2.1 %convolution_bitcast_fusion.1 = f32[256,512]{1,0:T(8,128)S(1)} fusion(f32[1024,512]{0,1:T(8,128)S(1)} %bitcast_subtract_fusion.2, f32[4,1024,256]{2,1,0:T(8,128)S(1)} %copy-done), kind=kOutput, calls=%fused_computation.5 | convolution fusion | flops 1610612736 | bytes 3670016 | tf_op jit(solution)/shard_map/dot_general | solution.py:14
  115.7 1.7 collective-permute-start.23
  117.4 6.8 %collective-permute-done.25 = f32[256,256]{1,0:T(8,128)S(1)} collective-permute-done((f32[256,256]{1,0:T(8,128)S(1)}, f32[256,256]{1,0:T(8,128)S(1)}, u32[]{:S(2)}, u32[]{:S(2)}) %collective-permute-start.25) | collective-permute-done | bytes 262176 | tf_op jit(solution)/shard_map/ppermute | solution.py:10
  124.3 1.0 collective-permute-start.26
  125.3 1.7 collective-permute-done.23
  127.4 10.3 %collective-permute-done.26 = f32[256,128]{1,0:T(8,128)S(1)} collective-permute-done((f32[256,128]{1,0:T(8,128)S(1)}, f32[256,128]{1,0:T(8,128)S(1)}, u32[]{:S(2)}, u32[]{:S(2)}) %collective-permute-start.26) | collective-permute-done | bytes 131104 | tf_op jit(solution)/shard_map/ppermute | solution.py:10
  137.8 3.7 %collective-permute-done.24 = f32[128,512]{1,0:T(8,128)S(1)} collective-permute-done((f32[128,512]{1,0:T(8,128)S(1)}, f32[128,512]{1,0:T(8,128)S(1)}, u32[]{:S(2)}, u32[]{:S(2)}) %collective-permute-start.24) | collective-permute-done | bytes 262176 | tf_op jit(solution)/shard_map/ppermute | solution.py:10
  142.3 6.9 %collective-permute-done.28 = f32[256,128]{0,1:T(8,128)S(1)} collective-permute-done((f32[256,128]{0,1:T(8,128)S(1)}, f32[256,128]{0,1:T(8,128)S(1)}, u32[]{:S(2)}, u32[]{:S(2)}) %collective-permute-start.28) | collective-permute-done | bytes 131104 | tf_op jit(solution)/shard_map/ppermute | solution.py:10
  149.3 7.4 %collective-permute-done.29 = f32[256,256]{0,1:T(8,128)S(1)} collective-permute-done((f32[256,256]{0,1:T(8,128)S(1)}, f32[256,256]{0,1:T(8,128)S(1)}, u32[]{:S(2)}, u32[]{:S(2)}) %collective-permute-start.29) | collective-permute-done | bytes 262176 | tf_op jit(solution)/shard_map/ppermute | solution.py:10
  156.7 2.2 %bitcast_subtract_fusion.1 = f32[1024,512]{0,1:T(8,128)S(1)} fusion(f32[1024,512]{0,1:T(8,128)S(1)} %bitcast_subtract_fusion.2, f32[4,1024,256]{2,1,0:T(8,128)S(1)} %copy-done.1, f32[256,256]{0,1:T(8,128)S(1)} %collective-permute-done.29, f32[256,256]{0,1:T(8,128)S(1)} %maximum_select_fusion.27, pred[]{:T(512)S(6)} %eq.79), kind=kOutput, calls=%fused_computation.1 | convolution fusion | flops 1611530240 | bytes 5767169 | tf_op jit(solution)/shard_map/dot_general | solution.py:20
  158.9 2.1 %convolution_bitcast_fusion = f32[256,512]{1,0:T(8,128)S(1)} fusion(f32[1024,512]{0,1:T(8,128)S(1)} %bitcast_subtract_fusion.1, f32[4,1024,256]{2,1,0:T(8,128)S(1)} %copy-done), kind=kOutput, calls=%fused_computation.4 | convolution fusion | flops 1610612736 | bytes 3670016 | tf_op jit(solution)/shard_map/dot_general | solution.py:14
  162.2 1.8 collective-permute-start.30
  164.0 10.0 %collective-permute-done.31 = f32[256,256]{1,0:T(8,128)S(1)} collective-permute-done((f32[256,256]{1,0:T(8,128)}, f32[256,256]{1,0:T(8,128)S(1)}, u32[]{:S(2)}, u32[]{:S(2)}) %collective-permute-start.31) | collective-permute-done | bytes 262176 | tf_op jit(solution)/shard_map/ppermute | solution.py:10
  174.1 2.7 %collective-permute-done.30 = f32[128,512]{0,1:T(8,128)S(1)} collective-permute-done((f32[128,512]{0,1:T(8,128)S(1)}, f32[128,512]{0,1:T(8,128)S(1)}, u32[]{:S(2)}, u32[]{:S(2)}) %collective-permute-start.30) | collective-permute-done | bytes 262176 | tf_op jit(solution)/shard_map/ppermute | solution.py:10
  176.9 6.5 %collective-permute-done.32 = f32[256,256]{1,0:T(8,128)S(1)} collective-permute-done((f32[256,256]{1,0:T(8,128)S(1)}, f32[256,256]{1,0:T(8,128)S(1)}, u32[]{:S(2)}, u32[]{:S(2)}) %collective-permute-start.32) | collective-permute-done | bytes 262176 | tf_op jit(solution)/shard_map/ppermute | solution.py:10
  183.4 1.0 fusion.50
  184.5 6.4 %collective-permute-done.33 = f32[256,256]{0,1:T(8,128)S(1)} collective-permute-done((f32[256,256]{0,1:T(8,128)S(1)}, f32[256,256]{0,1:T(8,128)S(1)}, u32[]{:S(2)}, u32[]{:S(2)}) %collective-permute-start.33) | collective-permute-done | bytes 262176 | tf_op jit(solution)/shard_map/ppermute | solution.py:10
  190.8 4.5 %bitcast_subtract_fusion = f32[1024,512]{0,1:T(8,128)} fusion(f32[1024,512]{0,1:T(8,128)S(1)} %bitcast_subtract_fusion.1, f32[4,1024,256]{2,1,0:T(8,128)} %param.8, f32[256,256]{0,1:T(8,128)S(1)} %collective-permute-done.33, f32[256,256]{0,1:T(8,128)S(1)} %fusion.50, pred[]{:T(512)S(6)} %eq.79), kind=kOutput, calls=%fused_computation | convolution fusion | flops 1611530240 | bytes 5767169 | tf_op jit(solution)/shard_map/dot_general | solution.py:20
  195.3 2.9 %copy.23 = f32[1024,512]{1,0:T(8,128)} copy(f32[1024,512]{0,1:T(8,128)} %bitcast_subtract_fusion) | data formatting | bytes 4194304 | tf_op jit(solution)/shard_map/sub | solution.py:101
  (81 shorter events, 9.3 us)
Async XLA Ops:
  0.0 7.0 %copy-start.5 = (f32[16,512]{1,0:T(8,128)S(1)}, f32[16,512]{1,0:T(8,128)}, u32[]{:S(2)}) copy-start(f32[16,512]{1,0:T(8,128)} %param.10) | copy-start | bytes 98308
  3.9 9.7 %collective-permute-start.4 = (f32[256,256]{1,0:T(8,128)S(1)}, f32[256,256]{1,0:T(8,128)S(1)}, u32[]{:S(2)}, u32[]{:S(2)}) collective-permute-start(f32[256,256]{1,0:T(8,128)S(1)} %slice_select_fusion.3), channel_id=1, source_target_pairs={{0,1},{1,0},{2,3},{3,2},{4,5},{5,4},{6,7},{7,6},{8,9},{9,8},{10,11... | collective-permute-start | bytes 786440 | tf_op jit(solution)/shard_map/ppermute | solution.py:10
  7.0 9.6 %collective-permute-start = (f32[16,512]{1,0:T(8,128)S(1)}, f32[16,512]{1,0:T(8,128)S(1)}, u32[]{:S(2)}, u32[]{:S(2)}) collective-permute-start(f32[16,512]{1,0:T(8,128)S(1)} %copy-done.5), channel_id=1, source_target_pairs={{0,1},{1,0},{2,3},{3,2},{4,5},{5,4},{6,7},{7,6},{8,9},{9,8},{10,11... | collective-permute-start | bytes 98312 | tf_op jit(solution)/shard_map/ppermute | solution.py:10
  13.7 10.2 %collective-permute-start.5 = (f32[256,128]{1,0:T(8,128)S(1)}, f32[256,128]{1,0:T(8,128)S(1)}, u32[]{:S(2)}, u32[]{:S(2)}) collective-permute-start(f32[256,128]{1,0:T(8,128)S(1)} %slice_select_fusion.9), channel_id=1, source_target_pairs={{0,2},{1,3},{2,0},{3,1},{4,6},{5,7},{6,4},{7,5},{8,10},{9,11},{10,... | collective-permute-start | bytes 393224 | tf_op jit(solution)/shard_map/ppermute | solution.py:10
  16.6 8.1 %collective-permute-start.1 = (f32[32,512]{1,0:T(8,128)S(1)}, f32[32,512]{1,0:T(8,128)S(1)}, u32[]{:S(2)}, u32[]{:S(2)}) collective-permute-start(f32[32,512]{1,0:T(8,128)S(1)} %maximum_select_fusion.32), channel_id=1, source_target_pairs={{0,2},{1,3},{2,0},{3,1},{4,6},{5,7},{6,4},{7,5},{8,10},{9,11},{10,... | collective-permute-start | bytes 196616 | tf_op jit(solution)/shard_map/ppermute | solution.py:10
  24.1 1.4 collective-permute-start.6
  24.7 2.4 %collective-permute-start.2 = (f32[64,512]{1,0:T(8,128)S(1)}, f32[64,512]{1,0:T(8,128)S(1)}, u32[]{:S(2)}, u32[]{:S(2)}) collective-permute-start(f32[64,512]{1,0:T(8,128)S(1)} %maximum_select_fusion.28), channel_id=1, source_target_pairs={{0,4},{4,0},{8,12},{12,8},{16,20},{20,16},{24,28},{28,24},{1,5},{5... | collective-permute-start | bytes 393224 | tf_op jit(solution)/shard_map/ppermute | solution.py:10
  25.7 6.4 %collective-permute-start.7 = (f32[256,32]{1,0:T(8,128)S(1)}, f32[256,32]{1,0:T(8,128)S(1)}, u32[]{:S(2)}, u32[]{:S(2)}) collective-permute-start(f32[256,32]{1,0:T(8,128)S(1)} %slice_select_fusion.7), channel_id=1, source_target_pairs={{0,8},{4,12},{8,0},{12,4},{16,24},{20,28},{24,16},{28,20},{1,9},{5... | collective-permute-start | bytes 98312 | tf_op jit(solution)/shard_map/ppermute | solution.py:10
  27.1 10.2 %collective-permute-start.3 = (f32[128,512]{1,0:T(8,128)S(1)}, f32[128,512]{1,0:T(8,128)S(1)}, u32[]{:S(2)}, u32[]{:S(2)}) collective-permute-start(f32[128,512]{1,0:T(8,128)S(1)} %maximum_select_fusion.18), channel_id=1, source_target_pairs={{0,8},{4,12},{8,0},{12,4},{16,24},{20,28},{24,16},{28,20},{1,9},{5... | collective-permute-start | bytes 786440 | tf_op jit(solution)/shard_map/ppermute | solution.py:10
  32.2 5.0 %collective-permute-start.8 = (f32[256,32]{1,0:T(8,128)S(1)}, f32[256,32]{1,0:T(8,128)S(1)}, u32[]{:S(2)}, u32[]{:S(2)}) collective-permute-start(f32[256,32]{1,0:T(8,128)S(1)} %select_add_fusion.7), channel_id=1, source_target_pairs={{0,16},{4,20},{8,24},{12,28},{16,0},{20,4},{24,8},{28,12},{1,17},{... | collective-permute-start | bytes 98312 | tf_op jit(solution)/shard_map/ppermute | solution.py:10
  37.9 4.0 %collective-permute-start.9 = (f32[256,32]{0,1:T(8,128)S(1)}, f32[256,32]{0,1:T(8,128)S(1)}, u32[]{:S(2)}, u32[]{:S(2)}) collective-permute-start(f32[256,32]{0,1:T(8,128)S(1)} %fusion.17), channel_id=1, source_target_pairs={{0,8},{4,12},{8,0},{12,4},{16,24},{20,28},{24,16},{28,20},{1,9},{5... | collective-permute-start | bytes 98312 | tf_op jit(solution)/shard_map/ppermute | solution.py:10
  41.9 1.3 collective-permute-start.10
  43.2 9.3 %collective-permute-start.11 = (f32[256,128]{0,1:T(8,128)S(1)}, f32[256,128]{0,1:T(8,128)S(1)}, u32[]{:S(2)}, u32[]{:S(2)}) collective-permute-start(f32[256,128]{0,1:T(8,128)S(1)} %maximum_select_fusion.29), channel_id=1, source_target_pairs={{0,2},{1,3},{2,0},{3,1},{4,6},{5,7},{6,4},{7,5},{8,10},{9,11},{10,... | collective-permute-start | bytes 393224 | tf_op jit(solution)/shard_map/ppermute | solution.py:10
  52.6 8.1 %collective-permute-start.12 = (f32[256,256]{0,1:T(8,128)S(1)}, f32[256,256]{0,1:T(8,128)S(1)}, u32[]{:S(2)}, u32[]{:S(2)}) collective-permute-start(f32[256,256]{0,1:T(8,128)S(1)} %maximum_select_fusion.19), channel_id=1, source_target_pairs={{0,1},{1,0},{2,3},{3,2},{4,5},{5,4},{6,7},{7,6},{8,9},{9,8},{10,11... | collective-permute-start | bytes 786440 | tf_op jit(solution)/shard_map/ppermute | solution.py:10
  54.8 9.1 %copy-start = (f32[4,1024,256]{2,1,0:T(8,128)S(1)}, f32[4,1024,256]{2,1,0:T(8,128)}, u32[]{:S(2)}) copy-start(f32[4,1024,256]{2,1,0:T(8,128)} %param.9) | copy-start | bytes 12582916
  63.8 2.5 %copy-start.4 = (f32[32,512]{1,0:T(8,128)S(1)}, f32[32,512]{1,0:T(8,128)}, u32[]{:S(2)}) copy-start(f32[32,512]{1,0:T(8,128)} %param.11) | copy-start | bytes 196612
  66.0 7.9 %collective-permute-start.16 = (f32[256,256]{1,0:T(8,128)S(1)}, f32[256,256]{1,0:T(8,128)S(1)}, u32[]{:S(2)}, u32[]{:S(2)}) collective-permute-start(f32[256,256]{1,0:T(8,128)S(1)} %slice_select_fusion.2), channel_id=1, source_target_pairs={{0,1},{1,0},{2,3},{3,2},{4,5},{5,4},{6,7},{7,6},{8,9},{9,8},{10,11... | collective-permute-start | bytes 786440 | tf_op jit(solution)/shard_map/ppermute | solution.py:10
  66.4 8.6 %collective-permute-start.13 = (f32[32,512]{1,0:T(8,128)S(1)}, f32[32,512]{1,0:T(8,128)S(1)}, u32[]{:S(2)}, u32[]{:S(2)}) collective-permute-start(f32[32,512]{1,0:T(8,128)S(1)} %copy-done.4), channel_id=1, source_target_pairs={{0,1},{1,0},{2,3},{3,2},{4,5},{5,4},{6,7},{7,6},{8,9},{9,8},{10,11... | collective-permute-start | bytes 196616 | tf_op jit(solution)/shard_map/ppermute | solution.py:10
  74.0 10.2 %collective-permute-start.17 = (f32[256,128]{1,0:T(8,128)S(1)}, f32[256,128]{1,0:T(8,128)S(1)}, u32[]{:S(2)}, u32[]{:S(2)}) collective-permute-start(f32[256,128]{1,0:T(8,128)S(1)} %slice_select_fusion.6), channel_id=1, source_target_pairs={{0,2},{1,3},{2,0},{3,1},{4,6},{5,7},{6,4},{7,5},{8,10},{9,11},{10,... | collective-permute-start | bytes 393224 | tf_op jit(solution)/shard_map/ppermute | solution.py:10
  74.9 36.3 %copy-start.1 = (f32[4,1024,256]{2,1,0:T(8,128)S(1)}, f32[4,1024,256]{2,1,0:T(8,128)}, u32[]{:S(2)}) copy-start(f32[4,1024,256]{2,1,0:T(8,128)} %param.8) | copy-start | bytes 12582916
  75.0 11.1 %collective-permute-start.14 = (f32[64,512]{1,0:T(8,128)S(1)}, f32[64,512]{1,0:T(8,128)S(1)}, u32[]{:S(2)}, u32[]{:S(2)}) collective-permute-start(f32[64,512]{1,0:T(8,128)S(1)} %maximum_select_fusion.30), channel_id=1, source_target_pairs={{0,2},{1,3},{2,0},{3,1},{4,6},{5,7},{6,4},{7,5},{8,10},{9,11},{10,... | collective-permute-start | bytes 393224 | tf_op jit(solution)/shard_map/ppermute | solution.py:10
  84.3 1.8 collective-permute-start.18
  86.1 1.6 collective-permute-start.15
  86.3 6.0 %collective-permute-start.19 = (f32[256,64]{1,0:T(8,128)S(1)}, f32[256,64]{1,0:T(8,128)S(1)}, u32[]{:S(2)}, u32[]{:S(2)}) collective-permute-start(f32[256,64]{1,0:T(8,128)S(1)} %select_add_fusion.5), channel_id=1, source_target_pairs={{0,8},{4,12},{8,0},{12,4},{16,24},{20,28},{24,16},{28,20},{1,9},{5... | collective-permute-start | bytes 196616 | tf_op jit(solution)/shard_map/ppermute | solution.py:10
  92.8 1.3 collective-permute-start.20
  94.2 8.7 %collective-permute-start.21 = (f32[256,128]{0,1:T(8,128)S(1)}, f32[256,128]{0,1:T(8,128)S(1)}, u32[]{:S(2)}, u32[]{:S(2)}) collective-permute-start(f32[256,128]{0,1:T(8,128)S(1)} %maximum_select_fusion.31), channel_id=1, source_target_pairs={{0,2},{1,3},{2,0},{3,1},{4,6},{5,7},{6,4},{7,5},{8,10},{9,11},{10,... | collective-permute-start | bytes 393224 | tf_op jit(solution)/shard_map/ppermute | solution.py:10
  102.9 8.3 %collective-permute-start.22 = (f32[256,256]{0,1:T(8,128)S(1)}, f32[256,256]{0,1:T(8,128)S(1)}, u32[]{:S(2)}, u32[]{:S(2)}) collective-permute-start(f32[256,256]{0,1:T(8,128)S(1)} %maximum_select_fusion.23), channel_id=1, source_target_pairs={{0,1},{1,0},{2,3},{3,2},{4,5},{5,4},{6,7},{7,6},{8,9},{9,8},{10,11... | collective-permute-start | bytes 786440 | tf_op jit(solution)/shard_map/ppermute | solution.py:10
  113.2 2.5 %copy-start.3 = (f32[64,512]{1,0:T(8,128)S(1)}, f32[64,512]{1,0:T(8,128)}, u32[]{:S(2)}) copy-start(f32[64,512]{1,0:T(8,128)} %param.12) | copy-start | bytes 393220
  115.3 8.9 %collective-permute-start.25 = (f32[256,256]{1,0:T(8,128)S(1)}, f32[256,256]{1,0:T(8,128)S(1)}, u32[]{:S(2)}, u32[]{:S(2)}) collective-permute-start(f32[256,256]{1,0:T(8,128)S(1)} %slice_select_fusion.1), channel_id=1, source_target_pairs={{0,1},{1,0},{2,3},{3,2},{4,5},{5,4},{6,7},{7,6},{8,9},{9,8},{10,11... | collective-permute-start | bytes 786440 | tf_op jit(solution)/shard_map/ppermute | solution.py:10
  115.7 11.3 %collective-permute-start.23 = (f32[64,512]{1,0:T(8,128)S(1)}, f32[64,512]{1,0:T(8,128)S(1)}, u32[]{:S(2)}, u32[]{:S(2)}) collective-permute-start(f32[64,512]{1,0:T(8,128)S(1)} %copy-done.3), channel_id=1, source_target_pairs={{0,1},{1,0},{2,3},{3,2},{4,5},{5,4},{6,7},{7,6},{8,9},{9,8},{10,11... | collective-permute-start | bytes 393224 | tf_op jit(solution)/shard_map/ppermute | solution.py:10
  124.3 13.4 %collective-permute-start.26 = (f32[256,128]{1,0:T(8,128)S(1)}, f32[256,128]{1,0:T(8,128)S(1)}, u32[]{:S(2)}, u32[]{:S(2)}) collective-permute-start(f32[256,128]{1,0:T(8,128)S(1)} %slice_select_fusion.4), channel_id=1, source_target_pairs={{0,2},{1,3},{2,0},{3,1},{4,6},{5,7},{6,4},{7,5},{8,10},{9,11},{10,... | collective-permute-start | bytes 393224 | tf_op jit(solution)/shard_map/ppermute | solution.py:10
  127.0 14.6 %collective-permute-start.24 = (f32[128,512]{1,0:T(8,128)S(1)}, f32[128,512]{1,0:T(8,128)S(1)}, u32[]{:S(2)}, u32[]{:S(2)}) collective-permute-start(f32[128,512]{1,0:T(8,128)S(1)} %maximum_select_fusion.24), channel_id=1, source_target_pairs={{0,2},{1,3},{2,0},{3,1},{4,6},{5,7},{6,4},{7,5},{8,10},{9,11},{10,... | collective-permute-start | bytes 786440 | tf_op jit(solution)/shard_map/ppermute | solution.py:10
  137.7 3.8 %collective-permute-start.27 = (f32[256,128]{1,0:T(8,128)S(1)}, f32[256,128]{1,0:T(8,128)S(1)}, u32[]{:S(2)}, u32[]{:S(2)}) collective-permute-start(f32[256,128]{1,0:T(8,128)S(1)} %select_add_fusion.4), channel_id=1, source_target_pairs={{0,4},{4,0},{8,12},{12,8},{16,20},{20,16},{24,28},{28,24},{1,5},{5... | collective-permute-start | bytes 393224 | tf_op jit(solution)/shard_map/ppermute | solution.py:10
  142.2 7.0 %collective-permute-start.28 = (f32[256,128]{0,1:T(8,128)S(1)}, f32[256,128]{0,1:T(8,128)S(1)}, u32[]{:S(2)}, u32[]{:S(2)}) collective-permute-start(f32[256,128]{0,1:T(8,128)S(1)} %fusion.39), channel_id=1, source_target_pairs={{0,2},{1,3},{2,0},{3,1},{4,6},{5,7},{6,4},{7,5},{8,10},{9,11},{10,... | collective-permute-start | bytes 393224 | tf_op jit(solution)/shard_map/ppermute | solution.py:10
  149.2 7.5 %collective-permute-start.29 = (f32[256,256]{0,1:T(8,128)S(1)}, f32[256,256]{0,1:T(8,128)S(1)}, u32[]{:S(2)}, u32[]{:S(2)}) collective-permute-start(f32[256,256]{0,1:T(8,128)S(1)} %maximum_select_fusion.27), channel_id=1, source_target_pairs={{0,1},{1,0},{2,3},{3,2},{4,5},{5,4},{6,7},{7,6},{8,9},{9,8},{10,11... | collective-permute-start | bytes 786440 | tf_op jit(solution)/shard_map/ppermute | solution.py:10
  158.8 3.2 %copy-start.2 = (f32[128,512]{1,0:T(8,128)S(1)}, f32[128,512]{1,0:T(8,128)}, u32[]{:S(2)}) copy-start(f32[128,512]{1,0:T(8,128)} %param.13) | copy-start | bytes 786436
  161.7 12.3 %collective-permute-start.31 = (f32[256,256]{1,0:T(8,128)}, f32[256,256]{1,0:T(8,128)S(1)}, u32[]{:S(2)}, u32[]{:S(2)}) collective-permute-start(f32[256,256]{1,0:T(8,128)} %slice_select_fusion), channel_id=1, source_target_pairs={{0,1},{1,0},{2,3},{3,2},{4,5},{5,4},{6,7},{7,6},{8,9},{9,8},{10,11... | collective-permute-start | bytes 786440 | tf_op jit(solution)/shard_map/ppermute | solution.py:10
  162.2 14.7 %collective-permute-start.30 = (f32[128,512]{0,1:T(8,128)S(1)}, f32[128,512]{0,1:T(8,128)S(1)}, u32[]{:S(2)}, u32[]{:S(2)}) collective-permute-start(f32[128,512]{0,1:T(8,128)S(1)} %copy.21), channel_id=1, source_target_pairs={{0,1},{1,0},{2,3},{3,2},{4,5},{5,4},{6,7},{7,6},{8,9},{9,8},{10,11... | collective-permute-start | bytes 786440 | tf_op jit(solution)/shard_map/ppermute | solution.py:10
  174.1 9.3 %collective-permute-start.32 = (f32[256,256]{1,0:T(8,128)S(1)}, f32[256,256]{1,0:T(8,128)S(1)}, u32[]{:S(2)}, u32[]{:S(2)}) collective-permute-start(f32[256,256]{1,0:T(8,128)S(1)} %select_add_fusion), channel_id=1, source_target_pairs={{0,2},{1,3},{2,0},{3,1},{4,6},{5,7},{6,4},{7,5},{8,10},{9,11},{10,... | collective-permute-start | bytes 786440 | tf_op jit(solution)/shard_map/ppermute | solution.py:10
  184.4 6.4 %collective-permute-start.33 = (f32[256,256]{0,1:T(8,128)S(1)}, f32[256,256]{0,1:T(8,128)S(1)}, u32[]{:S(2)}, u32[]{:S(2)}) collective-permute-start(f32[256,256]{0,1:T(8,128)S(1)} %fusion.50), channel_id=1, source_target_pairs={{0,1},{1,0},{2,3},{3,2},{4,5},{5,4},{6,7},{7,6},{8,9},{9,8},{10,11... | collective-permute-start | bytes 786440 | tf_op jit(solution)/shard_map/ppermute | solution.py:10
where the time goes:
time: 198 us
  waiting for transfers between devices  142 us (72%)
  matrix products  24.8 us (13%)
  starting transfers between devices  24.1 us (12%)
  local copies, waits for them, and re-layouts  5.27 us (3%)
    ppermute x34, waiting for transfers between devices, partner_2(): lax.ppermute(x, axis, [(i, i ^ 1 << bit) for i in range(lax.axis_size(axi...  142 us
    ppermute x34, starting transfers between devices, partner_2(): lax.ppermute(x, axis, [(i, i ^ 1 << bit) for i in range(lax.axis_size(axi...  24.1 us
    dot_general x8, matrix products, multiply(): jnp.dot(left, right, precision=HIGHEST, preferred_element_type=jnp.float32)  14.6 us
    dot_general x4, matrix products, contract(): lax.dot_general(left, right, (((0,), (0,)), ((), ())), precision=HIGHEST,...  10.2 us
  transfers between devices with their start and end apart: 34, of which 28 were waited for; matrix products, arithmetic and copies ran while one was open for 2% of the time, Pallas kernels for 0%

commit v1 on v0

v1 whole, which is shorter than its diff:
```python
import jax
import jax.numpy as jnp
from jax import lax
from jax.sharding import PartitionSpec as P

HIGH = lax.Precision.HIGH
CHUNKS = 1


def dot(left, right, left_dim, right_dim):
    return lax.dot_general(
        left, right, (((left_dim,), (right_dim,)), ((), ())), precision=HIGH, preferred_element_type=jnp.float32
    )


def bits_of(axis):
    return lax.axis_size(axis).bit_length() - 1


def swap(value, place):
    sub_bits = bits_of("sub")
    axis, bit = ("sub", place) if place < sub_bits else ("rows", place - sub_bits)
    return lax.ppermute(value, axis, [(i, i ^ 1 << bit) for i in range(lax.axis_size(axis))])


def digit(place):
    position = lax.axis_index("rows") * lax.axis_size("sub") + lax.axis_index("sub")
    return (position >> place) & 1


def halve(value, dim, place):
    first, second = jnp.split(value, 2, dim)
    lower = digit(place) == 0
    return jnp.where(lower, first, second) + swap(jnp.where(lower, second, first), place)


def ordered(own, other, dim, place):
    lower = digit(place) == 0
    return jnp.where(lower, jnp.concatenate([own, other], dim), jnp.concatenate([other, own], dim))


def widen(value, dim, place):
    return ordered(value, swap(value, place), dim, place)


def common_places(count):
    sub_bits = bits_of("sub")
    places = list(range(count))
    if count > sub_bits:
        places.remove(sub_bits)
        places.insert(0, sub_bits)
    return places


def gram(upper_u, lower_v, places, sibling_place):
    value = dot(lower_v, upper_u, 0, 0)
    for place in places:
        value = halve(value, 0, place)
    for place in reversed(places):
        value = widen(value, 0, place)
    return value, swap(value, sibling_place)


def level_pair(sums, grams, coupling, coupling_next, places, sibling_place):
    rank = sums.shape[2]
    for place in places:
        sums = halve(sums, 1, place)
    other = swap(sums, sibling_place)
    upper = sums[0] + other[0]
    pair = ordered(upper, swap(upper, sibling_place + 1), 1, sibling_place + 1)
    factors = dot(pair, coupling, 1, 1)
    own, sibling = (values[1] - dot(factors, each, 1, 1) for values, each in zip((sums, other), grams))
    factors_next = dot(ordered(own, sibling, 1, sibling_place), coupling_next, 1, 1)
    both = jnp.stack([factors, factors_next])
    for place in reversed(places):
        both = widen(both, 1, place)
    return both


def spread(rows, count):
    places = list(range(count))
    for place in places:
        rows = widen(rows, 0, place)
    return rows


def local(right_sides, bases_u, bases_v, couple_first, couple_second, couple_third, couple_fourth):
    couples = (couple_first, couple_second, couple_third, couple_fourth)
    levels = bases_u.shape[0]
    total_bits = bits_of("sub") + bits_of("rows")
    parts = jnp.split(right_sides, CHUNKS, 1)
    for level in range(0, levels, 2):
        sibling_place = total_bits - level - 2
        places = common_places(sibling_place)
        coupling = spread(couples[level], sibling_place + 1)
        coupling_next = spread(couples[level + 1], sibling_place)
        grams = gram(bases_u[level], bases_v[level + 1], places, sibling_place)
        for index, part in enumerate(parts):
            sums = jnp.stack([dot(part, bases_v[level + k], 0, 0) for k in range(2)])
            factors = level_pair(sums, grams, coupling, coupling_next, places, sibling_place)
            for k in range(2):
                part = part - dot(bases_u[level + k], factors[k], 1, 1)
            parts[index] = part
    return jnp.concatenate(parts, 1)


def solution(mesh):
    placed = (
        P(("rows", "sub"), None),
        P(None, ("rows", "sub"), None),
        P(None, ("rows", "sub"), None),
        P(("rows", "sub"), None),
        P(("rows", "sub"), None),
        P(("rows", "sub"), None),
        P(("rows", "sub"), None),
    )
    return jax.shard_map(
        local, mesh=mesh, in_specs=placed, out_specs=P(("rows", "sub"), None), check_vma=False
    )
```

time: 198 us -> 175 us (0.88)
  waiting for transfers between devices: 142 us -> 112 us
  other arithmetic: 1.9 us -> 5.34 us
  starting transfers between devices: 24.1 us -> 27.5 us
    ppermute x34 -> x32, waiting for transfers between devices: 142 us -> 112 us  [swap(): lax.ppermute(value, axis, [(i, i ^ 1 << bit) for i in range(lax.axis_size...]
    ppermute x34 -> x32, starting transfers between devices: 24.1 us -> 27.5 us  [swap(): lax.ppermute(value, axis, [(i, i ^ 1 << bit) for i in range(lax.axis_size...]
    select_n x22, other arithmetic: 1.36 us -> 3.85 us  [the longest x14 2.17 us: ordered(): jnp.where(lower, jnp.concatenate([own, other], dim), jnp.concatenate([oth...]
    dot_general x12 -> x18, matrix products: 24.8 us -> 23.9 us  [dot(): lax.dot_general(left, right, (((left_dim,), (right_dim,)), ((), ())), pre...]
  transfers between devices with their start and end apart: 34 -> 32, of which waited for: 28 -> 13; matrix products, arithmetic and copies ran while one was open for 2% -> 9% of each run, Pallas kernels for 0% -> 0%
where the time goes in v1:
time: 175 us; the launch traced here: 174 us
  waiting for transfers between devices  112 us (64%)
  starting transfers between devices  27.5 us (16%)
  matrix products  23.9 us (14%)
  other arithmetic  5.34 us (3%)
  local copies, waits for them, and re-layouts  4.9 us (3%)
    ppermute x32, waiting for transfers between devices, swap(): lax.ppermute(value, axis, [(i, i ^ 1 << bit) for i in range(lax.axis_size...  112 us
    ppermute x32, starting transfers between devices, swap(): lax.ppermute(value, axis, [(i, i ^ 1 << bit) for i in range(lax.axis_size...  27.5 us
    dot_general x18, matrix products, dot(): lax.dot_general(left, right, (((left_dim,), (right_dim,)), ((), ())), pre...  23.9 us
  transfers between devices with their start and end apart: 32, of which 13 were waited for; matrix products, arithmetic and copies ran while one was open for 9% of the time, Pallas kernels for 0%

profile of v1, /device:TPU:0, one launch (start us, length us, event | category | flops | bytes accessed | tf_op | source)
XLA Modules:
  0.0 174.2 jit_solution(2635760371041963862)
XLA Ops:
  0.0 2.7 %fusion.11 = f32[256,256]{1,0:T(8,128)S(1)} fusion(f32[4,1024,256]{2,1,0:T(8,128)} %param.8, f32[4,1024,256]{2,1,0:T(8,128)} %param.9), kind=kOutput, calls=%fused_computation.27 | convolution fusion | flops 402653184 | bytes 2359296 | tf_op jit(solution)/shard_map/dot_general | solution.py:11
  2.7 0.7 slice_select_fusion.2
  3.4 0.5 collective-permute-start.9
  3.8 2.6 %collective-permute-start.5 = (f32[16,512]{1,0:T(8,128)}, f32[16,512]{1,0:T(8,128)}, u32[]{:S(2)}, u32[]{:S(2)}) collective-permute-start(f32[16,512]{1,0:T(8,128)} %param.10), channel_id=1, source_target_pairs={{0,1},{1,0},{2,3},{3,2},{4,5},{5,4},{6,7},{7,6},{8,9},{9,8},{10,11... | collective-permute-start | bytes 98312 | tf_op jit(solution)/shard_map/ppermute | solution.py:23
  6.4 3.0 %convolution_bitcast_fusion.2 = f32[1,512,256]{2,1,0:T(8,128)S(1)} fusion(f32[1024,512]{1,0:T(8,128)S(1)} %copy-done, f32[4,1024,256]{2,1,0:T(8,128)} %param.9), kind=kOutput, calls=%fused_computation.6 | convolution fusion | flops 805306368 | bytes 3670016 | tf_op jit(solution)/shard_map/dot_general | solution.py:11
  9.4 3.0 %convolution_bitcast_fusion.3 = f32[1,512,256]{2,1,0:T(8,128)S(1)} fusion(f32[1024,512]{1,0:T(8,128)S(1)} %copy-done, f32[4,1024,256]{2,1,0:T(8,128)} %param.9), kind=kOutput, calls=%fused_computation.7 | convolution fusion | flops 805306368 | bytes 3670016 | tf_op jit(solution)/shard_map/dot_general | solution.py:11
  12.5 0.9 broadcast_select_fusion
  13.8 0.8 maximum_select_fusion.28
  14.7 2.8 %collective-permute-start.6 = (f32[32,512]{1,0:T(8,128)S(1)}, f32[32,512]{1,0:T(8,128)S(1)}, u32[]{:S(2)}, u32[]{:S(2)}) collective-permute-start(f32[32,512]{1,0:T(8,128)S(1)} %maximum_select_fusion.28), channel_id=1, source_target_pairs={{0,2},{1,3},{2,0},{3,1},{4,6},{5,7},{6,4},{7,5},{8,10},{9,11},{10,... | collective-permute-start | bytes 196616 | tf_op jit(solution)/shard_map/ppermute | solution.py:23
  17.6 1.6 collective-permute-start.10
  19.2 1.0 maximum_select_fusion.27
  20.2 2.2 %collective-permute-start.17 = (f32[64,512]{1,0:T(8,128)S(1)}, f32[64,512]{1,0:T(8,128)S(1)}, u32[]{:S(2)}, u32[]{:S(2)}) collective-permute-start(f32[64,512]{1,0:T(8,128)S(1)} %maximum_select_fusion.27), channel_id=1, source_target_pairs={{0,2},{1,3},{2,0},{3,1},{4,6},{5,7},{6,4},{7,5},{8,10},{9,11},{10,... | collective-permute-start | bytes 393224 | tf_op jit(solution)/shard_map/ppermute | solution.py:23
  22.4 1.1 collective-permute-start.11
  23.5 1.1 select_add_fusion.1
  24.7 0.9 collective-permute-start.1
  25.7 4.4 %collective-permute-done.11 = f32[32,256]{1,0:T(8,128)S(1)} collective-permute-done((f32[32,256]{1,0:T(8,128)S(1)}, f32[32,256]{1,0:T(8,128)S(1)}, u32[]{:S(2)}, u32[]{:S(2)}) %collective-permute-start.11) | collective-permute-done | bytes 32800 | tf_op jit(solution)/shard_map/ppermute | solution.py:23
  30.2 5.9 %collective-permute-done.1 = f32[2,128,256]{2,1,0:T(8,128)S(1)} collective-permute-done((f32[2,128,256]{2,1,0:T(8,128)S(1)}, f32[2,128,256]{2,1,0:T(8,128)S(1)}, u32[]{:S(2)}, u32[]{:S(2)}) %collective-permute-start.1) | collective-permute-done | bytes 262176 | tf_op jit(solution)/shard_map/ppermute | solution.py:23
  36.4 1.7 collective-permute-start.13
  38.1 5.7 %collective-permute-done.2 = f32[2,64,256]{2,1,0:T(8,128)S(1)} collective-permute-done((f32[2,64,256]{2,1,0:T(8,128)S(1)}, f32[2,64,256]{2,1,0:T(8,128)S(1)}, u32[]{:S(2)}, u32[]{:S(2)}) %collective-permute-start.2) | collective-permute-done | bytes 131104 | tf_op jit(solution)/shard_map/ppermute | solution.py:23
  43.8 1.6 collective-permute-start.3
  45.4 0.6 collective-permute-start.8
  46.1 4.1 %collective-permute-done.3 = f32[2,64,256]{2,1,0:T(8,128)S(1)} collective-permute-done((f32[2,64,256]{2,1,0:T(8,128)S(1)}, f32[2,64,256]{2,1,0:T(8,128)S(1)}, u32[]{:S(2)}, u32[]{:S(2)}) %collective-permute-start.3) | collective-permute-done | bytes 131104 | tf_op jit(solution)/shard_map/ppermute | solution.py:23
  50.3 1.6 collective-permute-start.4
  51.9 1.6 collective-permute-start.15
  53.5 2.4 %collective-permute-done.8 = f32[128,512]{1,0:T(8,128)S(1)} collective-permute-done((f32[128,512]{1,0:T(8,128)S(1)}, f32[128,512]{1,0:T(8,128)S(1)}, u32[]{:S(2)}, u32[]{:S(2)}) %collective-permute-start.8) | collective-permute-done | bytes 262176 | tf_op jit(solution)/shard_map/ppermute | solution.py:23
  56.6 4.0 %collective-permute-done.15 = f32[256,256]{1,0:T(8,128)S(1)} collective-permute-done((f32[256,256]{1,0:T(8,128)S(1)}, f32[256,256]{1,0:T(8,128)S(1)}, u32[]{:S(2)}, u32[]{:S(2)}) %collective-permute-start.15) | collective-permute-done | bytes 262176 | tf_op jit(solution)/shard_map/ppermute | solution.py:23
  61.4 6.1 %collective-permute-done.19 = f32[2,64,256]{2,1,0:T(8,128)S(1)} collective-permute-done((f32[2,64,256]{2,1,0:T(8,128)S(1)}, f32[2,64,256]{2,1,0:T(8,128)S(1)}, u32[]{:S(2)}, u32[]{:S(2)}) %collective-permute-start.19) | collective-permute-done | bytes 131104 | tf_op jit(solution)/shard_map/ppermute | solution.py:23
  67.5 7.1 %collective-permute-done.20 = f32[2,128,256]{2,1,0:T(8,128)S(1)} collective-permute-done((f32[2,128,256]{2,1,0:T(8,128)S(1)}, f32[2,128,256]{2,1,0:T(8,128)S(1)}, u32[]{:S(2)}, u32[]{:S(2)}) %collective-permute-start.20) | collective-permute-done | bytes 262176 | tf_op jit(solution)/shard_map/ppermute | solution.py:23
  74.7 2.0 %copy.8 = f32[1024,512]{0,1:T(8,128)} copy(f32[1024,512]{1,0:T(8,128)S(1)} %copy-done) | data formatting | bytes 4194304 | tf_op args[0]
  76.8 2.4 %fusion.9 = f32[512,1024]{1,0:T(8,128)S(1)} fusion(f32[4,1024,256]{2,1,0:T(8,128)} %param.8, f32[2,512,256]{2,1,0:T(8,128)S(1)} %maximum_select_fusion), kind=kOutput, calls=%fused_computation.25 | convolution fusion | flops 805306368 | bytes 3670016 | tf_op jit(solution)/shard_map/dot_general | solution.py:11
  79.3 3.0 %bitcast_subtract_fusion.2 = f32[1024,512]{0,1:T(8,128)S(1)} fusion(f32[1024,512]{0,1:T(8,128)} %copy.8, f32[512,1024]{1,0:T(8,128)S(1)} %fusion.9, f32[4,1024,256]{2,1,0:T(8,128)S(1)} %copy-done.2, f32[2,512,256]{2,1,0:T(8,128)S(1)} %maximum_select_fusion), kind=kOutput, calls=%fused_computation.2 | convolution fusion | flops 806354944 | bytes 7864320 | tf_op jit(solution)/shard_map/dot_general | solution.py:11
  82.3 1.0 convolution_bitcast_fusion
  83.4 1.0 convolution_bitcast_fusion.1
  84.8 1.7 collective-permute-start.25
  86.6 12.7 %collective-permute-done.22 = f32[2,256,256]{2,1,0:T(8,128)S(1)} collective-permute-done((f32[2,256,256]{2,1,0:T(8,128)S(1)}, f32[2,256,256]{2,1,0:T(8,128)S(1)}, u32[]{:S(2)}, u32[]{:S(2)}) %collective-permute-start.22) | collective-permute-done | bytes 524320 | tf_op jit(solution)/shard_map/ppermute | solution.py:23
  99.5 1.0 fusion.3
  100.6 2.0 %collective-permute-start.27 = (f32[128,256]{1,0:T(8,128)S(1)}, f32[128,256]{1,0:T(8,128)S(1)}, u32[]{:S(2)}, u32[]{:S(2)}) collective-permute-start(f32[128,256]{1,0:T(8,128)S(1)} %slice_select_fusion.1), channel_id=1, source_target_pairs={{0,1},{1,0},{2,3},{3,2},{4,5},{5,4},{6,7},{7,6},{8,9},{9,8},{10,11... | collective-permute-start | bytes 393224 | tf_op jit(solution)/shard_map/ppermute | solution.py:23
  102.6 1.3 collective-permute-start.26
  103.9 25.9 %collective-permute-done.23 = f32[2,256,256]{2,1,0:T(8,128)S(1)} collective-permute-done((f32[2,256,256]{2,1,0:T(8,128)S(1)}, f32[2,256,256]{2,1,0:T(8,128)S(1)}, u32[]{:S(2)}, u32[]{:S(2)}) %collective-permute-start.23) | collective-permute-done | bytes 524320 | tf_op jit(solution)/shard_map/ppermute | solution.py:23
  130.0 2.0 %collective-permute-start.30 = (f32[128,512]{1,0:T(8,128)S(1)}, f32[128,512]{1,0:T(8,128)S(1)}, u32[]{:S(2)}, u32[]{:S(2)}) collective-permute-start(f32[128,512]{1,0:T(8,128)S(1)} %copy-done.4), channel_id=1, source_target_pairs={{0,1},{1,0},{2,3},{3,2},{4,5},{5,4},{6,7},{7,6},{8,9},{9,8},{10,11... | collective-permute-start | bytes 786440 | tf_op jit(solution)/shard_map/ppermute | solution.py:23
  132.0 6.1 %collective-permute-done.28 = f32[128,256]{1,0:T(8,128)S(1)} collective-permute-done((f32[128,256]{1,0:T(8,128)S(1)}, f32[128,256]{1,0:T(8,128)S(1)}, u32[]{:S(2)}, u32[]{:S(2)}) %collective-permute-start.28) | collective-permute-done | bytes 131104 | tf_op jit(solution)/shard_map/ppermute | solution.py:23
  138.3 0.4 fusion.41
  139.1 13.9 %collective-permute-done.29 = f32[256,256]{1,0:T(8,128)S(1)} collective-permute-done((f32[256,256]{1,0:T(8,128)S(1)}, f32[256,256]{1,0:T(8,128)S(1)}, u32[]{:S(2)}, u32[]{:S(2)}) %collective-permute-start.29) | collective-permute-done | bytes 262176 | tf_op jit(solution)/shard_map/ppermute | solution.py:23
  153.3 0.4 convolution_bitcast_fusion.4
  153.8 13.7 %collective-permute-done.31 = f32[2,256,256]{2,1,0:T(8,128)S(1)} collective-permute-done((f32[2,256,256]{2,1,0:T(8,128)S(1)}, f32[2,256,256]{2,1,0:T(8,128)S(1)}, u32[]{:S(2)}, u32[]{:S(2)}) %collective-permute-start.31) | collective-permute-done | bytes 524320 | tf_op jit(solution)/shard_map/ppermute | solution.py:23
  167.6 1.1 fusion.1
  168.7 2.6 %bitcast_subtract_fusion = f32[1024,512]{0,1:T(8,128)} fusion(f32[1024,512]{0,1:T(8,128)S(1)} %bitcast_subtract_fusion.2, f32[512,1024]{1,0:T(8,128)S(1)} %fusion.1, f32[4,1024,256]{2,1,0:T(8,128)S(1)} %copy-done.2, f32[2,512,256]{2,1,0:T(8,128)S(1)} %maximum_select_fusion.1), kind=kOutput, calls=%fused_computation | convolution fusion | flops 806354944 | bytes 7864320 | tf_op jit(solution)/shard_map/dot_general | solution.py:11
  171.4 2.9 %copy.13 = f32[1024,512]{1,0:T(8,128)} copy(f32[1024,512]{0,1:T(8,128)} %bitcast_subtract_fusion) | data formatting | bytes 4194304 | tf_op jit(solution)/shard_map/sub | solution.py:102
  (80 shorter events, 4.7 us)
Async XLA Ops:
  0.0 6.4 %copy-start = (f32[1024,512]{1,0:T(8,128)S(1)}, f32[1024,512]{1,0:T(8,128)}, u32[]{:S(2)}) copy-start(f32[1024,512]{1,0:T(8,128)} %param.7) | copy-start | bytes 6291460
  3.4 14.2 %collective-permute-start.9 = (f32[128,256]{1,0:T(8,128)}, f32[128,256]{1,0:T(8,128)S(1)}, u32[]{:S(2)}, u32[]{:S(2)}) collective-permute-start(f32[128,256]{1,0:T(8,128)} %slice_select_fusion.2), channel_id=1, source_target_pairs={{0,4},{4,0},{8,12},{12,8},{16,20},{20,16},{24,28},{28,24},{1,5},{5... | collective-permute-start | bytes 393224 | tf_op jit(solution)/shard_map/ppermute | solution.py:23
  3.8 10.0 %collective-permute-start.5 = (f32[16,512]{1,0:T(8,128)}, f32[16,512]{1,0:T(8,128)}, u32[]{:S(2)}, u32[]{:S(2)}) collective-permute-start(f32[16,512]{1,0:T(8,128)} %param.10), channel_id=1, source_target_pairs={{0,1},{1,0},{2,3},{3,2},{4,5},{5,4},{6,7},{7,6},{8,9},{9,8},{10,11... | collective-permute-start | bytes 98312 | tf_op jit(solution)/shard_map/ppermute | solution.py:23
  13.3 10.2 %collective-permute-start = (f32[2,256,256]{2,1,0:T(8,128)}, f32[2,256,256]{2,1,0:T(8,128)}, u32[]{:S(2)}, u32[]{:S(2)}) collective-permute-start(f32[2,256,256]{2,1,0:T(8,128)} %broadcast_select_fusion), channel_id=1, source_target_pairs={{0,4},{4,0},{8,12},{12,8},{16,20},{20,16},{24,28},{28,24},{1,5},{5... | collective-permute-start | bytes 1572872 | tf_op jit(solution)/shard_map/ppermute | solution.py:23
  13.6 5.7 %collective-permute-start.16 = (f32[32,512]{1,0:T(8,128)}, f32[32,512]{1,0:T(8,128)}, u32[]{:S(2)}, u32[]{:S(2)}) collective-permute-start(f32[32,512]{1,0:T(8,128)} %param.11), channel_id=1, source_target_pairs={{0,1},{1,0},{2,3},{3,2},{4,5},{5,4},{6,7},{7,6},{8,9},{9,8},{10,11... | collective-permute-start | bytes 196616 | tf_op jit(solution)/shard_map/ppermute | solution.py:23
  14.7 10.9 %collective-permute-start.6 = (f32[32,512]{1,0:T(8,128)S(1)}, f32[32,512]{1,0:T(8,128)S(1)}, u32[]{:S(2)}, u32[]{:S(2)}) collective-permute-start(f32[32,512]{1,0:T(8,128)S(1)} %maximum_select_fusion.28), channel_id=1, source_target_pairs={{0,2},{1,3},{2,0},{3,1},{4,6},{5,7},{6,4},{7,5},{8,10},{9,11},{10,... | collective-permute-start | bytes 196616 | tf_op jit(solution)/shard_map/ppermute | solution.py:23
  17.6 4.8 %collective-permute-start.10 = (f32[64,256]{1,0:T(8,128)S(1)}, f32[64,256]{1,0:T(8,128)S(1)}, u32[]{:S(2)}, u32[]{:S(2)}) collective-permute-start(f32[64,256]{1,0:T(8,128)S(1)} %slice_select_fusion.4), channel_id=1, source_target_pairs={{0,1},{1,0},{2,3},{3,2},{4,5},{5,4},{6,7},{7,6},{8,9},{9,8},{10,11... | collective-permute-start | bytes 196616 | tf_op jit(solution)/shard_map/ppermute | solution.py:23
  20.2 16.0 %collective-permute-start.17 = (f32[64,512]{1,0:T(8,128)S(1)}, f32[64,512]{1,0:T(8,128)S(1)}, u32[]{:S(2)}, u32[]{:S(2)}) collective-permute-start(f32[64,512]{1,0:T(8,128)S(1)} %maximum_select_fusion.27), channel_id=1, source_target_pairs={{0,2},{1,3},{2,0},{3,1},{4,6},{5,7},{6,4},{7,5},{8,10},{9,11},{10,... | collective-permute-start | bytes 393224 | tf_op jit(solution)/shard_map/ppermute | solution.py:23
  22.4 7.7 %collective-permute-start.11 = (f32[32,256]{1,0:T(8,128)S(1)}, f32[32,256]{1,0:T(8,128)S(1)}, u32[]{:S(2)}, u32[]{:S(2)}) collective-permute-start(f32[32,256]{1,0:T(8,128)S(1)} %slice_select_fusion.5), channel_id=1, source_target_pairs={{0,2},{1,3},{2,0},{3,1},{4,6},{5,7},{6,4},{7,5},{8,10},{9,11},{10,... | collective-permute-start | bytes 98312 | tf_op jit(solution)/shard_map/ppermute | solution.py:23
  24.7 11.3 %collective-permute-start.1 = (f32[2,128,256]{2,1,0:T(8,128)S(1)}, f32[2,128,256]{2,1,0:T(8,128)S(1)}, u32[]{:S(2)}, u32[]{:S(2)}) collective-permute-start(f32[2,128,256]{2,1,0:T(8,128)S(1)} %slice_select_fusion), channel_id=1, source_target_pairs={{0,1},{1,0},{2,3},{3,2},{4,5},{5,4},{6,7},{7,6},{8,9},{9,8},{10,11... | collective-permute-start | bytes 786440 | tf_op jit(solution)/shard_map/ppermute | solution.py:23
  25.6 19.8 %collective-permute-start.7 = (f32[64,512]{1,0:T(8,128)S(1)}, f32[64,512]{1,0:T(8,128)S(1)}, u32[]{:S(2)}, u32[]{:S(2)}) collective-permute-start(f32[64,512]{1,0:T(8,128)S(1)} %maximum_select_fusion.23), channel_id=1, source_target_pairs={{0,4},{4,0},{8,12},{12,8},{16,20},{20,16},{24,28},{28,24},{1,5},{5... | collective-permute-start | bytes 393224 | tf_op jit(solution)/shard_map/ppermute | solution.py:23
  30.1 6.2 %collective-permute-start.12 = (f32[32,256]{1,0:T(8,128)S(1)}, f32[32,256]{1,0:T(8,128)S(1)}, u32[]{:S(2)}, u32[]{:S(2)}) collective-permute-start(f32[32,256]{1,0:T(8,128)S(1)} %select_add_fusion.7), channel_id=1, source_target_pairs={{0,2},{1,3},{2,0},{3,1},{4,6},{5,7},{6,4},{7,5},{8,10},{9,11},{10,... | collective-permute-start | bytes 98312 | tf_op jit(solution)/shard_map/ppermute | solution.py:23
  36.1 7.7 %collective-permute-start.2 = (f32[2,64,256]{2,1,0:T(8,128)S(1)}, f32[2,64,256]{2,1,0:T(8,128)S(1)}, u32[]{:S(2)}, u32[]{:S(2)}) collective-permute-start(f32[2,64,256]{2,1,0:T(8,128)S(1)} %slice_select_fusion.3), channel_id=1, source_target_pairs={{0,2},{1,3},{2,0},{3,1},{4,6},{5,7},{6,4},{7,5},{8,10},{9,11},{10,... | collective-permute-start | bytes 393224 | tf_op jit(solution)/shard_map/ppermute | solution.py:23
  36.2 24.6 %collective-permute-start.18 = (f32[128,512]{1,0:T(8,128)S(1)}, f32[128,512]{1,0:T(8,128)S(1)}, u32[]{:S(2)}, u32[]{:S(2)}) collective-permute-start(f32[128,512]{1,0:T(8,128)S(1)} %maximum_select_fusion.17), channel_id=1, source_target_pairs={{0,4},{4,0},{8,12},{12,8},{16,20},{20,16},{24,28},{28,24},{1,5},{5... | collective-permute-start | bytes 786440 | tf_op jit(solution)/shard_map/ppermute | solution.py:23
  36.4 9.7 %collective-permute-start.13 = (f32[64,256]{1,0:T(8,128)S(1)}, f32[64,256]{1,0:T(8,128)S(1)}, u32[]{:S(2)}, u32[]{:S(2)}) collective-permute-start(f32[64,256]{1,0:T(8,128)S(1)} %maximum_select_fusion.29), channel_id=1, source_target_pairs={{0,1},{1,0},{2,3},{3,2},{4,5},{5,4},{6,7},{7,6},{8,9},{9,8},{10,11... | collective-permute-start | bytes 196616 | tf_op jit(solution)/shard_map/ppermute | solution.py:23
  43.8 6.4 %collective-permute-start.3 = (f32[2,64,256]{2,1,0:T(8,128)S(1)}, f32[2,64,256]{2,1,0:T(8,128)S(1)}, u32[]{:S(2)}, u32[]{:S(2)}) collective-permute-start(f32[2,64,256]{2,1,0:T(8,128)S(1)} %select_add_fusion.5), channel_id=1, source_target_pairs={{0,8},{4,12},{8,0},{12,4},{16,24},{20,28},{24,16},{28,20},{1,9},{5... | collective-permute-start | bytes 393224 | tf_op jit(solution)/shard_map/ppermute | solution.py:23
  45.4 10.4 %collective-permute-start.8 = (f32[128,512]{1,0:T(8,128)S(1)}, f32[128,512]{1,0:T(8,128)S(1)}, u32[]{:S(2)}, u32[]{:S(2)}) collective-permute-start(f32[128,512]{1,0:T(8,128)S(1)} %maximum_select_fusion.15), channel_id=1, source_target_pairs={{0,8},{4,12},{8,0},{12,4},{16,24},{20,28},{24,16},{28,20},{1,9},{5... | collective-permute-start | bytes 786440 | tf_op jit(solution)/shard_map/ppermute | solution.py:23
  46.1 5.8 %collective-permute-start.14 = (f32[128,256]{1,0:T(8,128)S(1)}, f32[128,256]{1,0:T(8,128)S(1)}, u32[]{:S(2)}, u32[]{:S(2)}) collective-permute-start(f32[128,256]{1,0:T(8,128)S(1)} %maximum_select_fusion.24), channel_id=1, source_target_pairs={{0,4},{4,0},{8,12},{12,8},{16,20},{20,16},{24,28},{28,24},{1,5},{5... | collective-permute-start | bytes 393224 | tf_op jit(solution)/shard_map/ppermute | solution.py:23
  50.3 5.6 %collective-permute-start.4 = (f32[64,256]{1,0:T(8,128)S(1)}, f32[64,256]{1,0:T(8,128)S(1)}, u32[]{:S(2)}, u32[]{:S(2)}) collective-permute-start(f32[64,256]{1,0:T(8,128)S(1)} %fusion.83), channel_id=1, source_target_pairs={{0,16},{4,20},{8,24},{12,28},{16,0},{20,4},{24,8},{28,12},{1,17},{... | collective-permute-start | bytes 196616 | tf_op jit(solution)/shard_map/ppermute | solution.py:23
  51.9 8.7 %collective-permute-start.15 = (f32[256,256]{1,0:T(8,128)S(1)}, f32[256,256]{1,0:T(8,128)S(1)}, u32[]{:S(2)}, u32[]{:S(2)}) collective-permute-start(f32[256,256]{1,0:T(8,128)S(1)} %maximum_select_fusion.16), channel_id=1, source_target_pairs={{0,8},{4,12},{8,0},{12,4},{16,24},{20,28},{24,16},{28,20},{1,9},{5... | collective-permute-start | bytes 786440 | tf_op jit(solution)/shard_map/ppermute | solution.py:23
  61.3 6.2 %collective-permute-start.19 = (f32[2,64,256]{2,1,0:T(8,128)S(1)}, f32[2,64,256]{2,1,0:T(8,128)S(1)}, u32[]{:S(2)}, u32[]{:S(2)}) collective-permute-start(f32[2,64,256]{2,1,0:T(8,128)S(1)} %pad_maximum_fusion.3), channel_id=1, source_target_pairs={{0,2},{1,3},{2,0},{3,1},{4,6},{5,7},{6,4},{7,5},{8,10},{9,11},{10,... | collective-permute-start | bytes 393224 | tf_op jit(solution)/shard_map/ppermute | solution.py:23
  67.5 7.1 %collective-permute-start.20 = (f32[2,128,256]{2,1,0:T(8,128)S(1)}, f32[2,128,256]{2,1,0:T(8,128)S(1)}, u32[]{:S(2)}, u32[]{:S(2)}) collective-permute-start(f32[2,128,256]{2,1,0:T(8,128)S(1)} %maximum_select_fusion.18), channel_id=1, source_target_pairs={{0,1},{1,0},{2,3},{3,2},{4,5},{5,4},{6,7},{7,6},{8,9},{9,8},{10,11... | collective-permute-start | bytes 786440 | tf_op jit(solution)/shard_map/ppermute | solution.py:23
  74.7 2.1 %collective-permute-start.21 = (f32[2,256,256]{2,1,0:T(8,128)S(1)}, f32[2,256,256]{2,1,0:T(8,128)S(1)}, u32[]{:S(2)}, u32[]{:S(2)}) collective-permute-start(f32[2,256,256]{2,1,0:T(8,128)S(1)} %maximum_select_fusion.6), channel_id=1, source_target_pairs={{0,4},{4,0},{8,12},{12,8},{16,20},{20,16},{24,28},{28,24},{1,5},{5... | collective-permute-start | bytes 1572872 | tf_op jit(solution)/shard_map/ppermute | solution.py:23
  76.7 2.5 %copy-start.2 = (f32[4,1024,256]{2,1,0:T(8,128)S(1)}, f32[4,1024,256]{2,1,0:T(8,128)}, u32[]{:S(2)}) copy-start(f32[4,1024,256]{2,1,0:T(8,128)} %param.8) | copy-start | bytes 12582916
  79.2 3.1 %copy-start.1 = (f32[4,1024,256]{2,1,0:T(8,128)S(1)}, f32[4,1024,256]{2,1,0:T(8,128)}, u32[]{:S(2)}) copy-start(f32[4,1024,256]{2,1,0:T(8,128)} %param.9) | copy-start | bytes 12582916
  83.4 1.5 copy-start.3
  84.5 14.8 %collective-permute-start.22 = (f32[2,256,256]{2,1,0:T(8,128)S(1)}, f32[2,256,256]{2,1,0:T(8,128)S(1)}, u32[]{:S(2)}, u32[]{:S(2)}) collective-permute-start(f32[2,256,256]{2,1,0:T(8,128)S(1)} %broadcast_select_fusion.1), channel_id=1, source_target_pairs={{0,1},{1,0},{2,3},{3,2},{4,5},{5,4},{6,7},{7,6},{8,9},{9,8},{10,11... | collective-permute-start | bytes 1572872 | tf_op jit(solution)/shard_map/ppermute | solution.py:23
  84.8 17.7 %collective-permute-start.25 = (f32[64,512]{1,0:T(8,128)S(1)}, f32[64,512]{1,0:T(8,128)S(1)}, u32[]{:S(2)}, u32[]{:S(2)}) collective-permute-start(f32[64,512]{1,0:T(8,128)S(1)} %copy-done.3), channel_id=1, source_target_pairs={{0,1},{1,0},{2,3},{3,2},{4,5},{5,4},{6,7},{7,6},{8,9},{9,8},{10,11... | collective-permute-start | bytes 393224 | tf_op jit(solution)/shard_map/ppermute | solution.py:23
  99.4 30.6 %copy-start.4 = (f32[128,512]{1,0:T(8,128)S(1)}, f32[128,512]{1,0:T(8,128)}, u32[]{:S(2)}) copy-start(f32[128,512]{1,0:T(8,128)} %param.13) | copy-start | bytes 786436
  99.4 30.4 %collective-permute-start.23 = (f32[2,256,256]{2,1,0:T(8,128)S(1)}, f32[2,256,256]{2,1,0:T(8,128)S(1)}, u32[]{:S(2)}, u32[]{:S(2)}) collective-permute-start(f32[2,256,256]{2,1,0:T(8,128)S(1)} %select_add_fusion), channel_id=1, source_target_pairs={{0,2},{1,3},{2,0},{3,1},{4,6},{5,7},{6,4},{7,5},{8,10},{9,11},{10,... | collective-permute-start | bytes 1572872 | tf_op jit(solution)/shard_map/ppermute | solution.py:23
  100.6 29.3 %collective-permute-start.27 = (f32[128,256]{1,0:T(8,128)S(1)}, f32[128,256]{1,0:T(8,128)S(1)}, u32[]{:S(2)}, u32[]{:S(2)}) collective-permute-start(f32[128,256]{1,0:T(8,128)S(1)} %slice_select_fusion.1), channel_id=1, source_target_pairs={{0,1},{1,0},{2,3},{3,2},{4,5},{5,4},{6,7},{7,6},{8,9},{9,8},{10,11... | collective-permute-start | bytes 393224 | tf_op jit(solution)/shard_map/ppermute | solution.py:23
  102.6 35.6 %collective-permute-start.26 = (f32[128,512]{1,0:T(8,128)S(1)}, f32[128,512]{1,0:T(8,128)S(1)}, u32[]{:S(2)}, u32[]{:S(2)}) collective-permute-start(f32[128,512]{1,0:T(8,128)S(1)} %maximum_select_fusion.19), channel_id=1, source_target_pairs={{0,2},{1,3},{2,0},{3,1},{4,6},{5,7},{6,4},{7,5},{8,10},{9,11},{10,... | collective-permute-start | bytes 786440 | tf_op jit(solution)/shard_map/ppermute | solution.py:23
  129.8 8.4 %collective-permute-start.24 = (f32[256,256]{1,0:T(8,128)S(1)}, f32[256,256]{1,0:T(8,128)S(1)}, u32[]{:S(2)}, u32[]{:S(2)}) collective-permute-start(f32[256,256]{1,0:T(8,128)S(1)} %fusion.64), channel_id=1, source_target_pairs={{0,4},{4,0},{8,12},{12,8},{16,20},{20,16},{24,28},{28,24},{1,5},{5... | collective-permute-start | bytes 786440 | tf_op jit(solution)/shard_map/ppermute | solution.py:23
  129.9 8.2 %collective-permute-start.28 = (f32[128,256]{1,0:T(8,128)S(1)}, f32[128,256]{1,0:T(8,128)S(1)}, u32[]{:S(2)}, u32[]{:S(2)}) collective-permute-start(f32[128,256]{1,0:T(8,128)S(1)} %select_add_fusion.3), channel_id=1, source_target_pairs={{0,1},{1,0},{2,3},{3,2},{4,5},{5,4},{6,7},{7,6},{8,9},{9,8},{10,11... | collective-permute-start | bytes 393224 | tf_op jit(solution)/shard_map/ppermute | solution.py:23
  130.0 23.3 %collective-permute-start.30 = (f32[128,512]{1,0:T(8,128)S(1)}, f32[128,512]{1,0:T(8,128)S(1)}, u32[]{:S(2)}, u32[]{:S(2)}) collective-permute-start(f32[128,512]{1,0:T(8,128)S(1)} %copy-done.4), channel_id=1, source_target_pairs={{0,1},{1,0},{2,3},{3,2},{4,5},{5,4},{6,7},{7,6},{8,9},{9,8},{10,11... | collective-permute-start | bytes 786440 | tf_op jit(solution)/shard_map/ppermute | solution.py:23
  138.2 14.8 %collective-permute-start.29 = (f32[256,256]{1,0:T(8,128)S(1)}, f32[256,256]{1,0:T(8,128)S(1)}, u32[]{:S(2)}, u32[]{:S(2)}) collective-permute-start(f32[256,256]{1,0:T(8,128)S(1)} %maximum_select_fusion.20), channel_id=1, source_target_pairs={{0,2},{1,3},{2,0},{3,1},{4,6},{5,7},{6,4},{7,5},{8,10},{9,11},{10,... | collective-permute-start | bytes 786440 | tf_op jit(solution)/shard_map/ppermute | solution.py:23
  153.8 13.8 %collective-permute-start.31 = (f32[2,256,256]{2,1,0:T(8,128)S(1)}, f32[2,256,256]{2,1,0:T(8,128)S(1)}, u32[]{:S(2)}, u32[]{:S(2)}) collective-permute-start(f32[2,256,256]{2,1,0:T(8,128)S(1)} %pad_maximum_fusion.2), channel_id=1, source_target_pairs={{0,1},{1,0},{2,3},{3,2},{4,5},{5,4},{6,7},{7,6},{8,9},{9,8},{10,11... | collective-permute-start | bytes 1572872 | tf_op jit(solution)/shard_map/ppermute | solution.py:23

commit v2 on v1

v2 whole, which is shorter than its diff:
```python
import functools

import jax
import jax.numpy as jnp
from jax import lax
from jax.experimental import pallas as pl
from jax.experimental.pallas import tpu as pltpu
from jax.sharding import PartitionSpec as P

CHUNKS = 2
WHOLE = True
T = (0, 0, 1, 1, 3)
STEPS = 2
MIB = 1 << 20


def bits_of(axis):
    return lax.axis_size(axis).bit_length() - 1


def swap(value, place):
    sub_bits = bits_of("sub")
    axis, bit = ("sub", place) if place < sub_bits else ("rows", place - sub_bits)
    return lax.ppermute(value, axis, [(i, i ^ 1 << bit) for i in range(lax.axis_size(axis))])


def digit(place):
    position = lax.axis_index("rows") * lax.axis_size("sub") + lax.axis_index("sub")
    return (position >> place) & 1


def digits(*places):
    return jnp.stack([digit(place) for place in places]).astype(jnp.int32)


def halve(value, dim, place):
    first, second = jnp.split(value, 2, dim)
    lower = digit(place) == 0
    return jnp.where(lower, first, second) + swap(jnp.where(lower, second, first), place)


def ordered(own, other, dim, place):
    lower = digit(place) == 0
    return jnp.where(lower, jnp.concatenate([own, other], dim), jnp.concatenate([other, own], dim))


def widen(value, dim, place):
    return ordered(value, swap(value, place), dim, place)


def common_places(count):
    sub_bits = bits_of("sub")
    places = list(range(count))
    if count > sub_bits:
        places.remove(sub_bits)
        places.insert(0, sub_bits)
    return places


def swap_all(values, place):
    width = values[0].shape[-1]
    sent = swap(jnp.concatenate([value.reshape(-1, width) for value in values], 0), place)
    ends = [0]
    for value in values:
        ends.append(ends[-1] + value.size // width)
    return [sent[ends[i] : ends[i + 1]].reshape(value.shape) for i, value in enumerate(values)]


def after(value, tokens, index):
    return lax.optimization_barrier((value, tokens[min(index, len(tokens) - 1)]))[0]


def halves(value):
    high = value.astype(jnp.bfloat16)
    return high, (value - high.astype(jnp.float32)).astype(jnp.bfloat16)


def product(left, right, left_dim, right_dim):
    dims = (((left_dim,), (right_dim,)), ((), ()))

    def one(a, b):
        return lax.dot_general(a, b, dims, preferred_element_type=jnp.float32)

    return one(left[0], right[0]) + (one(left[0], right[1]) + one(left[1], right[0]))


def put_sums(keep_ref, send_ref, chunk, at, where, sums):
    width = keep_ref.shape[0]
    del width
    for ref, side in ((keep_ref, where), (send_ref, 1 - where)):
        for level, (total, width) in enumerate(sums):
            start = pl.multiple_of((side * chunk[1] + chunk[0]) * width, width)
            ref[pl.ds(at + level * width, width), :] = total[pl.ds(start, width), :]


def first_kernel(where_ref, x_ref, u_ref, v_ref, v_next_ref, keep_ref, send_ref, total, total_next):
    step = pl.program_id(0)

    @pl.when(step == 0)
    def _():
        total[...] = jnp.zeros_like(total)
        total_next[...] = jnp.zeros_like(total_next)

    sides = x_ref.shape[1]
    x, v, v_next = halves(x_ref[...]), halves(v_ref[0]), halves(v_next_ref[0])
    total[...] += product(x, v, 0, 0)
    total_next[:sides] += product(x, v_next, 0, 0)
    total_next[sides:] += product(halves(u_ref[0]), v_next, 0, 0)

    @pl.when(step == pl.num_programs(0) - 1)
    def _():
        where = where_ref[0]
        width = sides // (2 * CHUNKS)
        for ref, side in ((keep_ref, where), (send_ref, 1 - where)):
            start = pl.multiple_of(side * CHUNKS * width, width)
            ref[: CHUNKS * width, :] = total[pl.ds(start, CHUNKS * width), :]
            ref[CHUNKS * width : 2 * CHUNKS * width, :] = total_next[pl.ds(start, CHUNKS * width), :]
        rank = u_ref.shape[2]
        at = 2 * CHUNKS * width
        for ref, side in ((keep_ref, where), (send_ref, 1 - where)):
            start = pl.multiple_of(sides + side * (rank // 2), rank // 2)
            ref[at:, :] = total_next[pl.ds(start, rank // 2), :]


def slab(rows, rank, level):
    return pl.BlockSpec((1, rows, rank), lambda i, *_: (level, i, 0))


def whole(shape):
    return pl.BlockSpec(shape, lambda *_: (0,) * len(shape))


def shapes(*values):
    return [jax.ShapeDtypeStruct(value, jnp.float32) for value in values]


SMEM = pl.BlockSpec(memory_space=pltpu.SMEM)


def first_sums(where, x, bases_u, bases_v, level):
    rows, sides = x.shape
    rank = bases_u.shape[2]
    block = rows // STEPS
    out = (sides + rank // 2, rank)
    return pl.pallas_call(
        first_kernel,
        grid=(STEPS,),
        in_specs=[
            SMEM,
            pl.BlockSpec((block, sides), lambda i: (i, 0)),
            slab(block, rank, level),
            slab(block, rank, level),
            slab(block, rank, level + 1),
        ],
        out_specs=[whole(out)] * 2,
        out_shape=shapes(out, out),
        scratch_shapes=[pltpu.VMEM((sides, rank), jnp.float32), pltpu.VMEM((sides + rank, rank), jnp.float32)],
        compiler_params=pltpu.CompilerParams(vmem_limit_bytes=60 * MIB),
        cost_estimate=pl.CostEstimate(flops=6 * rows * rank * (2 * sides + rank), bytes_accessed=5 * rows * rank * 4, transcendentals=0),
    )(where, x, bases_u, bases_v, bases_v)


def update(x, u_ref, u_next_ref, factors):
    return x - (
        product(halves(u_ref[0]), halves(factors[0]), 1, 1) + product(halves(u_next_ref[0]), halves(factors[1]), 1, 1)
    )


def middle_kernel(
    where_ref, x0_ref, x1_ref, own_ref, partner_ref, u_ref, u_next_ref, v_ref, v_next_ref, x_ref, keep_ref, send_ref, total, total_next
):
    step = pl.program_id(0)

    @pl.when(step == 0)
    def _():
        total[...] = jnp.zeros_like(total)
        total_next[...] = jnp.zeros_like(total_next)

    own, partner = own_ref[...], partner_ref[...]
    lower = where_ref[0] == 0
    first, second = jnp.where(lower, own, partner), jnp.where(lower, partner, own)
    factors = [jnp.concatenate([first[k], second[k]], 0) for k in range(2)]
    x = update(jnp.concatenate([x0_ref[...], x1_ref[...]], 1), u_ref, u_next_ref, factors)
    x_ref[...] = x
    x = halves(x)
    total[...] += product(x, halves(v_ref[0]), 0, 0)
    total_next[...] += product(x, halves(v_next_ref[0]), 0, 0)

    @pl.when(step == pl.num_programs(0) - 1)
    def _():
        width = x0_ref.shape[1]
        put_sums(keep_ref, send_ref, (0, 1), 0, where_ref[1], ((total, width), (total_next, width)))


def middle(where, chunk, x, own, partner, bases_u, bases_v, level):
    rows, sides = x.shape
    rank = bases_u.shape[2]
    block, width = rows // STEPS, sides // (2 * CHUNKS)
    out = (2 * width, rank)
    return pl.pallas_call(
        middle_kernel,
        grid=(STEPS,),
        in_specs=[
            SMEM,
            pl.BlockSpec((block, width), lambda i: (i, chunk)),
            pl.BlockSpec((block, width), lambda i: (i, CHUNKS + chunk)),
            whole(own.shape),
            whole(own.shape),
            slab(block, rank, level),
            slab(block, rank, level + 1),
            slab(block, rank, level + 2),
            slab(block, rank, level + 3),
        ],
        out_specs=[pl.BlockSpec((block, 2 * width), lambda i: (i, 0)), whole(out), whole(out)],
        out_shape=shapes((rows, 2 * width), out, out),
        scratch_shapes=[pltpu.VMEM((2 * width, rank), jnp.float32)] * 2,
        compiler_params=pltpu.CompilerParams(vmem_limit_bytes=24 * MIB),
        cost_estimate=pl.CostEstimate(flops=24 * rows * rank * width * 2, bytes_accessed=4 * rows * rank * 4, transcendentals=0),
    )(where, x, x, own, partner, bases_u, bases_u, bases_v, bases_v)


def last_kernel(where_ref, x_ref, own_ref, partner_ref, u_ref, u_next_ref, *refs):
    out_ref = refs[-1]
    mine = where_ref[0] == pl.program_id(1)
    factors = jnp.where(mine, own_ref[...], partner_ref[...])
    out_ref[...] = update(x_ref[...], u_ref, u_next_ref, factors)


def last(where, chunk, x, own, partner, bases_u, level, into, sides):
    rows = x.shape[0]
    rank = bases_u.shape[2]
    block, width = rows // STEPS, sides // (2 * CHUNKS)
    more = [] if into is None else [into]
    return pl.pallas_call(
        last_kernel,
        grid=(STEPS, 2),
        in_specs=[
            SMEM,
            pl.BlockSpec((block, width), lambda i, b: (i, b)),
            whole(own.shape),
            whole(own.shape),
            slab(block, rank, level),
            slab(block, rank, level + 1),
        ]
        + [pl.BlockSpec(memory_space=pl.ANY)] * len(more),
        out_specs=pl.BlockSpec((block, width), lambda i, b: (i, CHUNKS * b + chunk)),
        out_shape=jax.ShapeDtypeStruct((rows, sides), jnp.float32),
        input_output_aliases={6: 0} if more else {},
        compiler_params=pltpu.CompilerParams(vmem_limit_bytes=24 * MIB),
        cost_estimate=pl.CostEstimate(flops=12 * rows * rank * width * 2, bytes_accessed=3 * rows * rank * 4, transcendentals=0),
    )(where, x, own, partner, bases_u, bases_u, *more)


def gram_kernel(u_ref, v_ref, out_ref):
    out_ref[...] = product(halves(u_ref[0]), halves(v_ref[0]), 0, 0)


def gram_term(bases_u, bases_v, level):
    rows, rank = bases_u.shape[1:]
    return pl.pallas_call(
        gram_kernel,
        grid=(1,),
        in_specs=[slab(rows, rank, level), slab(rows, rank, level + 1)],
        out_specs=whole((rank, rank)),
        out_shape=jax.ShapeDtypeStruct((rank, rank), jnp.float32),
        compiler_params=pltpu.CompilerParams(vmem_limit_bytes=24 * MIB),
        cost_estimate=pl.CostEstimate(flops=6 * rows * rank * rank, bytes_accessed=2 * rows * rank * 4, transcendentals=0),
    )(bases_u, bases_v)


def first_gram(value, places, sibling_place, tokens, start):
    for place in places[:0:-1]:
        value = after(value, tokens, start)
        value = value + swap(value, place)
        start += 1
    other = swap(after(value, tokens, start), sibling_place)
    both = widen(jnp.stack([value, other]), 1, places[0])
    return both[0], both[1]


def later_gram(value, places, sibling_place, tokens, start):
    for place in places:
        value = after(value, tokens, start)
        value = value + swap(value, place)
        start += 1
    return value, swap(after(value, tokens, start), sibling_place)


def couplings(rows, rows_next, places, sibling_place, tokens, start):
    values = [rows, rows_next]
    seen = [[], []]
    order = places[::-1]
    order.insert(len(order) - 1, sibling_place)
    for step, place in enumerate(order):
        if start + step >= 0:
            values = [after(value, tokens, start + step) for value in values]
        use = (0,) if place == sibling_place else (0, 1)
        grown = []
        for k in use:
            at = sum(other > place for other in seen[k])
            seen[k].append(place)
            grown.append((jnp.expand_dims(values[k], at), at))
        partners = swap_all([value for value, _ in grown], place)
        for k, (value, at), partner in zip(use, grown, partners):
            values[k] = ordered(value, partner, at, place)
    sides = []
    for k, place in ((0, sibling_place + 1), (1, sibling_place)):
        first, second = jnp.split(values[k].reshape(-1, rows.shape[1]), 2, 1)
        lower = digit(place) == 0
        sides.append((jnp.where(lower, first, second), jnp.where(lower, second, first)))
    return sides


def reduce(sums, places, sibling_place):
    tokens = [sums]
    for place in places[1:]:
        sums = halve(sums, 2, place)
        tokens.append(sums)
    other = swap(sums, sibling_place)
    upper = sums[0] + other[0]
    tokens.append(upper)
    upper_other = swap(upper, sibling_place + 1)
    tokens.append(upper_other)
    return (upper, upper_other, sums[1], other[1]), tokens


def factors_kernel(upper, upper_other, own, sibling, k_own, k_sibling, next_own, next_sibling, gram_own, gram_sibling, out_ref):
    def part(ref):
        return halves(ref[...])

    factors = product(part(upper), part(k_own), 1, 1) + product(part(upper_other), part(k_sibling), 1, 1)
    out_ref[0] = factors
    factors = halves(factors)
    own = halves(own[...] - product(factors, part(gram_own), 1, 0))
    sibling = halves(sibling[...] - product(factors, part(gram_sibling), 1, 0))
    out_ref[1] = product(own, part(next_own), 1, 1) + product(sibling, part(next_sibling), 1, 1)


def factors_of(reduced, grams, sides, places):
    count, width, rank = reduced[0].shape
    reduced = [value.reshape(count * width, rank) for value in reduced]
    both = pl.pallas_call(
        factors_kernel,
        out_shape=jax.ShapeDtypeStruct((2, count * width, rank), jnp.float32),
        compiler_params=pltpu.CompilerParams(vmem_limit_bytes=16 * MIB),
        cost_estimate=pl.CostEstimate(flops=36 * count * width * rank * rank, bytes_accessed=6 * rank * rank * 4, transcendentals=0),
    )(*reduced, *sides[0], *sides[1], *grams)
    found = []
    for k in range(count):
        own = both[:, k * width : (k + 1) * width]
        for place in places[:0:-1]:
            own = widen(own, 1, place)
        found.append((own, swap(own, places[0])))
    return found


def local(right_sides, bases_u, bases_v, couple_first, couple_second, couple_third, couple_fourth):
    couples = (couple_first, couple_second, couple_third, couple_fourth)
    sides, rank = right_sides.shape[1], bases_u.shape[2]
    width = sides // (2 * CHUNKS)
    total_bits = bits_of("sub") + bits_of("rows")
    sibling, sibling_next = total_bits - 2, total_bits - 4
    places, places_next = common_places(sibling), common_places(sibling_next)

    keep, send = first_sums(digits(places[0]), right_sides, bases_u, bases_v, 0)
    sums = keep + swap(send, places[0])
    stacked = sums[:sides].reshape(2, CHUNKS, width, rank)
    groups = [stacked] if WHOLE else [stacked[:, k : k + 1] for k in range(CHUNKS)]
    chunks = [reduce(group, places, sibling) for group in groups]
    tokens = chunks[0][1]
    grams = first_gram(sums[sides:], places, sibling, tokens, T[0])
    coupling = couplings(couples[0], couples[1], places, sibling, tokens, T[1])
    term = gram_term(after(bases_u, tokens, T[2]), bases_v, 2)
    grams_next = later_gram(term, places_next, sibling_next, tokens, T[3])
    coupling_next = couplings(couples[2], couples[3], places_next, sibling_next, tokens, T[4])

    found = [pair for values, _ in chunks for pair in factors_of(values, grams, coupling, places)]
    where = digits(places[0], places_next[0])
    parts, chunks = [], []
    for k, (own, partner) in enumerate(found):
        part, keep, send = middle(where, k, right_sides, own, partner, bases_u, bases_v, 0)
        parts.append(part)
        sums = keep + swap(send, places_next[0])
        chunks.append(reduce(sums.reshape(2, 1, width, rank), places_next, sibling_next))
    solved = None
    for k, (values, _) in enumerate(chunks):
        ((own, partner),) = factors_of(values, grams_next, coupling_next, places_next)
        solved = last(digits(places_next[0]), k, parts[k], own, partner, bases_u, 2, solved, sides)
    return solved


def solution(mesh):
    placed = (
        P(("rows", "sub"), None),
        P(None, ("rows", "sub"), None),
        P(None, ("rows", "sub"), None),
        P(("rows", "sub"), None),
        P(("rows", "sub"), None),
        P(("rows", "sub"), None),
        P(("rows", "sub"), None),
    )
    return jax.shard_map(
        local, mesh=mesh, in_specs=placed, out_specs=P(("rows", "sub"), None), check_vma=False
    )
```

time: 175 us -> 141 us (0.81)
  waiting for transfers between devices: 112 us -> 73 us
  Pallas kernels: 0 us -> 25.4 us
  matrix products: 23.9 us -> 0 us
  starting transfers between devices: 27.5 us -> 39.3 us
  local copies, waits for them, and re-layouts: 4.9 us -> 0.38 us
  other arithmetic: 5.34 us -> 2.27 us
    ppermute x32 -> x31, waiting for transfers between devices: 112 us -> 73 us  [swap(): lax.ppermute(value, axis, [(i, i ^ 1 << bit) for i in range(lax.axis_size...]
    pallas_call x0 -> x9, Pallas kernels: none -> 25.4 us  [the longest x2 9.07 us: middle(): pl.pallas_call(middle_kernel, grid=(STEPS,), in_specs=[SMEM, pl.BlockSpec...]
    dot_general x18 -> x0, matrix products: 23.9 us -> none  [dot(): lax.dot_general(left, right, (((left_dim,), (right_dim,)), ((), ())), pre...]
    ppermute x32 -> x31, starting transfers between devices: 27.5 us -> 39.3 us  [swap(): lax.ppermute(value, axis, [(i, i ^ 1 << bit) for i in range(lax.axis_size...]
    sub x1 -> x0, local copies, waits for them, and re-layouts: 2.88 us -> none  [local(): part = part - dot(bases_u[level + k], factors[k], 1, 1)]
    unnamed x11 -> x14, local copies, waits for them, and re-layouts: 2.02 us -> 0.04 us
    select_n x14 -> x15, other arithmetic: 2.17 us -> 0.39 us  [ordered(): jnp.where(lower, jnp.concatenate([own, other], dim), jnp.concatenate([oth...]
  transfers between devices with their start and end apart: 32 -> 31, of which waited for: 13 -> 23; matrix products, arithmetic and copies ran while one was open for 9% -> 1% of each run, Pallas kernels for 0% -> 11%
where the time goes in v2:
time: 141 us
  waiting for transfers between devices  73 us (52%)
  starting transfers between devices  39.3 us (28%)
  Pallas kernels  25.4 us (18%)
  other arithmetic  2.27 us (2%)
    ppermute x31, waiting for transfers between devices, swap(): lax.ppermute(value, axis, [(i, i ^ 1 << bit) for i in range(lax.axis_size...  73 us
    ppermute x31, starting transfers between devices, swap(): lax.ppermute(value, axis, [(i, i ^ 1 << bit) for i in range(lax.axis_size...  39.3 us
    pallas_call x2, Pallas kernels, middle(): pl.pallas_call(middle_kernel, grid=(STEPS,), in_specs=[SMEM, pl.BlockSpec...  9.07 us
    pallas_call x2, Pallas kernels, last(): pl.pallas_call(last_kernel, grid=(STEPS, 2), in_specs=[SMEM, pl.BlockSpec...  6.64 us
    pallas_call x1, Pallas kernels, first_sums(): pl.pallas_call(first_kernel, grid=(STEPS,), in_specs=[SMEM, pl.BlockSpec(...  5.46 us
    pallas_call x3, Pallas kernels, factors_of(): pl.pallas_call(factors_kernel, out_shape=jax.ShapeDtypeStruct((2, count *...  3.55 us
  transfers between devices with their start and end apart: 31, of which 23 were waited for; matrix products, arithmetic and copies ran while one was open for 1% of the time, Pallas kernels for 11%

profile of v2, /device:TPU:0, one launch (start us, length us, event | category | flops | bytes accessed | tf_op | source)
XLA Modules:
  0.0 140.8 jit_solution(8610544103378724290)
XLA Ops:
  0.0 5.5 %shard_map.73 = (f32[640,256]{1,0:T(8,128)}, f32[640,256]{1,0:T(8,128)}) custom-call(s32[1]{0:T(128)} %bitcast.1.where_ref, f32[1024,512]{1,0:T(8,128)} %x1_ref.3, f32[4,1024,256]{2,1,0:T(8,128)} %u_next_ref.7, f32[4,1024,256]{2,1,0:T(8,128)} %v_next_ref.5, f32[4,1024,256]{2,1,0:T(8,128)} %v_next_ref.5), custom_call_target="tpu_custom_call" | custom-call | flops 2013265920 | bytes 5242880 | tf_op jit(solution)/shard_map/pallas_call | solution.py:145
  6.0 1.9 %collective-permute-done = f32[640,256]{1,0:T(8,128)S(1)} collective-permute-done((f32[640,256]{1,0:T(8,128)}, f32[640,256]{1,0:T(8,128)S(1)}, u32[]{:S(2)}, u32[]{:S(2)}) %collective-permute-start) | collective-permute-done | bytes 655392 | tf_op jit(solution)/shard_map/ppermute | solution.py:24
  7.9 1.2 add.75
  9.2 4.0 %collective-permute-start.5 = (f32[48,512]{1,0:T(8,128)S(1)}, f32[48,512]{1,0:T(8,128)S(1)}, u32[]{:S(2)}, u32[]{:S(2)}) collective-permute-start(f32[48,512]{1,0:T(8,128)S(1)} %pad_maximum_fusion.4), channel_id=1, source_target_pairs={{0,2},{1,3},{2,0},{3,1},{4,6},{5,7},{6,4},{7,5},{8,10},{9,11},{10,... | collective-permute-start | bytes 294920 | tf_op jit(solution)/shard_map/ppermute | solution.py:24
  13.3 1.9 %collective-permute-start.1 = (f32[2,2,64,256]{3,2,1,0:T(8,128)S(1)}, f32[2,2,64,256]{3,2,1,0:T(8,128)S(1)}, u32[]{:S(2)}, u32[]{:S(2)}) collective-permute-start(f32[2,2,64,256]{3,2,1,0:T(8,128)S(1)} %slice_select_fusion.8), channel_id=1, source_target_pairs={{0,1},{1,0},{2,3},{3,2},{4,5},{5,4},{6,7},{7,6},{8,9},{9,8},{10,11... | collective-permute-start | bytes 786440 | tf_op jit(solution)/shard_map/ppermute | solution.py:24
  15.2 6.6 %collective-permute-done.5 = f32[48,512]{1,0:T(8,128)S(1)} collective-permute-done((f32[48,512]{1,0:T(8,128)S(1)}, f32[48,512]{1,0:T(8,128)S(1)}, u32[]{:S(2)}, u32[]{:S(2)}) %collective-permute-start.5) | collective-permute-done | bytes 98336 | tf_op jit(solution)/shard_map/ppermute | solution.py:24
  21.8 3.4 %collective-permute-done.1 = f32[2,2,64,256]{3,2,1,0:T(8,128)S(1)} collective-permute-done((f32[2,2,64,256]{3,2,1,0:T(8,128)S(1)}, f32[2,2,64,256]{3,2,1,0:T(8,128)S(1)}, u32[]{:S(2)}, u32[]{:S(2)}) %collective-permute-start.1) | collective-permute-done | bytes 262176 | tf_op jit(solution)/shard_map/ppermute | solution.py:24
  25.3 2.8 %collective-permute-start.2 = (f32[2,2,32,256]{3,2,1,0:T(8,128)S(1)}, f32[2,2,32,256]{3,2,1,0:T(8,128)S(1)}, u32[]{:S(2)}, u32[]{:S(2)}) collective-permute-start(f32[2,2,32,256]{3,2,1,0:T(8,128)S(1)} %slice_select_fusion.9), channel_id=1, source_target_pairs={{0,2},{1,3},{2,0},{3,1},{4,6},{5,7},{6,4},{7,5},{8,10},{9,11},{10,... | collective-permute-start | bytes 393224 | tf_op jit(solution)/shard_map/ppermute | solution.py:24
  28.1 2.5 %collective-permute-start.10 = (f32[128,256]{1,0:T(8,128)S(1)}, f32[128,256]{1,0:T(8,128)S(1)}, u32[]{:S(2)}, u32[]{:S(2)}) collective-permute-start(f32[128,256]{1,0:T(8,128)S(1)} %add.81), channel_id=1, source_target_pairs={{0,1},{1,0},{2,3},{3,2},{4,5},{5,4},{6,7},{7,6},{8,9},{9,8},{10,11... | collective-permute-start | bytes 393224 | tf_op jit(solution)/shard_map/ppermute | solution.py:24
  30.8 2.3 %collective-permute-done.2 = f32[2,2,32,256]{3,2,1,0:T(8,128)S(1)} collective-permute-done((f32[2,2,32,256]{3,2,1,0:T(8,128)S(1)}, f32[2,2,32,256]{3,2,1,0:T(8,128)S(1)}, u32[]{:S(2)}, u32[]{:S(2)}) %collective-permute-start.2) | collective-permute-done | bytes 131104 | tf_op jit(solution)/shard_map/ppermute | solution.py:24
  33.1 1.6 %collective-permute-start.3 = (f32[2,2,32,256]{3,2,1,0:T(8,128)S(1)}, f32[2,2,32,256]{3,2,1,0:T(8,128)S(1)}, u32[]{:S(2)}, u32[]{:S(2)}) collective-permute-start(f32[2,2,32,256]{3,2,1,0:T(8,128)S(1)} %select_add_fusion.1), channel_id=1, source_target_pairs={{0,8},{4,12},{8,0},{12,4},{16,24},{20,28},{24,16},{28,20},{1,9},{5... | collective-permute-start | bytes 393224 | tf_op jit(solution)/shard_map/ppermute | solution.py:24
  35.5 1.6 %collective-permute-start.11 = (f32[128,256]{1,0:T(8,128)S(1)}, f32[128,256]{1,0:T(8,128)S(1)}, u32[]{:S(2)}, u32[]{:S(2)}) collective-permute-start(f32[128,256]{1,0:T(8,128)S(1)} %add.82), channel_id=1, source_target_pairs={{0,8},{4,12},{8,0},{12,4},{16,24},{20,28},{24,16},{28,20},{1,9},{5... | collective-permute-start | bytes 393224 | tf_op jit(solution)/shard_map/ppermute | solution.py:24
  37.1 1.2 collective-permute-done.6
  38.4 1.6 %collective-permute-start.7 = (f32[64,512]{1,0:T(8,128)S(1)}, f32[64,512]{1,0:T(8,128)S(1)}, u32[]{:S(2)}, u32[]{:S(2)}) collective-permute-start(f32[64,512]{1,0:T(8,128)S(1)} %bitcast.102), channel_id=1, source_target_pairs={{0,8},{4,12},{8,0},{12,4},{16,24},{20,28},{24,16},{28,20},{1,9},{5... | collective-permute-start | bytes 393224 | tf_op jit(solution)/shard_map/ppermute | solution.py:24
  40.0 1.4 collective-permute-done.11
  41.5 1.9 %collective-permute-done.7 = f32[64,512]{1,0:T(8,128)S(1)} collective-permute-done((f32[64,512]{1,0:T(8,128)S(1)}, f32[64,512]{1,0:T(8,128)S(1)}, u32[]{:S(2)}, u32[]{:S(2)}) %collective-permute-start.7) | collective-permute-done | bytes 131104 | tf_op jit(solution)/shard_map/ppermute | solution.py:24
  43.6 1.6 %collective-permute-start.4 = (f32[2,32,256]{2,1,0:T(8,128)S(1)}, f32[2,32,256]{2,1,0:T(8,128)S(1)}, u32[]{:S(2)}, u32[]{:S(2)}) collective-permute-start(f32[2,32,256]{2,1,0:T(8,128)S(1)} %bitcast.72), channel_id=1, source_target_pairs={{0,16},{4,20},{8,24},{12,28},{16,0},{20,4},{24,8},{28,12},{1,17},{... | collective-permute-start | bytes 196616 | tf_op jit(solution)/shard_map/ppermute | solution.py:24
  45.8 2.2 %collective-permute-done.4 = f32[2,32,256]{2,1,0:T(8,128)S(1)} collective-permute-done((f32[2,32,256]{2,1,0:T(8,128)S(1)}, f32[2,32,256]{2,1,0:T(8,128)S(1)}, u32[]{:S(2)}, u32[]{:S(2)}) %collective-permute-start.4) | collective-permute-done | bytes 65568 | tf_op jit(solution)/shard_map/ppermute | solution.py:24
  48.1 1.2 shard_map.74
  49.3 1.8 %collective-permute-start.13 = (f32[2,32,256]{2,1,0:T(8,128)S(1)}, f32[2,32,256]{2,1,0:T(8,128)S(1)}, u32[]{:S(2)}, u32[]{:S(2)}) collective-permute-start(f32[2,32,256]{2,1,0:T(8,128)S(1)} %get-tuple-element.76), channel_id=1, source_target_pairs={{0,2},{1,3},{2,0},{3,1},{4,6},{5,7},{6,4},{7,5},{8,10},{9,11},{10,... | collective-permute-start | bytes 196616 | tf_op jit(solution)/shard_map/ppermute | solution.py:24
  51.1 1.2 collective-permute-start.19
  53.0 1.8 %collective-permute-start.21 = (f32[256,256]{1,0:T(8,128)S(1)}, f32[256,256]{1,0:T(8,128)S(1)}, u32[]{:S(2)}, u32[]{:S(2)}) collective-permute-start(f32[256,256]{1,0:T(8,128)S(1)} %shard_map.76), channel_id=1, source_target_pairs={{0,1},{1,0},{2,3},{3,2},{4,5},{5,4},{6,7},{7,6},{8,9},{9,8},{10,11... | collective-permute-start | bytes 786440 | tf_op jit(solution)/shard_map/ppermute | solution.py:24
  54.8 1.7 %collective-permute-start.24 = (f32[2,32,256]{2,1,0:T(8,128)S(1)}, f32[2,32,256]{2,1,0:T(8,128)S(1)}, u32[]{:S(2)}, u32[]{:S(2)}) collective-permute-start(f32[2,32,256]{2,1,0:T(8,128)S(1)} %get-tuple-element.75), channel_id=1, source_target_pairs={{0,2},{1,3},{2,0},{3,1},{4,6},{5,7},{6,4},{7,5},{8,10},{9,11},{10,... | collective-permute-start | bytes 196616 | tf_op jit(solution)/shard_map/ppermute | solution.py:24
  56.5 2.5 %collective-permute-done.13 = f32[2,32,256]{2,1,0:T(8,128)S(1)} collective-permute-done((f32[2,32,256]{2,1,0:T(8,128)S(1)}, f32[2,32,256]{2,1,0:T(8,128)S(1)}, u32[]{:S(2)}, u32[]{:S(2)}) %collective-permute-start.13) | collective-permute-done | bytes 65568 | tf_op jit(solution)/shard_map/ppermute | solution.py:24
  59.1 3.1 %collective-permute-done.19 = f32[64,512]{1,0:T(8,128)S(1)} collective-permute-done((f32[64,512]{1,0:T(8,128)S(1)}, f32[64,512]{1,0:T(8,128)S(1)}, u32[]{:S(2)}, u32[]{:S(2)}) %collective-permute-start.19) | collective-permute-done | bytes 131104 | tf_op jit(solution)/shard_map/ppermute | solution.py:24
  62.2 1.1 collective-permute-done.24
  63.3 4.0 %collective-permute-start.25 = (f32[2,64,256]{2,1,0:T(8,128)S(1)}, f32[2,64,256]{2,1,0:T(8,128)S(1)}, u32[]{:S(2)}, u32[]{:S(2)}) collective-permute-start(f32[2,64,256]{2,1,0:T(8,128)S(1)} %maximum_select_fusion.13), channel_id=1, source_target_pairs={{0,1},{1,0},{2,3},{3,2},{4,5},{5,4},{6,7},{7,6},{8,9},{9,8},{10,11... | collective-permute-start | bytes 393224 | tf_op jit(solution)/shard_map/ppermute | solution.py:24
  67.3 1.9 %collective-permute-done.14 = f32[2,64,256]{2,1,0:T(8,128)S(1)} collective-permute-done((f32[2,64,256]{2,1,0:T(8,128)S(1)}, f32[2,64,256]{2,1,0:T(8,128)S(1)}, u32[]{:S(2)}, u32[]{:S(2)}) %collective-permute-start.14) | collective-permute-done | bytes 131104 | tf_op jit(solution)/shard_map/ppermute | solution.py:24
  69.4 1.2 collective-permute-done.25
  70.8 3.3 %collective-permute-start.22 = (f32[256,256]{1,0:T(8,128)S(1)}, f32[256,256]{1,0:T(8,128)S(1)}, u32[]{:S(2)}, u32[]{:S(2)}) collective-permute-start(f32[256,256]{1,0:T(8,128)S(1)} %add.86.gram_own), channel_id=1, source_target_pairs={{0,2},{1,3},{2,0},{3,1},{4,6},{5,7},{6,4},{7,5},{8,10},{9,11},{10,... | collective-permute-start | bytes 786440 | tf_op jit(solution)/shard_map/ppermute | solution.py:24
  74.1 4.5 %shard_map.75 = (f32[1024,256]{1,0:T(8,128)S(1)}, f32[256,256]{1,0:T(8,128)S(1)}, f32[256,256]{1,0:T(8,128)S(1)}) custom-call(s32[2]{0:T(128)S(1)} %pad_add_fusion.where_ref, f32[1024,512]{1,0:T(8,128)S(1)} %copy-done.2, f32[1024,512]{1,0:T(8,128)S(1)} %copy-done.2, f32[2,128,256]{2,1,0:T(8,128)S(1)} %maximum_select_fusion.7.own_ref, ...), custom_call_target="tpu_custom_call" | custom-call | flops 1610612736 | bytes 4194304 | tf_op jit(solution)/shard_map/pallas_call | solution.py:200
  78.6 1.1 collective-permute-start.16
  79.7 4.5 %shard_map.78 = (f32[1024,256]{1,0:T(8,128)S(1)}, f32[256,256]{1,0:T(8,128)S(1)}, f32[256,256]{1,0:T(8,128)S(1)}) custom-call(s32[2]{0:T(128)S(1)} %pad_add_fusion.where_ref, f32[1024,512]{1,0:T(8,128)S(1)} %copy-done.2, f32[1024,512]{1,0:T(8,128)S(1)} %copy-done.2, f32[2,128,256]{2,1,0:T(8,128)S(1)} %maximum_select_fusion.9.own_ref, ...), custom_call_target="tpu_custom_call" | custom-call | flops 1610612736 | bytes 4194304 | tf_op jit(solution)/shard_map/pallas_call | solution.py:200
  84.2 1.1 collective-permute-start.27
  85.3 4.4 %collective-permute-done.20 = f32[256,512]{1,0:T(8,128)S(1)} collective-permute-done((f32[256,512]{1,0:T(8,128)S(1)}, f32[256,512]{1,0:T(8,128)S(1)}, u32[]{:S(2)}, u32[]{:S(2)}) %collective-permute-start.20) | collective-permute-done | bytes 524320 | tf_op jit(solution)/shard_map/ppermute | solution.py:24
  89.9 5.4 %collective-permute-done.16 = f32[256,256]{1,0:T(8,128)S(1)} collective-permute-done((f32[256,256]{1,0:T(8,128)S(1)}, f32[256,256]{1,0:T(8,128)S(1)}, u32[]{:S(2)}, u32[]{:S(2)}) %collective-permute-start.16) | collective-permute-done | bytes 262176 | tf_op jit(solution)/shard_map/ppermute | solution.py:24
  95.3 2.3 %collective-permute-start.17 = (f32[2,1,128,256]{3,2,1,0:T(8,128)S(1)}, f32[2,1,128,256]{3,2,1,0:T(8,128)S(1)}, u32[]{:S(2)}, u32[]{:S(2)}) collective-permute-start(f32[2,1,128,256]{3,2,1,0:T(8,128)S(1)} %bitcast.93), channel_id=1, source_target_pairs={{0,2},{1,3},{2,0},{3,1},{4,6},{5,7},{6,4},{7,5},{8,10},{9,11},{10,... | collective-permute-start | bytes 786440 | tf_op jit(solution)/shard_map/ppermute | solution.py:24
  97.7 7.1 %collective-permute-done.27 = f32[256,256]{1,0:T(8,128)S(1)} collective-permute-done((f32[256,256]{1,0:T(8,128)S(1)}, f32[256,256]{1,0:T(8,128)S(1)}, u32[]{:S(2)}, u32[]{:S(2)}) %collective-permute-start.27) | collective-permute-done | bytes 262176 | tf_op jit(solution)/shard_map/ppermute | solution.py:24
  105.0 11.5 %collective-permute-done.17 = f32[2,1,128,256]{3,2,1,0:T(8,128)S(1)} collective-permute-done((f32[2,1,128,256]{3,2,1,0:T(8,128)S(1)}, f32[2,1,128,256]{3,2,1,0:T(8,128)S(1)}, u32[]{:S(2)}, u32[]{:S(2)}) %collective-permute-start.17) | collective-permute-done | bytes 262176 | tf_op jit(solution)/shard_map/ppermute | solution.py:24
  116.6 4.2 %collective-permute-done.28 = f32[2,1,128,256]{3,2,1,0:T(8,128)S(1)} collective-permute-done((f32[2,1,128,256]{3,2,1,0:T(8,128)S(1)}, f32[2,1,128,256]{3,2,1,0:T(8,128)S(1)}, u32[]{:S(2)}, u32[]{:S(2)}) %collective-permute-start.28) | collective-permute-done | bytes 262176 | tf_op jit(solution)/shard_map/ppermute | solution.py:24
  120.9 1.3 collective-permute-done.29
  122.2 1.2 shard_map.79.own_ref
  124.2 1.2 shard_map.77.own_ref
  125.4 1.3 collective-permute-start.23
  126.8 5.8 %collective-permute-done.30.partner_ref = f32[2,128,256]{2,1,0:T(8,128)S(1)} collective-permute-done((f32[2,128,256]{2,1,0:T(8,128)S(1)}, f32[2,128,256]{2,1,0:T(8,128)S(1)}, u32[]{:S(2)}, u32[]{:S(2)}) %collective-permute-start.30) | collective-permute-done | bytes 262176 | tf_op jit(solution)/shard_map/ppermute | solution.py:24
  132.6 3.3 %shard_map.80.refs_0_ = f32[1024,512]{1,0:T(8,128)} custom-call(s32[1]{0:T(128)} %bitcast.where_ref, f32[1024,256]{1,0:T(8,128)S(1)} %get-tuple-element.54.x_ref, f32[2,128,256]{2,1,0:T(8,128)S(1)} %shard_map.79.own_ref, f32[2,128,256]{2,1,0:T(8,128)S(1)} %collective-permute-done.30.partner_ref, f32[4,1024,256]{2,1,0:T(8,128)S(1)} %copy-done, ...), custom_call_target="tpu_custom_call" | custom-call | flops 805306368 | bytes 3145728 | tf_op jit(solution)/shard_map/pallas_call | solution.py:234
  135.9 1.5 %collective-permute-done.23.partner_ref = f32[2,128,256]{2,1,0:T(8,128)S(1)} collective-permute-done((f32[2,128,256]{2,1,0:T(8,128)S(1)}, f32[2,128,256]{2,1,0:T(8,128)S(1)}, u32[]{:S(2)}, u32[]{:S(2)}) %collective-permute-start.23) | collective-permute-done | bytes 262176 | tf_op jit(solution)/shard_map/ppermute | solution.py:24
  137.4 3.3 %shard_map.81 = f32[1024,512]{1,0:T(8,128)} custom-call(s32[1]{0:T(128)} %bitcast.where_ref, f32[1024,256]{1,0:T(8,128)S(1)} %get-tuple-element.44.x_ref, f32[2,128,256]{2,1,0:T(8,128)S(1)} %shard_map.77.own_ref, f32[2,128,256]{2,1,0:T(8,128)S(1)} %collective-permute-done.23.partner_ref, ...), custom_call_target="tpu_custom_call", output_to_operand_aliasing={{}: (6, {})} | custom-call | flops 805306368 | bytes 3145728 | tf_op jit(solution)/shard_map/pallas_call | solution.py:234
  (89 shorter events, 5.3 us)
Async XLA Ops:
  5.5 3.7 %copy-start.4 = (f32[32,512]{1,0:T(8,128)S(1)}, f32[32,512]{1,0:T(8,128)}, u32[]{:S(2)}) copy-start(f32[32,512]{1,0:T(8,128)} %param.11) | copy-start | bytes 196612
  5.5 3.7 %copy-start.6 = (f32[16,512]{1,0:T(8,128)S(1)}, f32[16,512]{1,0:T(8,128)}, u32[]{:S(2)}) copy-start(f32[16,512]{1,0:T(8,128)} %param.10) | copy-start | bytes 98308
  5.5 2.4 %collective-permute-start = (f32[640,256]{1,0:T(8,128)}, f32[640,256]{1,0:T(8,128)S(1)}, u32[]{:S(2)}, u32[]{:S(2)}) collective-permute-start(f32[640,256]{1,0:T(8,128)} %get-tuple-element.32), channel_id=1, source_target_pairs={{0,4},{4,0},{8,12},{12,8},{16,20},{20,16},{24,28},{28,24},{1,5},{5... | collective-permute-start | bytes 1966088 | tf_op jit(solution)/shard_map/ppermute | solution.py:24
  9.2 12.6 %collective-permute-start.5 = (f32[48,512]{1,0:T(8,128)S(1)}, f32[48,512]{1,0:T(8,128)S(1)}, u32[]{:S(2)}, u32[]{:S(2)}) collective-permute-start(f32[48,512]{1,0:T(8,128)S(1)} %pad_maximum_fusion.4), channel_id=1, source_target_pairs={{0,2},{1,3},{2,0},{3,1},{4,6},{5,7},{6,4},{7,5},{8,10},{9,11},{10,... | collective-permute-start | bytes 294920 | tf_op jit(solution)/shard_map/ppermute | solution.py:24
  13.2 14.9 %collective-permute-start.9 = (f32[128,256]{1,0:T(8,128)S(1)}, f32[128,256]{1,0:T(8,128)S(1)}, u32[]{:S(2)}, u32[]{:S(2)}) collective-permute-start(f32[128,256]{1,0:T(8,128)S(1)} %slice.119), channel_id=1, source_target_pairs={{0,2},{1,3},{2,0},{3,1},{4,6},{5,7},{6,4},{7,5},{8,10},{9,11},{10,... | collective-permute-start | bytes 393224 | tf_op jit(solution)/shard_map/ppermute | solution.py:24
  13.3 11.9 %collective-permute-start.1 = (f32[2,2,64,256]{3,2,1,0:T(8,128)S(1)}, f32[2,2,64,256]{3,2,1,0:T(8,128)S(1)}, u32[]{:S(2)}, u32[]{:S(2)}) collective-permute-start(f32[2,2,64,256]{3,2,1,0:T(8,128)S(1)} %slice_select_fusion.8), channel_id=1, source_target_pairs={{0,1},{1,0},{2,3},{3,2},{4,5},{5,4},{6,7},{7,6},{8,9},{9,8},{10,11... | collective-permute-start | bytes 786440 | tf_op jit(solution)/shard_map/ppermute | solution.py:24
  25.3 7.8 %collective-permute-start.2 = (f32[2,2,32,256]{3,2,1,0:T(8,128)S(1)}, f32[2,2,32,256]{3,2,1,0:T(8,128)S(1)}, u32[]{:S(2)}, u32[]{:S(2)}) collective-permute-start(f32[2,2,32,256]{3,2,1,0:T(8,128)S(1)} %slice_select_fusion.9), channel_id=1, source_target_pairs={{0,2},{1,3},{2,0},{3,1},{4,6},{5,7},{6,4},{7,5},{8,10},{9,11},{10,... | collective-permute-start | bytes 393224 | tf_op jit(solution)/shard_map/ppermute | solution.py:24
  28.1 7.4 %collective-permute-start.10 = (f32[128,256]{1,0:T(8,128)S(1)}, f32[128,256]{1,0:T(8,128)S(1)}, u32[]{:S(2)}, u32[]{:S(2)}) collective-permute-start(f32[128,256]{1,0:T(8,128)S(1)} %add.81), channel_id=1, source_target_pairs={{0,1},{1,0},{2,3},{3,2},{4,5},{5,4},{6,7},{7,6},{8,9},{9,8},{10,11... | collective-permute-start | bytes 393224 | tf_op jit(solution)/shard_map/ppermute | solution.py:24
  30.7 7.6 %collective-permute-start.6 = (f32[96,512]{1,0:T(8,128)S(1)}, f32[96,512]{1,0:T(8,128)S(1)}, u32[]{:S(2)}, u32[]{:S(2)}) collective-permute-start(f32[96,512]{1,0:T(8,128)S(1)} %pad_maximum_fusion.3), channel_id=1, source_target_pairs={{0,1},{1,0},{2,3},{3,2},{4,5},{5,4},{6,7},{7,6},{8,9},{9,8},{10,11... | collective-permute-start | bytes 589832 | tf_op jit(solution)/shard_map/ppermute | solution.py:24
  33.1 6.9 %collective-permute-start.3 = (f32[2,2,32,256]{3,2,1,0:T(8,128)S(1)}, f32[2,2,32,256]{3,2,1,0:T(8,128)S(1)}, u32[]{:S(2)}, u32[]{:S(2)}) collective-permute-start(f32[2,2,32,256]{3,2,1,0:T(8,128)S(1)} %select_add_fusion.1), channel_id=1, source_target_pairs={{0,8},{4,12},{8,0},{12,4},{16,24},{20,28},{24,16},{28,20},{1,9},{5... | collective-permute-start | bytes 393224 | tf_op jit(solution)/shard_map/ppermute | solution.py:24
  35.5 5.9 %collective-permute-start.11 = (f32[128,256]{1,0:T(8,128)S(1)}, f32[128,256]{1,0:T(8,128)S(1)}, u32[]{:S(2)}, u32[]{:S(2)}) collective-permute-start(f32[128,256]{1,0:T(8,128)S(1)} %add.82), channel_id=1, source_target_pairs={{0,8},{4,12},{8,0},{12,4},{16,24},{20,28},{24,16},{28,20},{1,9},{5... | collective-permute-start | bytes 393224 | tf_op jit(solution)/shard_map/ppermute | solution.py:24
  38.4 5.0 %collective-permute-start.7 = (f32[64,512]{1,0:T(8,128)S(1)}, f32[64,512]{1,0:T(8,128)S(1)}, u32[]{:S(2)}, u32[]{:S(2)}) collective-permute-start(f32[64,512]{1,0:T(8,128)S(1)} %bitcast.102), channel_id=1, source_target_pairs={{0,8},{4,12},{8,0},{12,4},{16,24},{20,28},{24,16},{28,20},{1,9},{5... | collective-permute-start | bytes 393224 | tf_op jit(solution)/shard_map/ppermute | solution.py:24
  41.4 3.8 %collective-permute-start.12 = (f32[2,128,256]{2,1,0:T(8,128)S(1)}, f32[2,128,256]{2,1,0:T(8,128)S(1)}, u32[]{:S(2)}, u32[]{:S(2)}) collective-permute-start(f32[2,128,256]{2,1,0:T(8,128)S(1)} %pad_maximum_fusion.2), channel_id=1, source_target_pairs={{0,4},{4,0},{8,12},{12,8},{16,20},{20,16},{24,28},{28,24},{1,5},{5... | collective-permute-start | bytes 786440 | tf_op jit(solution)/shard_map/ppermute | solution.py:24
  43.5 2.0 %collective-permute-start.8 = (f32[256,512]{1,0:T(8,128)S(1)}, f32[256,512]{1,0:T(8,128)S(1)}, u32[]{:S(2)}, u32[]{:S(2)}) collective-permute-start(f32[256,512]{1,0:T(8,128)S(1)} %pad_maximum_fusion), channel_id=1, source_target_pairs={{0,4},{4,0},{8,12},{12,8},{16,20},{20,16},{24,28},{28,24},{1,5},{5... | collective-permute-start | bytes 1572872 | tf_op jit(solution)/shard_map/ppermute | solution.py:24
  43.6 4.5 %collective-permute-start.4 = (f32[2,32,256]{2,1,0:T(8,128)S(1)}, f32[2,32,256]{2,1,0:T(8,128)S(1)}, u32[]{:S(2)}, u32[]{:S(2)}) collective-permute-start(f32[2,32,256]{2,1,0:T(8,128)S(1)} %bitcast.72), channel_id=1, source_target_pairs={{0,16},{4,20},{8,24},{12,28},{16,0},{20,4},{24,8},{28,12},{1,17},{... | collective-permute-start | bytes 196616 | tf_op jit(solution)/shard_map/ppermute | solution.py:24
  45.5 6.8 %copy-start.1 = (f32[4,1024,256]{2,1,0:T(8,128)S(1)}, f32[4,1024,256]{2,1,0:T(8,128)}, u32[]{:S(2)}) copy-start(f32[4,1024,256]{2,1,0:T(8,128)} %v_next_ref.5) | copy-start | bytes 12582916
  45.7 5.3 %copy-start.5 = (f32[64,512]{1,0:T(8,128)S(1)}, f32[64,512]{1,0:T(8,128)}, u32[]{:S(2)}) copy-start(f32[64,512]{1,0:T(8,128)} %param.12) | copy-start | bytes 393220
  45.7 6.6 %copy-start = (f32[4,1024,256]{2,1,0:T(8,128)S(1)}, f32[4,1024,256]{2,1,0:T(8,128)}, u32[]{:S(2)}) copy-start(f32[4,1024,256]{2,1,0:T(8,128)} %u_next_ref.7) | copy-start | bytes 12582916
  49.3 20.0 %copy-start.3 = (f32[128,512]{1,0:T(8,128)S(1)}, f32[128,512]{1,0:T(8,128)}, u32[]{:S(2)}) copy-start(f32[128,512]{1,0:T(8,128)} %param.13) | copy-start | bytes 786436
  49.3 9.7 %collective-permute-start.13 = (f32[2,32,256]{2,1,0:T(8,128)S(1)}, f32[2,32,256]{2,1,0:T(8,128)S(1)}, u32[]{:S(2)}, u32[]{:S(2)}) collective-permute-start(f32[2,32,256]{2,1,0:T(8,128)S(1)} %get-tuple-element.76), channel_id=1, source_target_pairs={{0,2},{1,3},{2,0},{3,1},{4,6},{5,7},{6,4},{7,5},{8,10},{9,11},{10,... | collective-permute-start | bytes 196616 | tf_op jit(solution)/shard_map/ppermute | solution.py:24
  51.1 11.1 %collective-permute-start.19 = (f32[64,512]{1,0:T(8,128)S(1)}, f32[64,512]{1,0:T(8,128)S(1)}, u32[]{:S(2)}, u32[]{:S(2)}) collective-permute-start(f32[64,512]{1,0:T(8,128)S(1)} %copy-done.5), channel_id=1, source_target_pairs={{0,2},{1,3},{2,0},{3,1},{4,6},{5,7},{6,4},{7,5},{8,10},{9,11},{10,... | collective-permute-start | bytes 393224 | tf_op jit(solution)/shard_map/ppermute | solution.py:24
  52.9 21.1 %copy-start.2 = (f32[1024,512]{1,0:T(8,128)S(1)}, f32[1024,512]{1,0:T(8,128)}, u32[]{:S(2)}) copy-start(f32[1024,512]{1,0:T(8,128)} %x1_ref.3) | copy-start | bytes 6291460
  53.0 17.8 %collective-permute-start.21 = (f32[256,256]{1,0:T(8,128)S(1)}, f32[256,256]{1,0:T(8,128)S(1)}, u32[]{:S(2)}, u32[]{:S(2)}) collective-permute-start(f32[256,256]{1,0:T(8,128)S(1)} %shard_map.76), channel_id=1, source_target_pairs={{0,1},{1,0},{2,3},{3,2},{4,5},{5,4},{6,7},{7,6},{8,9},{9,8},{10,11... | collective-permute-start | bytes 786440 | tf_op jit(solution)/shard_map/ppermute | solution.py:24
  54.8 8.5 %collective-permute-start.24 = (f32[2,32,256]{2,1,0:T(8,128)S(1)}, f32[2,32,256]{2,1,0:T(8,128)S(1)}, u32[]{:S(2)}, u32[]{:S(2)}) collective-permute-start(f32[2,32,256]{2,1,0:T(8,128)S(1)} %get-tuple-element.75), channel_id=1, source_target_pairs={{0,2},{1,3},{2,0},{3,1},{4,6},{5,7},{6,4},{7,5},{8,10},{9,11},{10,... | collective-permute-start | bytes 196616 | tf_op jit(solution)/shard_map/ppermute | solution.py:24
  59.0 10.1 %collective-permute-start.14 = (f32[2,64,256]{2,1,0:T(8,128)S(1)}, f32[2,64,256]{2,1,0:T(8,128)S(1)}, u32[]{:S(2)}, u32[]{:S(2)}) collective-permute-start(f32[2,64,256]{2,1,0:T(8,128)S(1)} %maximum_select_fusion.12), channel_id=1, source_target_pairs={{0,1},{1,0},{2,3},{3,2},{4,5},{5,4},{6,7},{7,6},{8,9},{9,8},{10,11... | collective-permute-start | bytes 393224 | tf_op jit(solution)/shard_map/ppermute | solution.py:24
  63.3 7.2 %collective-permute-start.25 = (f32[2,64,256]{2,1,0:T(8,128)S(1)}, f32[2,64,256]{2,1,0:T(8,128)S(1)}, u32[]{:S(2)}, u32[]{:S(2)}) collective-permute-start(f32[2,64,256]{2,1,0:T(8,128)S(1)} %maximum_select_fusion.13), channel_id=1, source_target_pairs={{0,1},{1,0},{2,3},{3,2},{4,5},{5,4},{6,7},{7,6},{8,9},{9,8},{10,11... | collective-permute-start | bytes 393224 | tf_op jit(solution)/shard_map/ppermute | solution.py:24
  69.2 4.9 %collective-permute-start.15 = (f32[2,128,256]{2,1,0:T(8,128)S(1)}, f32[2,128,256]{2,1,0:T(8,128)S(1)}, u32[]{:S(2)}, u32[]{:S(2)}) collective-permute-start(f32[2,128,256]{2,1,0:T(8,128)S(1)} %maximum_select_fusion.7.own_ref), channel_id=1, source_target_pairs={{0,4},{4,0},{8,12},{12,8},{16,20},{20,16},{24,28},{28,24},{1,5},{5... | collective-permute-start | bytes 786440 | tf_op jit(solution)/shard_map/ppermute | solution.py:24
  69.3 20.4 %collective-permute-start.20 = (f32[256,512]{1,0:T(8,128)S(1)}, f32[256,512]{1,0:T(8,128)S(1)}, u32[]{:S(2)}, u32[]{:S(2)}) collective-permute-start(f32[256,512]{1,0:T(8,128)S(1)} %pad_maximum_fusion.1), channel_id=1, source_target_pairs={{0,1},{1,0},{2,3},{3,2},{4,5},{5,4},{6,7},{7,6},{8,9},{9,8},{10,11... | collective-permute-start | bytes 1572872 | tf_op jit(solution)/shard_map/ppermute | solution.py:24
  70.6 9.1 %collective-permute-start.26 = (f32[2,128,256]{2,1,0:T(8,128)S(1)}, f32[2,128,256]{2,1,0:T(8,128)S(1)}, u32[]{:S(2)}, u32[]{:S(2)}) collective-permute-start(f32[2,128,256]{2,1,0:T(8,128)S(1)} %maximum_select_fusion.9.own_ref), channel_id=1, source_target_pairs={{0,4},{4,0},{8,12},{12,8},{16,20},{20,16},{24,28},{28,24},{1,5},{5... | collective-permute-start | bytes 786440 | tf_op jit(solution)/shard_map/ppermute | solution.py:24
  70.8 50.1 %collective-permute-start.22 = (f32[256,256]{1,0:T(8,128)S(1)}, f32[256,256]{1,0:T(8,128)S(1)}, u32[]{:S(2)}, u32[]{:S(2)}) collective-permute-start(f32[256,256]{1,0:T(8,128)S(1)} %add.86.gram_own), channel_id=1, source_target_pairs={{0,2},{1,3},{2,0},{3,1},{4,6},{5,7},{6,4},{7,5},{8,10},{9,11},{10,... | collective-permute-start | bytes 786440 | tf_op jit(solution)/shard_map/ppermute | solution.py:24
  78.6 16.7 %collective-permute-start.16 = (f32[256,256]{1,0:T(8,128)S(1)}, f32[256,256]{1,0:T(8,128)S(1)}, u32[]{:S(2)}, u32[]{:S(2)}) collective-permute-start(f32[256,256]{1,0:T(8,128)S(1)} %get-tuple-element.46), channel_id=1, source_target_pairs={{0,1},{1,0},{2,3},{3,2},{4,5},{5,4},{6,7},{7,6},{8,9},{9,8},{10,11... | collective-permute-start | bytes 786440 | tf_op jit(solution)/shard_map/ppermute | solution.py:24
  84.2 20.6 %collective-permute-start.27 = (f32[256,256]{1,0:T(8,128)S(1)}, f32[256,256]{1,0:T(8,128)S(1)}, u32[]{:S(2)}, u32[]{:S(2)}) collective-permute-start(f32[256,256]{1,0:T(8,128)S(1)} %get-tuple-element.56), channel_id=1, source_target_pairs={{0,1},{1,0},{2,3},{3,2},{4,5},{5,4},{6,7},{7,6},{8,9},{9,8},{10,11... | collective-permute-start | bytes 786440 | tf_op jit(solution)/shard_map/ppermute | solution.py:24
  95.3 21.1 %collective-permute-start.17 = (f32[2,1,128,256]{3,2,1,0:T(8,128)S(1)}, f32[2,1,128,256]{3,2,1,0:T(8,128)S(1)}, u32[]{:S(2)}, u32[]{:S(2)}) collective-permute-start(f32[2,1,128,256]{3,2,1,0:T(8,128)S(1)} %bitcast.93), channel_id=1, source_target_pairs={{0,2},{1,3},{2,0},{3,1},{4,6},{5,7},{6,4},{7,5},{8,10},{9,11},{10,... | collective-permute-start | bytes 786440 | tf_op jit(solution)/shard_map/ppermute | solution.py:24
  104.8 16.0 %collective-permute-start.28 = (f32[2,1,128,256]{3,2,1,0:T(8,128)S(1)}, f32[2,1,128,256]{3,2,1,0:T(8,128)S(1)}, u32[]{:S(2)}, u32[]{:S(2)}) collective-permute-start(f32[2,1,128,256]{3,2,1,0:T(8,128)S(1)} %bitcast.94), channel_id=1, source_target_pairs={{0,2},{1,3},{2,0},{3,1},{4,6},{5,7},{6,4},{7,5},{8,10},{9,11},{10,... | collective-permute-start | bytes 786440 | tf_op jit(solution)/shard_map/ppermute | solution.py:24
  116.5 7.8 %collective-permute-start.18 = (f32[1,128,256]{2,1,0:T(8,128)S(1)}, f32[1,128,256]{2,1,0:T(8,128)S(1)}, u32[]{:S(2)}, u32[]{:S(2)}) collective-permute-start(f32[1,128,256]{2,1,0:T(8,128)S(1)} %bitcast.69), channel_id=1, source_target_pairs={{0,4},{4,0},{8,12},{12,8},{16,20},{20,16},{24,28},{28,24},{1,5},{5... | collective-permute-start | bytes 393224 | tf_op jit(solution)/shard_map/ppermute | solution.py:24
  120.8 1.4 %collective-permute-start.29 = (f32[1,128,256]{2,1,0:T(8,128)S(1)}, f32[1,128,256]{2,1,0:T(8,128)S(1)}, u32[]{:S(2)}, u32[]{:S(2)}) collective-permute-start(f32[1,128,256]{2,1,0:T(8,128)S(1)} %bitcast.70), channel_id=1, source_target_pairs={{0,4},{4,0},{8,12},{12,8},{16,20},{20,16},{24,28},{28,24},{1,5},{5... | collective-permute-start | bytes 393224 | tf_op jit(solution)/shard_map/ppermute | solution.py:24
  123.4 9.2 %collective-permute-start.30 = (f32[2,128,256]{2,1,0:T(8,128)S(1)}, f32[2,128,256]{2,1,0:T(8,128)S(1)}, u32[]{:S(2)}, u32[]{:S(2)}) collective-permute-start(f32[2,128,256]{2,1,0:T(8,128)S(1)} %shard_map.79.own_ref), channel_id=1, source_target_pairs={{0,1},{1,0},{2,3},{3,2},{4,5},{5,4},{6,7},{7,6},{8,9},{9,8},{10,11... | collective-permute-start | bytes 786440 | tf_op jit(solution)/shard_map/ppermute | solution.py:24
  125.4 12.0 %collective-permute-start.23 = (f32[2,128,256]{2,1,0:T(8,128)S(1)}, f32[2,128,256]{2,1,0:T(8,128)S(1)}, u32[]{:S(2)}, u32[]{:S(2)}) collective-permute-start(f32[2,128,256]{2,1,0:T(8,128)S(1)} %shard_map.77.own_ref), channel_id=1, source_target_pairs={{0,1},{1,0},{2,3},{3,2},{4,5},{5,4},{6,7},{7,6},{8,9},{9,8},{10,11... | collective-permute-start | bytes 786440 | tf_op jit(solution)/shard_map/ppermute | solution.py:24

commit v3 on v1

v3 whole, which is shorter than its diff:
```python
import functools

import jax
import jax.numpy as jnp
from jax import lax
from jax.experimental import pallas as pl
from jax.experimental.pallas import tpu as pltpu
from jax.sharding import PartitionSpec as P

CHUNKS = 2
STEPS = 2
MIB = 1 << 20
LOW = -1
MID = 24
LAST = 24


def bits_of(axis):
    return lax.axis_size(axis).bit_length() - 1


def swap(value, place):
    sub_bits = bits_of("sub")
    axis, bit = ("sub", place) if place < sub_bits else ("rows", place - sub_bits)
    return lax.ppermute(value, axis, [(i, i ^ 1 << bit) for i in range(lax.axis_size(axis))])


def digit(place):
    position = lax.axis_index("rows") * lax.axis_size("sub") + lax.axis_index("sub")
    return (position >> place) & 1


def digits(*places):
    return jnp.stack([digit(place) for place in places]).astype(jnp.int32)


def halve(value, dim, place):
    first, second = jnp.split(value, 2, dim)
    lower = digit(place) == 0
    return jnp.where(lower, first, second) + swap(jnp.where(lower, second, first), place)


def ordered(own, other, dim, place):
    lower = digit(place) == 0
    return jnp.where(lower, jnp.concatenate([own, other], dim), jnp.concatenate([other, own], dim))


def widen(value, dim, place):
    return ordered(value, swap(value, place), dim, place)


def common_places(count):
    sub_bits = bits_of("sub")
    places = list(range(count))
    if count > sub_bits:
        places.remove(sub_bits)
        places.insert(0, sub_bits)
    return places


def swap_all(values, place):
    width = values[0].shape[-1]
    sent = swap(jnp.concatenate([value.reshape(-1, width) for value in values], 0), place)
    ends = [0]
    for value in values:
        ends.append(ends[-1] + value.size // width)
    return [sent[ends[i] : ends[i + 1]].reshape(value.shape) for i, value in enumerate(values)]


def after(value, token):
    return lax.optimization_barrier((value, token))[0]


def halves(value):
    high = value.astype(jnp.bfloat16)
    return high, (value - high.astype(jnp.float32)).astype(jnp.bfloat16)


def product(left, right, left_dim, right_dim):
    dims = (((left_dim,), (right_dim,)), ((), ()))
    left = jnp.concatenate([left[0], left[0], left[1]], left_dim)
    right = jnp.concatenate([right[0], right[1], right[0]], right_dim)
    return lax.dot_general(left, right, dims, preferred_element_type=jnp.float32)


def first_kernel(where_ref, x_ref, u_ref, v_ref, v_next_ref, keep_ref, send_ref, total, total_next):
    step = pl.program_id(0)

    @pl.when(step == 0)
    def _():
        total[...] = jnp.zeros_like(total)
        total_next[...] = jnp.zeros_like(total_next)

    sides = x_ref.shape[1]
    x, v, v_next = halves(x_ref[...]), halves(v_ref[0]), halves(v_next_ref[0])
    total[...] += product(x, v, 0, 0)
    total_next[:sides] += product(x, v_next, 0, 0)
    total_next[sides:] += product(halves(u_ref[0]), v_next, 0, 0)

    @pl.when(step == pl.num_programs(0) - 1)
    def _():
        where = where_ref[0]
        width = sides // (2 * CHUNKS)
        for ref, side in ((keep_ref, where), (send_ref, 1 - where)):
            for level, each in enumerate((total, total_next)):
                for k in range(CHUNKS):
                    start = pl.multiple_of((2 * k + side) * width, width)
                    at = (level * CHUNKS + k) * width
                    ref[at : at + width, :] = each[pl.ds(start, width), :]
        rank = u_ref.shape[2]
        at = 2 * CHUNKS * width
        for ref, side in ((keep_ref, where), (send_ref, 1 - where)):
            start = pl.multiple_of(sides + side * (rank // 2), rank // 2)
            ref[at:, :] = total_next[pl.ds(start, rank // 2), :]


def slab(rows, rank, level):
    return pl.BlockSpec((1, rows, rank), lambda i, *_: (level, i, 0))


def whole(shape):
    return pl.BlockSpec(shape, lambda *_: (0,) * len(shape))


def shapes(*values):
    return [jax.ShapeDtypeStruct(value, jnp.float32) for value in values]


SMEM = pl.BlockSpec(memory_space=pltpu.SMEM)


def first_sums(where, x, bases_u, bases_v, level):
    rows, sides = x.shape
    rank = bases_u.shape[2]
    block = rows // STEPS
    out = (sides + rank // 2, rank)
    return pl.pallas_call(
        first_kernel,
        grid=(STEPS,),
        in_specs=[
            SMEM,
            pl.BlockSpec((block, sides), lambda i: (i, 0)),
            slab(block, rank, level),
            slab(block, rank, level),
            slab(block, rank, level + 1),
        ],
        out_specs=[whole(out)] * 2,
        out_shape=shapes(out, out),
        scratch_shapes=[pltpu.VMEM((sides, rank), jnp.float32), pltpu.VMEM((sides + rank, rank), jnp.float32)],
        compiler_params=pltpu.CompilerParams(vmem_limit_bytes=60 * MIB),
        cost_estimate=pl.CostEstimate(flops=6 * rows * rank * (2 * sides + rank), bytes_accessed=5 * rows * rank * 4, transcendentals=0),
    )(where, x, bases_u, bases_v, bases_v)


def whole_factors(where, own_ref, partner_ref):
    own, partner = own_ref[...], partner_ref[...]
    first, second = jnp.where(where == 0, own, partner), jnp.where(where == 0, partner, own)
    return [jnp.concatenate([first[k], second[k]], 0) for k in range(2)]


def update(x, left, left_next, factors):
    return x - (product(halves(left), factors[0], 1, 1) + product(halves(left_next), factors[1], 1, 1))


def middle_kernel(chunk, level, where_ref, old_ref, own_ref, partner_ref, u_ref, v_ref, x_ref, keep_ref, send_ref, total, total_next):
    factors = [halves(each) for each in whole_factors(where_ref[0], own_ref, partner_ref)]
    rows, columns = x_ref.shape
    block = rows // STEPS
    sums = None
    for step in range(STEPS):
        at = slice(step * block, (step + 1) * block)
        x = old_ref[at, chunk * columns : (chunk + 1) * columns]
        x = update(x, u_ref[level, at], u_ref[level + 1, at], factors)
        x_ref[at, :] = x
        x = halves(x)
        terms = [product(x, halves(v_ref[level + 2 + k, at]), 0, 0) for k in range(2)]
        sums = terms if sums is None else [a + b for a, b in zip(sums, terms)]
    total[...], total_next[...] = sums
    width = columns // 2
    for ref, side in ((keep_ref, where_ref[1]), (send_ref, 1 - where_ref[1])):
        start = pl.multiple_of(side * width, width)
        ref[:width, :] = total[pl.ds(start, width), :]
        ref[width:, :] = total_next[pl.ds(start, width), :]


VMEM = pl.BlockSpec(memory_space=pltpu.VMEM)
ANY = pl.BlockSpec(memory_space=pl.ANY)


def middle(where, chunk, x, own, partner, bases_u, bases_v, level):
    rows, sides = x.shape
    rank = bases_u.shape[2]
    width = sides // (2 * CHUNKS)
    out = (2 * width, rank)
    return pl.pallas_call(
        functools.partial(middle_kernel, chunk, level),
        in_specs=[SMEM] + [VMEM] * 5,
        out_specs=[VMEM] * 3,
        out_shape=shapes((rows, 2 * width), out, out),
        scratch_shapes=[pltpu.VMEM((2 * width, rank), jnp.float32)] * 2,
        compiler_params=pltpu.CompilerParams(vmem_limit_bytes=MID * MIB),
        cost_estimate=pl.CostEstimate(flops=24 * rows * rank * width * 2, bytes_accessed=4 * rows * rank * 4, transcendentals=0),
    )(where, x, own, partner, bases_u, bases_v)


def last_kernel(chunk, level, where_ref, x_ref, own_ref, partner_ref, u_ref, *refs):
    out_ref, found, sems = refs[-3:]
    factors = [halves(each) for each in whole_factors(where_ref[0], own_ref, partner_ref)]
    rows, columns = x_ref.shape
    block = rows // STEPS
    copies = []
    for step in range(STEPS):
        at = slice(step * block, (step + 1) * block)
        found[at, :] = update(x_ref[at, :], u_ref[level, at], u_ref[level + 1, at], factors)
        place = (pl.ds(step * block, block), pl.ds(chunk * columns, columns))
        copies.append(pltpu.make_async_copy(found.at[pl.ds(step * block, block)], out_ref.at[place], sems.at[step]))
        copies[-1].start()
    for copy in copies:
        copy.wait()


def last(where, chunk, x, own, partner, bases_u, level, into, sides):
    rows = x.shape[0]
    rank = bases_u.shape[2]
    width = sides // (2 * CHUNKS)
    more = [] if into is None else [into]
    return pl.pallas_call(
        functools.partial(last_kernel, chunk, level),
        in_specs=[SMEM] + [VMEM] * 4 + [ANY] * len(more),
        out_specs=ANY,
        out_shape=jax.ShapeDtypeStruct((rows, sides), jnp.float32),
        scratch_shapes=[pltpu.VMEM((rows, 2 * width), jnp.float32), pltpu.SemaphoreType.DMA((STEPS,))],
        input_output_aliases={5: 0} if more else {},
        compiler_params=pltpu.CompilerParams(vmem_limit_bytes=LAST * MIB),
        cost_estimate=pl.CostEstimate(flops=12 * rows * rank * width * 2, bytes_accessed=3 * rows * rank * 4, transcendentals=0),
    )(where, x, own, partner, bases_u, *more)


def gram_kernel(level, u_ref, v_ref, out_ref):
    out_ref[...] = product(halves(u_ref[level]), halves(v_ref[level + 1]), 0, 0)


def gram_term(bases_u, bases_v, level):
    rows, rank = bases_u.shape[1:]
    return pl.pallas_call(
        functools.partial(gram_kernel, level),
        in_specs=[VMEM] * 2,
        out_specs=VMEM,
        out_shape=jax.ShapeDtypeStruct((rank, rank), jnp.float32),
        compiler_params=pltpu.CompilerParams(vmem_limit_bytes=24 * MIB),
        cost_estimate=pl.CostEstimate(flops=6 * rows * rank * rank, bytes_accessed=2 * rows * rank * 4, transcendentals=0),
    )(bases_u, bases_v)


def checkpoint(*values):
    return lax.optimization_barrier(values)


def both_halves(rows):
    return jnp.stack(jnp.split(rows, 2, 1))


class Gather:
    def __init__(self, rows):
        self.values = [both_halves(each) for each in rows]
        self.seen = [[] for _ in rows]

    def begin(self, place, use, extra=()):
        grown = []
        for k in use:
            at = 1 + sum(other > place for other in self.seen[k])
            self.seen[k].append(place)
            grown.append((jnp.expand_dims(self.values[k], at), at))
        sent = [value for value, _ in grown] + list(extra)
        self.held = place, use, grown
        return swap_all(sent, place)

    def end(self, received):
        place, use, grown = self.held
        for k, (value, at), partner in zip(use, grown, received):
            self.values[k] = ordered(value, partner, at, place)
        return received[len(use) :]

    def sides(self, k, place):
        first, second = self.values[k].reshape(2, -1, self.values[k].shape[-1])
        lower = digit(place) == 0
        return jnp.where(lower, first, second), jnp.where(lower, second, first)


def factors_kernel(upper, upper_other, own, sibling, k_own, k_sibling, next_own, next_sibling, gram_own, gram_sibling, out_ref):
    def part(ref):
        return halves(ref[...])

    found = product(part(upper), part(k_own), 1, 1) + product(part(upper_other), part(k_sibling), 1, 1)
    high = halves(found)
    own = halves(own[...] - product(high, part(gram_own), 1, 0))
    sibling = halves(sibling[...] - product(high, part(gram_sibling), 1, 0))
    found_next = product(own, part(next_own), 1, 1) + product(sibling, part(next_sibling), 1, 1)
    count, _, width, _ = out_ref.shape
    for k in range(count):
        out_ref[k, 0] = found[k * width : (k + 1) * width]
        out_ref[k, 1] = found_next[k * width : (k + 1) * width]


def factors(reduced, grams, coupling):
    count, width, rank = reduced[0].shape
    reduced = [value.reshape(count * width, rank) for value in reduced]
    return pl.pallas_call(
        factors_kernel,
        out_shape=jax.ShapeDtypeStruct((count, 2, width, rank), jnp.float32),
        compiler_params=pltpu.CompilerParams(vmem_limit_bytes=16 * MIB),
        cost_estimate=pl.CostEstimate(flops=36 * count * width * rank * rank, bytes_accessed=6 * rank * rank * 4, transcendentals=0),
    )(*reduced, *coupling[0], *coupling[1], *grams)


def upper_kernel(upper, upper_other, own, k_own, k_sibling, gram, factors_ref, own_ref):
    def part(ref):
        return halves(ref[...])

    found = product(part(upper), part(k_own), 1, 1) + product(part(upper_other), part(k_sibling), 1, 1)
    factors_ref[...] = found
    own_ref[...] = own[...] - product(halves(found), part(gram), 1, 0)


def upper_factors(upper, upper_other, own, gram, coupling):
    width, rank = own.shape
    return pl.pallas_call(
        upper_kernel,
        out_shape=shapes((width, rank), (width, rank)),
        compiler_params=pltpu.CompilerParams(vmem_limit_bytes=16 * MIB),
        cost_estimate=pl.CostEstimate(flops=18 * width * rank * rank, bytes_accessed=3 * rank * rank * 4, transcendentals=0),
    )(upper, upper_other, own, *coupling, gram)


def lower_kernel(upper, own, sibling, k_own, k_sibling, out_ref):
    def part(ref):
        return halves(ref[...])

    out_ref[0] = upper[...]
    out_ref[1] = product(part(own), part(k_own), 1, 1) + product(part(sibling), part(k_sibling), 1, 1)


def lower_factors(upper, own, sibling, coupling):
    return pl.pallas_call(
        lower_kernel,
        out_shape=jax.ShapeDtypeStruct((2, *own.shape), jnp.float32),
        compiler_params=pltpu.CompilerParams(vmem_limit_bytes=16 * MIB),
        cost_estimate=pl.CostEstimate(flops=12 * own.size * own.shape[1], bytes_accessed=2 * own.shape[1] ** 2 * 4, transcendentals=0),
    )(upper, own, sibling, *coupling)


def local(right_sides, bases_u, bases_v, couple_first, couple_second, couple_third, couple_fourth):
    couples = (couple_first, couple_second, couple_third, couple_fourth)
    sides, rank = right_sides.shape[1], bases_u.shape[2]
    width = sides // (2 * CHUNKS)
    total_bits = bits_of("sub") + bits_of("rows")
    sibling, sibling_next = total_bits - 2, total_bits - 4
    places, places_next = common_places(sibling), common_places(sibling_next)

    near, far, low = Gather(couples[:2]), Gather(couples[2:3]), Gather(couples[3:])
    inner = places[1:]
    behind = inner[::-1]
    far_order = places_next[::-1]
    far_order.insert(len(far_order) - 1, sibling_next)

    keep, send = first_sums(digits(places[0]), right_sides, bases_u, bases_v, 0)
    sums = keep + swap(send, places[0])
    sums, near.values, far.values = checkpoint(sums, near.values, far.values)
    main, gram = sums[:sides].reshape(2, CHUNKS, width, rank), sums[sides:]
    for step, place in enumerate(inner):
        main = halve(main, 2, place)
        (other,) = near.end(near.begin(behind[step], (0, 1), (gram,)))
        gram = gram + other
        main, gram, near.values, far.values = checkpoint(main, gram, near.values, far.values)
    gram_other, other = near.end(near.begin(sibling, (0,), (gram, main)))
    upper = main[0] + other[0]
    for place in far_order[:-1]:
        far.end(far.begin(place, (0,)))
    term = gram_term(bases_u, bases_v, 2)
    for place in places_next[:-1]:
        term = term + swap(term, place)
    term_other = swap(term, places_next[-1])
    upper_other = swap(upper, sibling + 1)
    pair = jnp.stack([gram, gram_other])
    (pair_partner,) = near.end(near.begin(places[0], (0, 1), (pair,)))
    far.values = after(far.values, upper)
    received = far.begin(far_order[-1], (0,))
    grams = ordered(pair, pair_partner, 1, places[0])
    coupling = near.sides(0, sibling + 1), near.sides(1, sibling)
    found = factors((upper, upper_other, main[1], other[1]), grams, coupling)
    for place in behind[:-1]:
        found = widen(found, 2, place)
    found, term_other, received = checkpoint(found, term_other, received)
    found = [widen(each, 1, place) for each in found for place in behind[-1:]]
    term = term + term_other
    far.end(received)

    where = digits(places[0], places_next[0])
    parts, mains = [], []
    for k, own in enumerate(found):
        part, keep, send = middle(where, k, right_sides, own, swap(own, places[0]), bases_u, bases_v, 0)
        parts.append(part)
        main = (keep + swap(send, places_next[0])).reshape(2, width, rank)
        for place in places_next[1:]:
            main = halve(main, 1, place)
        mains.append(main)
    low.values = after(low.values, mains[LOW])
    for place in places_next[::-1]:
        low.end(low.begin(place, (0,)))
    coupling = far.sides(0, sibling_next + 1), low.sides(0, sibling_next)
    first, done = [], None
    for main in mains:
        other = swap(main[0], sibling_next)
        upper = main[0] + (after(other, done) if first else other)
        first.append(upper_factors(upper, swap(upper, sibling_next + 1), main[1], term, coupling[0]))
        done = first[-1]
    solved, found = None, []
    for part, (upper, own) in zip(parts, first):
        other = swap(own, sibling_next)
        own = lower_factors(upper, own, after(other, done) if found else other, coupling[1])
        found.append(own)
        done = own
    for k, own in enumerate(found):
        for place in places_next[:0:-1]:
            own = widen(own, 1, place)
        partner = swap(own, places_next[0])
        solved = last(digits(places_next[0]), k, parts[k], own, after(partner, solved) if k else partner, bases_u, 2, solved, sides)
    return solved


def solution(mesh):
    placed = (
        P(("rows", "sub"), None),
        P(None, ("rows", "sub"), None),
        P(None, ("rows", "sub"), None),
        P(("rows", "sub"), None),
        P(("rows", "sub"), None),
        P(("rows", "sub"), None),
        P(("rows", "sub"), None),
    )
    return jax.shard_map(
        local, mesh=mesh, in_specs=placed, out_specs=P(("rows", "sub"), None), check_vma=False
    )
```

time: 175 us -> 125 us (0.71)
  waiting for transfers between devices: 112 us -> 69.3 us
  matrix products: 23.9 us -> 0 us
  Pallas kernels: 0 us -> 18.7 us
  starting transfers between devices: 27.5 us -> 33.4 us
  local copies, waits for them, and re-layouts: 4.9 us -> 0.34 us
  other arithmetic: 5.34 us -> 2.35 us
    ppermute x32 -> x27, waiting for transfers between devices: 112 us -> 69.3 us  [swap(): lax.ppermute(value, axis, [(i, i ^ 1 << bit) for i in range(lax.axis_size...]
    dot_general x18 -> x0, matrix products: 23.9 us -> none  [dot(): lax.dot_general(left, right, (((left_dim,), (right_dim,)), ((), ())), pre...]
    pallas_call x0 -> x11, Pallas kernels: none -> 18.7 us  [the longest x1 5.55 us: first_sums(): pl.pallas_call(first_kernel, grid=(STEPS,), in_specs=[SMEM, pl.BlockSpec(...]
    ppermute x32 -> x27, starting transfers between devices: 27.5 us -> 33.4 us  [swap(): lax.ppermute(value, axis, [(i, i ^ 1 << bit) for i in range(lax.axis_size...]
    sub x1 -> x0, local copies, waits for them, and re-layouts: 2.88 us -> none  [local(): part = part - dot(bases_u[level + k], factors[k], 1, 1)]
    unnamed x11 -> x18, local copies, waits for them, and re-layouts: 2.02 us -> 0.05 us
    select_n x14 -> x15, other arithmetic: 2.17 us -> 0.38 us  [ordered(): jnp.where(lower, jnp.concatenate([own, other], dim), jnp.concatenate([oth...]
  transfers between devices with their start and end apart: 32 -> 27, of which waited for: 13 -> 19; matrix products, arithmetic and copies ran while one was open for 9% -> 1% of each run, Pallas kernels for 0% -> 9%
where the time goes in v3:
time: 125 us
  waiting for transfers between devices  69.3 us (55%)
  starting transfers between devices  33.4 us (27%)
  Pallas kernels  18.7 us (15%)
  other arithmetic  2.35 us (2%)
    ppermute x27, waiting for transfers between devices, swap(): lax.ppermute(value, axis, [(i, i ^ 1 << bit) for i in range(lax.axis_size...  69.3 us
    ppermute x27, starting transfers between devices, swap(): lax.ppermute(value, axis, [(i, i ^ 1 << bit) for i in range(lax.axis_size...  33.4 us
    pallas_call x1, Pallas kernels, first_sums(): pl.pallas_call(first_kernel, grid=(STEPS,), in_specs=[SMEM, pl.BlockSpec(...  5.55 us
    pallas_call x2, Pallas kernels, middle(): pl.pallas_call(functools.partial(middle_kernel, chunk, level), in_specs=[...  5.16 us
    pallas_call x2, Pallas kernels, last(): pl.pallas_call(functools.partial(last_kernel, chunk, level), in_specs=[SM...  4.08 us
  transfers between devices with their start and end apart: 27, of which 19 were waited for; matrix products, arithmetic and copies ran while one was open for 1% of the time, Pallas kernels for 9%

profile of v3, /device:TPU:0, one launch (start us, length us, event | category | flops | bytes accessed | tf_op | source)
XLA Modules:
  0.0 124.7 jit_solution(9190129793949582489)
XLA Ops:
  0.0 5.5 %shard_map.73 = (f32[640,256]{1,0:T(8,128)}, f32[640,256]{1,0:T(8,128)}) custom-call(s32[1]{0:T(128)} %bitcast.1.where_ref, f32[1024,512]{1,0:T(8,128)} %old_ref.3, f32[4,1024,256]{2,1,0:T(8,128)} %u_ref.11, f32[4,1024,256]{2,1,0:T(8,128)} %v_ref.7, f32[4,1024,256]{2,1,0:T(8,128)} %v_ref.7), custom_call_target="tpu_custom_call" | custom-call | flops 2013265920 | bytes 5242880 | tf_op jit(solution)/shard_map/pallas_call | solution.py:137
  5.6 0.5 collective-permute-start
  6.1 1.8 %collective-permute-done = f32[640,256]{1,0:T(8,128)S(1)} collective-permute-done((f32[640,256]{1,0:T(8,128)}, f32[640,256]{1,0:T(8,128)S(1)}, u32[]{:S(2)}, u32[]{:S(2)}) %collective-permute-start) | collective-permute-done | bytes 655392 | tf_op jit(solution)/shard_map/ppermute | solution.py:25
  7.9 1.2 add.28
  9.2 4.0 %collective-permute-start.2 = (f32[224,256]{1,0:T(8,128)S(1)}, f32[224,256]{1,0:T(8,128)S(1)}, u32[]{:S(2)}, u32[]{:S(2)}) collective-permute-start(f32[224,256]{1,0:T(8,128)S(1)} %pad_maximum_fusion.5), channel_id=1, source_target_pairs={{0,2},{1,3},{2,0},{3,1},{4,6},{5,7},{6,4},{7,5},{8,10},{9,11},{10,... | collective-permute-start | bytes 688136 | tf_op jit(solution)/shard_map/ppermute | solution.py:25
  13.3 1.6 %collective-permute-start.1 = (f32[2,2,64,256]{3,2,1,0:T(8,128)S(1)}, f32[2,2,64,256]{3,2,1,0:T(8,128)S(1)}, u32[]{:S(2)}, u32[]{:S(2)}) collective-permute-start(f32[2,2,64,256]{3,2,1,0:T(8,128)S(1)} %slice_select_fusion.8), channel_id=1, source_target_pairs={{0,1},{1,0},{2,3},{3,2},{4,5},{5,4},{6,7},{7,6},{8,9},{9,8},{10,11... | collective-permute-start | bytes 786440 | tf_op jit(solution)/shard_map/ppermute | solution.py:25
  14.9 9.2 %collective-permute-done.2 = f32[224,256]{1,0:T(8,128)S(1)} collective-permute-done((f32[224,256]{1,0:T(8,128)S(1)}, f32[224,256]{1,0:T(8,128)S(1)}, u32[]{:S(2)}, u32[]{:S(2)}) %collective-permute-start.2) | collective-permute-done | bytes 229408 | tf_op jit(solution)/shard_map/ppermute | solution.py:25
  24.2 0.9 collective-permute-done.1
  25.2 1.3 %collective-permute-start.3 = (f32[2,2,32,256]{3,2,1,0:T(8,128)S(1)}, f32[2,2,32,256]{3,2,1,0:T(8,128)S(1)}, u32[]{:S(2)}, u32[]{:S(2)}) collective-permute-start(f32[2,2,32,256]{3,2,1,0:T(8,128)S(1)} %slice_select_fusion.9), channel_id=1, source_target_pairs={{0,2},{1,3},{2,0},{3,1},{4,6},{5,7},{6,4},{7,5},{8,10},{9,11},{10,... | collective-permute-start | bytes 393224 | tf_op jit(solution)/shard_map/ppermute | solution.py:25
  26.6 2.0 %collective-permute-start.4 = (f32[320,256]{1,0:T(8,128)S(1)}, f32[320,256]{1,0:T(8,128)S(1)}, u32[]{:S(2)}, u32[]{:S(2)}) collective-permute-start(f32[320,256]{1,0:T(8,128)S(1)} %pad_maximum_fusion.2), channel_id=1, source_target_pairs={{0,1},{1,0},{2,3},{3,2},{4,5},{5,4},{6,7},{7,6},{8,9},{9,8},{10,11... | collective-permute-start | bytes 983048 | tf_op jit(solution)/shard_map/ppermute | solution.py:25
  28.6 4.2 %collective-permute-done.3 = f32[2,2,32,256]{3,2,1,0:T(8,128)S(1)} collective-permute-done((f32[2,2,32,256]{3,2,1,0:T(8,128)S(1)}, f32[2,2,32,256]{3,2,1,0:T(8,128)S(1)}, u32[]{:S(2)}, u32[]{:S(2)}) %collective-permute-start.3) | collective-permute-done | bytes 131104 | tf_op jit(solution)/shard_map/ppermute | solution.py:25
  32.9 4.7 %collective-permute-done.4 = f32[320,256]{1,0:T(8,128)S(1)} collective-permute-done((f32[320,256]{1,0:T(8,128)S(1)}, f32[320,256]{1,0:T(8,128)S(1)}, u32[]{:S(2)}, u32[]{:S(2)}) %collective-permute-start.4) | collective-permute-done | bytes 327712 | tf_op jit(solution)/shard_map/ppermute | solution.py:25
  37.7 1.6 %collective-permute-start.5 = (f32[384,256]{1,0:T(8,128)S(1)}, f32[384,256]{1,0:T(8,128)S(1)}, u32[]{:S(2)}, u32[]{:S(2)}) collective-permute-start(f32[384,256]{1,0:T(8,128)S(1)} %pad_maximum_fusion.1), channel_id=1, source_target_pairs={{0,8},{4,12},{8,0},{12,4},{16,24},{20,28},{24,16},{28,20},{1,9},{5... | collective-permute-start | bytes 1179656 | tf_op jit(solution)/shard_map/ppermute | solution.py:25
  39.2 0.6 shard_map.75
  39.9 1.1 collective-permute-start.9
  41.0 2.6 %collective-permute-start.10 = (f32[128,256]{1,0:T(8,128)S(1)}, f32[128,256]{1,0:T(8,128)S(1)}, u32[]{:S(2)}, u32[]{:S(2)}) collective-permute-start(f32[128,256]{1,0:T(8,128)S(1)} %bitcast.131), channel_id=1, source_target_pairs={{0,2},{1,3},{2,0},{3,1},{4,6},{5,7},{6,4},{7,5},{8,10},{9,11},{10,... | collective-permute-start | bytes 393224 | tf_op jit(solution)/shard_map/ppermute | solution.py:25
  43.5 4.3 %collective-permute-done.5 = f32[384,256]{1,0:T(8,128)S(1)} collective-permute-done((f32[384,256]{1,0:T(8,128)S(1)}, f32[384,256]{1,0:T(8,128)S(1)}, u32[]{:S(2)}, u32[]{:S(2)}) %collective-permute-start.5) | collective-permute-done | bytes 393248 | tf_op jit(solution)/shard_map/ppermute | solution.py:25
  48.0 0.6 collective-permute-done.10
  48.7 1.6 %collective-permute-start.6 = (f32[2,32,256]{2,1,0:T(8,128)S(1)}, f32[2,32,256]{2,1,0:T(8,128)S(1)}, u32[]{:S(2)}, u32[]{:S(2)}) collective-permute-start(f32[2,32,256]{2,1,0:T(8,128)S(1)} %bitcast_add_fusion), channel_id=1, source_target_pairs={{0,16},{4,20},{8,24},{12,28},{16,0},{20,4},{24,8},{28,12},{1,17},{... | collective-permute-start | bytes 196616 | tf_op jit(solution)/shard_map/ppermute | solution.py:25
  50.3 2.3 %collective-permute-start.11 = (f32[256,256]{1,0:T(8,128)S(1)}, f32[256,256]{1,0:T(8,128)S(1)}, u32[]{:S(2)}, u32[]{:S(2)}) collective-permute-start(f32[256,256]{1,0:T(8,128)S(1)} %bitcast.117), channel_id=1, source_target_pairs={{0,1},{1,0},{2,3},{3,2},{4,5},{5,4},{6,7},{7,6},{8,9},{9,8},{10,11... | collective-permute-start | bytes 786440 | tf_op jit(solution)/shard_map/ppermute | solution.py:25
  53.0 1.2 shard_map.74
  54.2 3.4 %collective-permute-start.8 = (f32[2,2,32,256]{3,2,1,0:T(8,128)S(1)}, f32[2,2,32,256]{3,2,1,0:T(8,128)S(1)}, u32[]{:S(2)}, u32[]{:S(2)}) collective-permute-start(f32[2,2,32,256]{3,2,1,0:T(8,128)S(1)} %shard_map.74), channel_id=1, source_target_pairs={{0,2},{1,3},{2,0},{3,1},{4,6},{5,7},{6,4},{7,5},{8,10},{9,11},{10,... | collective-permute-start | bytes 393224 | tf_op jit(solution)/shard_map/ppermute | solution.py:25
  57.7 4.9 %collective-permute-done.8 = f32[2,2,32,256]{3,2,1,0:T(8,128)S(1)} collective-permute-done((f32[2,2,32,256]{3,2,1,0:T(8,128)S(1)}, f32[2,2,32,256]{3,2,1,0:T(8,128)S(1)}, u32[]{:S(2)}, u32[]{:S(2)}) %collective-permute-start.8) | collective-permute-done | bytes 131104 | tf_op jit(solution)/shard_map/ppermute | solution.py:25
  63.1 1.7 %collective-permute-start.12 = (f32[2,64,256]{2,1,0:T(8,128)S(1)}, f32[2,64,256]{2,1,0:T(8,128)S(1)}, u32[]{:S(2)}, u32[]{:S(2)}) collective-permute-start(f32[2,64,256]{2,1,0:T(8,128)S(1)} %get-tuple-element.98), channel_id=1, source_target_pairs={{0,1},{1,0},{2,3},{3,2},{4,5},{5,4},{6,7},{7,6},{8,9},{9,8},{10,11... | collective-permute-start | bytes 393224 | tf_op jit(solution)/shard_map/ppermute | solution.py:25
  64.8 2.9 %collective-permute-done.16 = f32[2,64,256]{2,1,0:T(8,128)S(1)} collective-permute-done((f32[2,64,256]{2,1,0:T(8,128)S(1)}, f32[2,64,256]{2,1,0:T(8,128)S(1)}, u32[]{:S(2)}, u32[]{:S(2)}) %collective-permute-start.16) | collective-permute-done | bytes 131104 | tf_op jit(solution)/shard_map/ppermute | solution.py:25
  67.8 1.3 %collective-permute-done.12 = f32[2,64,256]{2,1,0:T(8,128)S(1)} collective-permute-done((f32[2,64,256]{2,1,0:T(8,128)S(1)}, f32[2,64,256]{2,1,0:T(8,128)S(1)}, u32[]{:S(2)}, u32[]{:S(2)}) %collective-permute-start.12) | collective-permute-done | bytes 131104 | tf_op jit(solution)/shard_map/ppermute | solution.py:25
  69.4 2.6 %shard_map.77 = (f32[1024,256]{1,0:T(8,128)S(1)}, f32[256,256]{1,0:T(8,128)S(1)}, f32[256,256]{1,0:T(8,128)S(1)}) custom-call(s32[2]{0:T(128)S(1)} %pad_add_fusion.where_ref, f32[1024,512]{1,0:T(8,128)S(1)} %copy-done.4, f32[2,128,256]{2,1,0:T(8,128)S(1)} %maximum_select_fusion.11.own_ref, f32[2,128,256]{2,1,0:T(8,128)S(1)} %collective-permute-done.17.partner_ref, ...), custom_call_target="tpu_custom_call" | custom-call | flops 1610612736 | bytes 4194304 | tf_op jit(solution)/shard_map/pallas_call | solution.py:195
  72.0 0.7 collective-permute-start.18
  72.6 2.6 %shard_map.76 = (f32[1024,256]{1,0:T(8,128)S(1)}, f32[256,256]{1,0:T(8,128)S(1)}, f32[256,256]{1,0:T(8,128)S(1)}) custom-call(s32[2]{0:T(128)S(1)} %pad_add_fusion.where_ref, f32[1024,512]{1,0:T(8,128)S(1)} %copy-done.4, f32[2,128,256]{2,1,0:T(8,128)S(1)} %maximum_select_fusion.10.own_ref, f32[2,128,256]{2,1,0:T(8,128)S(1)} %collective-permute-done.13.partner_ref, ...), custom_call_target="tpu_custom_call" | custom-call | flops 1610612736 | bytes 4194304 | tf_op jit(solution)/shard_map/pallas_call | solution.py:195
  75.2 1.5 %collective-permute-start.14 = (f32[256,256]{1,0:T(8,128)S(1)}, f32[256,256]{1,0:T(8,128)S(1)}, u32[]{:S(2)}, u32[]{:S(2)}) collective-permute-start(f32[256,256]{1,0:T(8,128)S(1)} %get-tuple-element.58), channel_id=1, source_target_pairs={{0,1},{1,0},{2,3},{3,2},{4,5},{5,4},{6,7},{7,6},{8,9},{9,8},{10,11... | collective-permute-start | bytes 786440 | tf_op jit(solution)/shard_map/ppermute | solution.py:25
  76.7 4.4 %collective-permute-done.18 = f32[256,256]{1,0:T(8,128)S(1)} collective-permute-done((f32[256,256]{1,0:T(8,128)S(1)}, f32[256,256]{1,0:T(8,128)S(1)}, u32[]{:S(2)}, u32[]{:S(2)}) %collective-permute-start.18) | collective-permute-done | bytes 262176 | tf_op jit(solution)/shard_map/ppermute | solution.py:25
  81.2 1.5 %collective-permute-start.19 = (f32[128,256]{1,0:T(8,128)S(1)}, f32[128,256]{1,0:T(8,128)S(1)}, u32[]{:S(2)}, u32[]{:S(2)}) collective-permute-start(f32[128,256]{1,0:T(8,128)S(1)} %slice.117), channel_id=1, source_target_pairs={{0,2},{1,3},{2,0},{3,1},{4,6},{5,7},{6,4},{7,5},{8,10},{9,11},{10,... | collective-permute-start | bytes 393224 | tf_op jit(solution)/shard_map/ppermute | solution.py:25
  82.7 1.5 %collective-permute-start.24 = (f32[256,256]{1,0:T(8,128)S(1)}, f32[256,256]{1,0:T(8,128)S(1)}, u32[]{:S(2)}, u32[]{:S(2)}) collective-permute-start(f32[256,256]{1,0:T(8,128)S(1)} %bitcast.120), channel_id=1, source_target_pairs={{0,1},{1,0},{2,3},{3,2},{4,5},{5,4},{6,7},{7,6},{8,9},{9,8},{10,11... | collective-permute-start | bytes 786440 | tf_op jit(solution)/shard_map/ppermute | solution.py:25
  84.2 5.3 %collective-permute-done.14 = f32[256,256]{1,0:T(8,128)S(1)} collective-permute-done((f32[256,256]{1,0:T(8,128)S(1)}, f32[256,256]{1,0:T(8,128)S(1)}, u32[]{:S(2)}, u32[]{:S(2)}) %collective-permute-start.14) | collective-permute-done | bytes 262176 | tf_op jit(solution)/shard_map/ppermute | solution.py:25
  90.0 1.2 collective-permute-done.20.upper_other
  91.1 0.6 shard_map.78
  91.8 4.1 %collective-permute-done.15 = f32[128,256]{1,0:T(8,128)S(1)} collective-permute-done((f32[128,256]{1,0:T(8,128)S(1)}, f32[128,256]{1,0:T(8,128)S(1)}, u32[]{:S(2)}, u32[]{:S(2)}) %collective-permute-start.15) | collective-permute-done | bytes 131104 | tf_op jit(solution)/shard_map/ppermute | solution.py:25
  96.0 1.6 %collective-permute-done.24 = f32[256,256]{1,0:T(8,128)S(1)} collective-permute-done((f32[256,256]{1,0:T(8,128)S(1)}, f32[256,256]{1,0:T(8,128)S(1)}, u32[]{:S(2)}, u32[]{:S(2)}) %collective-permute-start.24) | collective-permute-done | bytes 262176 | tf_op jit(solution)/shard_map/ppermute | solution.py:25
  97.6 1.8 %collective-permute-start.23 = (f32[128,256]{1,0:T(8,128)S(1)}, f32[128,256]{1,0:T(8,128)S(1)}, u32[]{:S(2)}, u32[]{:S(2)}) collective-permute-start(f32[128,256]{1,0:T(8,128)S(1)} %get-tuple-element.64.own), channel_id=1, source_target_pairs={{0,2},{1,3},{2,0},{3,1},{4,6},{5,7},{6,4},{7,5},{8,10},{9,11},{10,... | collective-permute-start | bytes 393224 | tf_op jit(solution)/shard_map/ppermute | solution.py:25
  99.4 0.6 shard_map.79
  100.1 1.3 %collective-permute-start.22 = (f32[128,256]{1,0:T(8,128)S(1)}, f32[128,256]{1,0:T(8,128)S(1)}, u32[]{:S(2)}, u32[]{:S(2)}) collective-permute-start(f32[128,256]{1,0:T(8,128)S(1)} %get-tuple-element.67.own), channel_id=1, source_target_pairs={{0,2},{1,3},{2,0},{3,1},{4,6},{5,7},{6,4},{7,5},{8,10},{9,11},{10,... | collective-permute-start | bytes 393224 | tf_op jit(solution)/shard_map/ppermute | solution.py:25
  101.4 8.8 %collective-permute-done.23.sibling = f32[128,256]{1,0:T(8,128)S(1)} collective-permute-done((f32[128,256]{1,0:T(8,128)S(1)}, f32[128,256]{1,0:T(8,128)S(1)}, u32[]{:S(2)}, u32[]{:S(2)}) %collective-permute-start.23) | collective-permute-done | bytes 131104 | tf_op jit(solution)/shard_map/ppermute | solution.py:25
  110.7 1.5 %collective-permute-done.22.sibling = f32[128,256]{1,0:T(8,128)S(1)} collective-permute-done((f32[128,256]{1,0:T(8,128)S(1)}, f32[128,256]{1,0:T(8,128)S(1)}, u32[]{:S(2)}, u32[]{:S(2)}) %collective-permute-start.22) | collective-permute-done | bytes 131104 | tf_op jit(solution)/shard_map/ppermute | solution.py:25
  112.6 0.6 collective-permute-start.25
  113.2 6.5 %collective-permute-done.26.partner_ref = f32[2,128,256]{2,1,0:T(8,128)S(1)} collective-permute-done((f32[2,128,256]{2,1,0:T(8,128)S(1)}, f32[2,128,256]{2,1,0:T(8,128)S(1)}, u32[]{:S(2)}, u32[]{:S(2)}) %collective-permute-start.26) | collective-permute-done | bytes 262176 | tf_op jit(solution)/shard_map/ppermute | solution.py:25
  119.6 2.0 %shard_map.82.refs_0_ = f32[1024,512]{1,0:T(8,128)} custom-call(s32[1]{0:T(128)} %bitcast.where_ref, f32[1024,256]{1,0:T(8,128)S(1)} %get-tuple-element.69.x_ref, f32[2,128,256]{2,1,0:T(8,128)S(1)} %shard_map.80.own_ref, f32[2,128,256]{2,1,0:T(8,128)S(1)} %collective-permute-done.26.partner_ref, f32[4,1024,256]{2,1,0:T(8,128)S(1)} %copy-done.1), custom_call_target="tpu_custom_call" | custom-call | flops 805306368 | bytes 3145728 | tf_op jit(solution)/shard_map/pallas_call | solution.py:227
  121.7 1.0 collective-permute-done.25.partner_ref
  122.7 2.0 %shard_map.83 = f32[1024,512]{1,0:T(8,128)} custom-call(s32[1]{0:T(128)} %bitcast.where_ref, f32[1024,256]{1,0:T(8,128)S(1)} %get-tuple-element.56.x_ref, f32[2,128,256]{2,1,0:T(8,128)S(1)} %shard_map.81.own_ref, f32[2,128,256]{2,1,0:T(8,128)S(1)} %collective-permute-done.25.partner_ref, ...), custom_call_target="tpu_custom_call", output_to_operand_aliasing={{}: (5, {})} | custom-call | flops 805306368 | bytes 3145728 | tf_op jit(solution)/shard_map/pallas_call | solution.py:227
  (96 shorter events, 3.2 us)
Async XLA Ops:
  0.0 6.0 %copy-start.8 = (f32[16,512]{1,0:T(8,128)S(1)}, f32[16,512]{1,0:T(8,128)}, u32[]{:S(2)}) copy-start(f32[16,512]{1,0:T(8,128)} %param.10) | copy-start | bytes 98308
  0.0 6.0 %copy-start.7 = (f32[32,512]{1,0:T(8,128)S(1)}, f32[32,512]{1,0:T(8,128)}, u32[]{:S(2)}) copy-start(f32[32,512]{1,0:T(8,128)} %param.11) | copy-start | bytes 196612
  0.0 6.1 %copy-start.6 = (f32[64,512]{1,0:T(8,128)S(1)}, f32[64,512]{1,0:T(8,128)}, u32[]{:S(2)}) copy-start(f32[64,512]{1,0:T(8,128)} %param.12) | copy-start | bytes 393220
  5.6 2.4 %collective-permute-start = (f32[640,256]{1,0:T(8,128)}, f32[640,256]{1,0:T(8,128)S(1)}, u32[]{:S(2)}, u32[]{:S(2)}) collective-permute-start(f32[640,256]{1,0:T(8,128)} %get-tuple-element.39), channel_id=1, source_target_pairs={{0,4},{4,0},{8,12},{12,8},{16,20},{20,16},{24,28},{28,24},{1,5},{5... | collective-permute-start | bytes 1966088 | tf_op jit(solution)/shard_map/ppermute | solution.py:25
  9.1 30.1 %copy-start.2 = (f32[4,1024,256]{2,1,0:T(8,128)S(1)}, f32[4,1024,256]{2,1,0:T(8,128)}, u32[]{:S(2)}) copy-start(f32[4,1024,256]{2,1,0:T(8,128)} %v_ref.7) | copy-start | bytes 12582916
  9.2 15.0 %collective-permute-start.2 = (f32[224,256]{1,0:T(8,128)S(1)}, f32[224,256]{1,0:T(8,128)S(1)}, u32[]{:S(2)}, u32[]{:S(2)}) collective-permute-start(f32[224,256]{1,0:T(8,128)S(1)} %pad_maximum_fusion.5), channel_id=1, source_target_pairs={{0,2},{1,3},{2,0},{3,1},{4,6},{5,7},{6,4},{7,5},{8,10},{9,11},{10,... | collective-permute-start | bytes 688136 | tf_op jit(solution)/shard_map/ppermute | solution.py:25
  13.3 11.9 %collective-permute-start.1 = (f32[2,2,64,256]{3,2,1,0:T(8,128)S(1)}, f32[2,2,64,256]{3,2,1,0:T(8,128)S(1)}, u32[]{:S(2)}, u32[]{:S(2)}) collective-permute-start(f32[2,2,64,256]{3,2,1,0:T(8,128)S(1)} %slice_select_fusion.8), channel_id=1, source_target_pairs={{0,1},{1,0},{2,3},{3,2},{4,5},{5,4},{6,7},{7,6},{8,9},{9,8},{10,11... | collective-permute-start | bytes 786440 | tf_op jit(solution)/shard_map/ppermute | solution.py:25
  25.2 14.1 %copy-start = (f32[4,1024,256]{2,1,0:T(8,128)S(1)}, f32[4,1024,256]{2,1,0:T(8,128)}, u32[]{:S(2)}) copy-start(f32[4,1024,256]{2,1,0:T(8,128)} %u_ref.11) | copy-start | bytes 12582916
  25.2 7.6 %collective-permute-start.3 = (f32[2,2,32,256]{3,2,1,0:T(8,128)S(1)}, f32[2,2,32,256]{3,2,1,0:T(8,128)S(1)}, u32[]{:S(2)}, u32[]{:S(2)}) collective-permute-start(f32[2,2,32,256]{3,2,1,0:T(8,128)S(1)} %slice_select_fusion.9), channel_id=1, source_target_pairs={{0,2},{1,3},{2,0},{3,1},{4,6},{5,7},{6,4},{7,5},{8,10},{9,11},{10,... | collective-permute-start | bytes 393224 | tf_op jit(solution)/shard_map/ppermute | solution.py:25
  26.6 10.9 %collective-permute-start.4 = (f32[320,256]{1,0:T(8,128)S(1)}, f32[320,256]{1,0:T(8,128)S(1)}, u32[]{:S(2)}, u32[]{:S(2)}) collective-permute-start(f32[320,256]{1,0:T(8,128)S(1)} %pad_maximum_fusion.2), channel_id=1, source_target_pairs={{0,1},{1,0},{2,3},{3,2},{4,5},{5,4},{6,7},{7,6},{8,9},{9,8},{10,11... | collective-permute-start | bytes 983048 | tf_op jit(solution)/shard_map/ppermute | solution.py:25
  37.7 10.1 %collective-permute-start.5 = (f32[384,256]{1,0:T(8,128)S(1)}, f32[384,256]{1,0:T(8,128)S(1)}, u32[]{:S(2)}, u32[]{:S(2)}) collective-permute-start(f32[384,256]{1,0:T(8,128)S(1)} %pad_maximum_fusion.1), channel_id=1, source_target_pairs={{0,8},{4,12},{8,0},{12,4},{16,24},{20,28},{24,16},{28,20},{1,9},{5... | collective-permute-start | bytes 1179656 | tf_op jit(solution)/shard_map/ppermute | solution.py:25
  39.9 22.8 %collective-permute-start.9 = (f32[256,256]{1,0:T(8,128)S(1)}, f32[256,256]{1,0:T(8,128)S(1)}, u32[]{:S(2)}, u32[]{:S(2)}) collective-permute-start(f32[256,256]{1,0:T(8,128)S(1)} %shard_map.75), channel_id=1, source_target_pairs={{0,1},{1,0},{2,3},{3,2},{4,5},{5,4},{6,7},{7,6},{8,9},{9,8},{10,11... | collective-permute-start | bytes 786440 | tf_op jit(solution)/shard_map/ppermute | solution.py:25
  41.0 7.7 %collective-permute-start.10 = (f32[128,256]{1,0:T(8,128)S(1)}, f32[128,256]{1,0:T(8,128)S(1)}, u32[]{:S(2)}, u32[]{:S(2)}) collective-permute-start(f32[128,256]{1,0:T(8,128)S(1)} %bitcast.131), channel_id=1, source_target_pairs={{0,2},{1,3},{2,0},{3,1},{4,6},{5,7},{6,4},{7,5},{8,10},{9,11},{10,... | collective-permute-start | bytes 393224 | tf_op jit(solution)/shard_map/ppermute | solution.py:25
  48.0 4.6 %collective-permute-start.7 = (f32[768,256]{1,0:T(8,128)S(1)}, f32[768,256]{1,0:T(8,128)S(1)}, u32[]{:S(2)}, u32[]{:S(2)}) collective-permute-start(f32[768,256]{1,0:T(8,128)S(1)} %pad_maximum_fusion), channel_id=1, source_target_pairs={{0,4},{4,0},{8,12},{12,8},{16,20},{20,16},{24,28},{28,24},{1,5},{5... | collective-permute-start | bytes 2359304 | tf_op jit(solution)/shard_map/ppermute | solution.py:25
  48.7 4.3 %collective-permute-start.6 = (f32[2,32,256]{2,1,0:T(8,128)S(1)}, f32[2,32,256]{2,1,0:T(8,128)S(1)}, u32[]{:S(2)}, u32[]{:S(2)}) collective-permute-start(f32[2,32,256]{2,1,0:T(8,128)S(1)} %bitcast_add_fusion), channel_id=1, source_target_pairs={{0,16},{4,20},{8,24},{12,28},{16,0},{20,4},{24,8},{28,12},{1,17},{... | collective-permute-start | bytes 196616 | tf_op jit(solution)/shard_map/ppermute | solution.py:25
  50.3 12.4 %collective-permute-start.11 = (f32[256,256]{1,0:T(8,128)S(1)}, f32[256,256]{1,0:T(8,128)S(1)}, u32[]{:S(2)}, u32[]{:S(2)}) collective-permute-start(f32[256,256]{1,0:T(8,128)S(1)} %bitcast.117), channel_id=1, source_target_pairs={{0,1},{1,0},{2,3},{3,2},{4,5},{5,4},{6,7},{7,6},{8,9},{9,8},{10,11... | collective-permute-start | bytes 786440 | tf_op jit(solution)/shard_map/ppermute | solution.py:25
  52.6 16.7 %copy-start.4 = (f32[1024,512]{1,0:T(8,128)S(1)}, f32[1024,512]{1,0:T(8,128)}, u32[]{:S(2)}) copy-start(f32[1024,512]{1,0:T(8,128)} %old_ref.3) | copy-start | bytes 6291460
  52.7 16.6 %copy-start.3 = (f32[4,1024,256]{2,1,0:T(8,128)S(1)}, f32[4,1024,256]{2,1,0:T(8,128)}, u32[]{:S(2)}) copy-start(f32[4,1024,256]{2,1,0:T(8,128)} %v_ref.7) | copy-start | bytes 12582916
  52.9 16.4 %copy-start.1 = (f32[4,1024,256]{2,1,0:T(8,128)S(1)}, f32[4,1024,256]{2,1,0:T(8,128)}, u32[]{:S(2)}) copy-start(f32[4,1024,256]{2,1,0:T(8,128)} %u_ref.11) | copy-start | bytes 12582916
  54.2 8.4 %collective-permute-start.8 = (f32[2,2,32,256]{3,2,1,0:T(8,128)S(1)}, f32[2,2,32,256]{3,2,1,0:T(8,128)S(1)}, u32[]{:S(2)}, u32[]{:S(2)}) collective-permute-start(f32[2,2,32,256]{3,2,1,0:T(8,128)S(1)} %shard_map.74), channel_id=1, source_target_pairs={{0,2},{1,3},{2,0},{3,1},{4,6},{5,7},{6,4},{7,5},{8,10},{9,11},{10,... | collective-permute-start | bytes 393224 | tf_op jit(solution)/shard_map/ppermute | solution.py:25
  62.7 5.0 %collective-permute-start.16 = (f32[2,64,256]{2,1,0:T(8,128)S(1)}, f32[2,64,256]{2,1,0:T(8,128)S(1)}, u32[]{:S(2)}, u32[]{:S(2)}) collective-permute-start(f32[2,64,256]{2,1,0:T(8,128)S(1)} %get-tuple-element.97), channel_id=1, source_target_pairs={{0,1},{1,0},{2,3},{3,2},{4,5},{5,4},{6,7},{7,6},{8,9},{9,8},{10,11... | collective-permute-start | bytes 393224 | tf_op jit(solution)/shard_map/ppermute | solution.py:25
  63.1 6.1 %collective-permute-start.12 = (f32[2,64,256]{2,1,0:T(8,128)S(1)}, f32[2,64,256]{2,1,0:T(8,128)S(1)}, u32[]{:S(2)}, u32[]{:S(2)}) collective-permute-start(f32[2,64,256]{2,1,0:T(8,128)S(1)} %get-tuple-element.98), channel_id=1, source_target_pairs={{0,1},{1,0},{2,3},{3,2},{4,5},{5,4},{6,7},{7,6},{8,9},{9,8},{10,11... | collective-permute-start | bytes 393224 | tf_op jit(solution)/shard_map/ppermute | solution.py:25
  67.7 1.6 %collective-permute-start.17 = (f32[2,128,256]{2,1,0:T(8,128)S(1)}, f32[2,128,256]{2,1,0:T(8,128)S(1)}, u32[]{:S(2)}, u32[]{:S(2)}) collective-permute-start(f32[2,128,256]{2,1,0:T(8,128)S(1)} %maximum_select_fusion.11.own_ref), channel_id=1, source_target_pairs={{0,4},{4,0},{8,12},{12,8},{16,20},{20,16},{24,28},{28,24},{1,5},{5... | collective-permute-start | bytes 786440 | tf_op jit(solution)/shard_map/ppermute | solution.py:25
  69.1 3.5 %collective-permute-start.13 = (f32[2,128,256]{2,1,0:T(8,128)S(1)}, f32[2,128,256]{2,1,0:T(8,128)S(1)}, u32[]{:S(2)}, u32[]{:S(2)}) collective-permute-start(f32[2,128,256]{2,1,0:T(8,128)S(1)} %maximum_select_fusion.10.own_ref), channel_id=1, source_target_pairs={{0,4},{4,0},{8,12},{12,8},{16,20},{20,16},{24,28},{28,24},{1,5},{5... | collective-permute-start | bytes 786440 | tf_op jit(solution)/shard_map/ppermute | solution.py:25
  71.9 4.8 %copy-start.5 = (f32[128,512]{1,0:T(8,128)S(1)}, f32[128,512]{1,0:T(8,128)}, u32[]{:S(2)}) copy-start(f32[128,512]{1,0:T(8,128)} %param.13) | copy-start | bytes 786436
  72.0 9.2 %collective-permute-start.18 = (f32[256,256]{1,0:T(8,128)S(1)}, f32[256,256]{1,0:T(8,128)S(1)}, u32[]{:S(2)}, u32[]{:S(2)}) collective-permute-start(f32[256,256]{1,0:T(8,128)S(1)} %get-tuple-element.60), channel_id=1, source_target_pairs={{0,1},{1,0},{2,3},{3,2},{4,5},{5,4},{6,7},{7,6},{8,9},{9,8},{10,11... | collective-permute-start | bytes 786440 | tf_op jit(solution)/shard_map/ppermute | solution.py:25
  75.2 14.4 %collective-permute-start.14 = (f32[256,256]{1,0:T(8,128)S(1)}, f32[256,256]{1,0:T(8,128)S(1)}, u32[]{:S(2)}, u32[]{:S(2)}) collective-permute-start(f32[256,256]{1,0:T(8,128)S(1)} %get-tuple-element.58), channel_id=1, source_target_pairs={{0,1},{1,0},{2,3},{3,2},{4,5},{5,4},{6,7},{7,6},{8,9},{9,8},{10,11... | collective-permute-start | bytes 786440 | tf_op jit(solution)/shard_map/ppermute | solution.py:25
  81.2 8.5 %collective-permute-start.19 = (f32[128,256]{1,0:T(8,128)S(1)}, f32[128,256]{1,0:T(8,128)S(1)}, u32[]{:S(2)}, u32[]{:S(2)}) collective-permute-start(f32[128,256]{1,0:T(8,128)S(1)} %slice.117), channel_id=1, source_target_pairs={{0,2},{1,3},{2,0},{3,1},{4,6},{5,7},{6,4},{7,5},{8,10},{9,11},{10,... | collective-permute-start | bytes 393224 | tf_op jit(solution)/shard_map/ppermute | solution.py:25
  82.7 14.9 %collective-permute-start.24 = (f32[256,256]{1,0:T(8,128)S(1)}, f32[256,256]{1,0:T(8,128)S(1)}, u32[]{:S(2)}, u32[]{:S(2)}) collective-permute-start(f32[256,256]{1,0:T(8,128)S(1)} %bitcast.120), channel_id=1, source_target_pairs={{0,1},{1,0},{2,3},{3,2},{4,5},{5,4},{6,7},{7,6},{8,9},{9,8},{10,11... | collective-permute-start | bytes 786440 | tf_op jit(solution)/shard_map/ppermute | solution.py:25
  89.6 6.2 %collective-permute-start.15 = (f32[128,256]{1,0:T(8,128)S(1)}, f32[128,256]{1,0:T(8,128)S(1)}, u32[]{:S(2)}, u32[]{:S(2)}) collective-permute-start(f32[128,256]{1,0:T(8,128)S(1)} %slice.116), channel_id=1, source_target_pairs={{0,2},{1,3},{2,0},{3,1},{4,6},{5,7},{6,4},{7,5},{8,10},{9,11},{10,... | collective-permute-start | bytes 393224 | tf_op jit(solution)/shard_map/ppermute | solution.py:25
  89.7 1.4 %collective-permute-start.20 = (f32[128,256]{1,0:T(8,128)S(1)}, f32[128,256]{1,0:T(8,128)S(1)}, u32[]{:S(2)}, u32[]{:S(2)}) collective-permute-start(f32[128,256]{1,0:T(8,128)S(1)} %get-tuple-element.96.upper), channel_id=1, source_target_pairs={{0,4},{4,0},{8,12},{12,8},{16,20},{20,16},{24,28},{28,24},{1,5},{5... | collective-permute-start | bytes 393224 | tf_op jit(solution)/shard_map/ppermute | solution.py:25
  95.9 3.5 %collective-permute-start.21 = (f32[128,256]{1,0:T(8,128)S(1)}, f32[128,256]{1,0:T(8,128)S(1)}, u32[]{:S(2)}, u32[]{:S(2)}) collective-permute-start(f32[128,256]{1,0:T(8,128)S(1)} %get-tuple-element.94.upper), channel_id=1, source_target_pairs={{0,4},{4,0},{8,12},{12,8},{16,20},{20,16},{24,28},{28,24},{1,5},{5... | collective-permute-start | bytes 393224 | tf_op jit(solution)/shard_map/ppermute | solution.py:25
  97.6 12.6 %collective-permute-start.23 = (f32[128,256]{1,0:T(8,128)S(1)}, f32[128,256]{1,0:T(8,128)S(1)}, u32[]{:S(2)}, u32[]{:S(2)}) collective-permute-start(f32[128,256]{1,0:T(8,128)S(1)} %get-tuple-element.64.own), channel_id=1, source_target_pairs={{0,2},{1,3},{2,0},{3,1},{4,6},{5,7},{6,4},{7,5},{8,10},{9,11},{10,... | collective-permute-start | bytes 393224 | tf_op jit(solution)/shard_map/ppermute | solution.py:25
  100.1 12.1 %collective-permute-start.22 = (f32[128,256]{1,0:T(8,128)S(1)}, f32[128,256]{1,0:T(8,128)S(1)}, u32[]{:S(2)}, u32[]{:S(2)}) collective-permute-start(f32[128,256]{1,0:T(8,128)S(1)} %get-tuple-element.67.own), channel_id=1, source_target_pairs={{0,2},{1,3},{2,0},{3,1},{4,6},{5,7},{6,4},{7,5},{8,10},{9,11},{10,... | collective-permute-start | bytes 393224 | tf_op jit(solution)/shard_map/ppermute | solution.py:25
  110.6 9.0 %collective-permute-start.26 = (f32[2,128,256]{2,1,0:T(8,128)S(1)}, f32[2,128,256]{2,1,0:T(8,128)S(1)}, u32[]{:S(2)}, u32[]{:S(2)}) collective-permute-start(f32[2,128,256]{2,1,0:T(8,128)S(1)} %shard_map.80.own_ref), channel_id=1, source_target_pairs={{0,1},{1,0},{2,3},{3,2},{4,5},{5,4},{6,7},{7,6},{8,9},{9,8},{10,11... | collective-permute-start | bytes 786440 | tf_op jit(solution)/shard_map/ppermute | solution.py:25
  112.6 10.1 %collective-permute-start.25 = (f32[2,128,256]{2,1,0:T(8,128)S(1)}, f32[2,128,256]{2,1,0:T(8,128)S(1)}, u32[]{:S(2)}, u32[]{:S(2)}) collective-permute-start(f32[2,128,256]{2,1,0:T(8,128)S(1)} %shard_map.81.own_ref), channel_id=1, source_target_pairs={{0,1},{1,0},{2,3},{3,2},{4,5},{5,4},{6,7},{7,6},{8,9},{9,8},{10,11... | collective-permute-start | bytes 786440 | tf_op jit(solution)/shard_map/ppermute | solution.py:25

commit v4 on v3

--- a/solution.py
+++ b/solution.py
@@ -11,6 +11,10 @@
 STEPS = 2
 MIB = 1 << 20
 LOW = -1
+HOLD = True
+FIRST = 50
+FIRST_STEPS = 4
+LAST_STEPS = 4
 MID = 24
 LAST = 24
 
@@ -83,43 +87,47 @@
     return lax.dot_general(left, right, dims, preferred_element_type=jnp.float32)
 
 
-def first_kernel(where_ref, x_ref, u_ref, v_ref, v_next_ref, keep_ref, send_ref, total, total_next):
-    step = pl.program_id(0)
-
-    @pl.when(step == 0)
-    def _():
-        total[...] = jnp.zeros_like(total)
-        total_next[...] = jnp.zeros_like(total_next)
-
-    sides = x_ref.shape[1]
-    x, v, v_next = halves(x_ref[...]), halves(v_ref[0]), halves(v_next_ref[0])
-    total[...] += product(x, v, 0, 0)
-    total_next[:sides] += product(x, v_next, 0, 0)
-    total_next[sides:] += product(halves(u_ref[0]), v_next, 0, 0)
-
-    @pl.when(step == pl.num_programs(0) - 1)
-    def _():
-        where = where_ref[0]
-        width = sides // (2 * CHUNKS)
-        for ref, side in ((keep_ref, where), (send_ref, 1 - where)):
-            for level, each in enumerate((total, total_next)):
-                for k in range(CHUNKS):
-                    start = pl.multiple_of((2 * k + side) * width, width)
-                    at = (level * CHUNKS + k) * width
-                    ref[at : at + width, :] = each[pl.ds(start, width), :]
-        rank = u_ref.shape[2]
-        at = 2 * CHUNKS * width
-        for ref, side in ((keep_ref, where), (send_ref, 1 - where)):
-            start = pl.multiple_of(sides + side * (rank // 2), rank // 2)
-            ref[at:, :] = total_next[pl.ds(start, rank // 2), :]
-
-
-def slab(rows, rank, level):
-    return pl.BlockSpec((1, rows, rank), lambda i, *_: (level, i, 0))
-
-
-def whole(shape):
-    return pl.BlockSpec(shape, lambda *_: (0,) * len(shape))
+def first_kernel(level, where_ref, x_hbm, u_hbm, v_hbm, keep_ref, send_ref, x_ref, u_ref, v_ref, total, total_next, sems):
+    rows, sides = x_ref.shape
+    rank = u_ref.shape[1]
+    block = rows // FIRST_STEPS
+    copies = []
+    for step in range(FIRST_STEPS):
+        at = pl.ds(step * block, block)
+        pairs = [
+            (x_hbm.at[at], x_ref.at[at]),
+            (v_hbm.at[level + 1, at], v_ref.at[1, at]),
+            (v_hbm.at[level, at], v_ref.at[0, at]),
+            (u_hbm.at[level, at], u_ref.at[at]),
+        ]
+        copies.append([pltpu.make_async_copy(*pair, sems.at[step, k]) for k, pair in enumerate(pairs)])
+        for copy in copies[-1]:
+            copy.start()
+    for step in range(FIRST_STEPS):
+        at = slice(step * block, (step + 1) * block)
+        for copy in copies[step]:
+            copy.wait()
+        x, v, v_next = halves(x_ref[at, :]), halves(v_ref[0, at]), halves(v_ref[1, at])
+        terms = product(x, v, 0, 0), product(x, v_next, 0, 0), product(halves(u_ref[at, :]), v_next, 0, 0)
+        if step:
+            total[...] += terms[0]
+            total_next[:sides] += terms[1]
+            total_next[sides:] += terms[2]
+        else:
+            total[...] = terms[0]
+            total_next[:sides] = terms[1]
+            total_next[sides:] = terms[2]
+    where = where_ref[0]
+    width = sides // (2 * CHUNKS)
+    at = 2 * CHUNKS * width
+    for ref, side in ((keep_ref, where), (send_ref, 1 - where)):
+        for level, each in enumerate((total, total_next)):
+            for k in range(CHUNKS):
+                start = pl.multiple_of((2 * k + side) * width, width)
+                into = (level * CHUNKS + k) * width
+                ref[into : into + width, :] = each[pl.ds(start, width), :]
+        start = pl.multiple_of(sides + side * (rank // 2), rank // 2)
+        ref[at:, :] = total_next[pl.ds(start, rank // 2), :]
 
 
 def shapes(*values):
@@ -127,29 +135,30 @@
 
 
 SMEM = pl.BlockSpec(memory_space=pltpu.SMEM)
+VMEM = pl.BlockSpec(memory_space=pltpu.VMEM)
+ANY = pl.BlockSpec(memory_space=pl.ANY)
 
 
 def first_sums(where, x, bases_u, bases_v, level):
     rows, sides = x.shape
     rank = bases_u.shape[2]
-    block = rows // STEPS
     out = (sides + rank // 2, rank)
     return pl.pallas_call(
-        first_kernel,
-        grid=(STEPS,),
-        in_specs=[
-            SMEM,
-            pl.BlockSpec((block, sides), lambda i: (i, 0)),
-            slab(block, rank, level),
-            slab(block, rank, level),
-            slab(block, rank, level + 1),
+        functools.partial(first_kernel, level),
+        in_specs=[SMEM] + [ANY] * 3,
+        out_specs=[VMEM] * 2,
+        out_shape=shapes(out, out),
+        scratch_shapes=[
+            pltpu.VMEM((rows, sides), jnp.float32),
+            pltpu.VMEM((rows, rank), jnp.float32),
+            pltpu.VMEM((2, rows, rank), jnp.float32),
+            pltpu.VMEM((sides, rank), jnp.float32),
+            pltpu.VMEM((sides + rank, rank), jnp.float32),
+            pltpu.SemaphoreType.DMA((FIRST_STEPS, 4)),
         ],
-        out_specs=[whole(out)] * 2,
-        out_shape=shapes(out, out),
-        scratch_shapes=[pltpu.VMEM((sides, rank), jnp.float32), pltpu.VMEM((sides + rank, rank), jnp.float32)],
-        compiler_params=pltpu.CompilerParams(vmem_limit_bytes=60 * MIB),
+        compiler_params=pltpu.CompilerParams(vmem_limit_bytes=FIRST * MIB),
         cost_estimate=pl.CostEstimate(flops=6 * rows * rank * (2 * sides + rank), bytes_accessed=5 * rows * rank * 4, transcendentals=0),
-    )(where, x, bases_u, bases_v, bases_v)
+    )(where, x, bases_u, bases_v)
 
 
 def whole_factors(where, own_ref, partner_ref):
@@ -183,10 +192,6 @@
         ref[width:, :] = total_next[pl.ds(start, width), :]
 
 
-VMEM = pl.BlockSpec(memory_space=pltpu.VMEM)
-ANY = pl.BlockSpec(memory_space=pl.ANY)
-
-
 def middle(where, chunk, x, own, partner, bases_u, bases_v, level):
     rows, sides = x.shape
     rank = bases_u.shape[2]
@@ -207,9 +212,9 @@
     out_ref, found, sems = refs[-3:]
     factors = [halves(each) for each in whole_factors(where_ref[0], own_ref, partner_ref)]
     rows, columns = x_ref.shape
-    block = rows // STEPS
+    block = rows // LAST_STEPS
     copies = []
-    for step in range(STEPS):
+    for step in range(LAST_STEPS):
         at = slice(step * block, (step + 1) * block)
         found[at, :] = update(x_ref[at, :], u_ref[level, at], u_ref[level + 1, at], factors)
         place = (pl.ds(step * block, block), pl.ds(chunk * columns, columns))
@@ -229,7 +234,7 @@
         in_specs=[SMEM] + [VMEM] * 4 + [ANY] * len(more),
         out_specs=ANY,
         out_shape=jax.ShapeDtypeStruct((rows, sides), jnp.float32),
-        scratch_shapes=[pltpu.VMEM((rows, 2 * width), jnp.float32), pltpu.SemaphoreType.DMA((STEPS,))],
+        scratch_shapes=[pltpu.VMEM((rows, 2 * width), jnp.float32), pltpu.SemaphoreType.DMA((LAST_STEPS,))],
         input_output_aliases={5: 0} if more else {},
         compiler_params=pltpu.CompilerParams(vmem_limit_bytes=LAST * MIB),
         cost_estimate=pl.CostEstimate(flops=12 * rows * rank * width * 2, bytes_accessed=3 * rows * rank * 4, transcendentals=0),
@@ -366,6 +371,8 @@
     keep, send = first_sums(digits(places[0]), right_sides, bases_u, bases_v, 0)
     sums = keep + swap(send, places[0])
     sums, near.values, far.values = checkpoint(sums, near.values, far.values)
+    if HOLD:
+        right_sides, bases_u, bases_v = after((right_sides, bases_u, bases_v), send)
     main, gram = sums[:sides].reshape(2, CHUNKS, width, rank), sums[sides:]
     for step, place in enumerate(inner):
         main = halve(main, 2, place)

time: 125 us -> 125 us (level)
  local copies, waits for them, and re-layouts: 0.34 us -> 1.93 us
    unnamed x18 -> x20, local copies, waits for them, and re-layouts: 0.05 us -> 1.64 us
where the time goes in v4:
time: 125 us; the launch traced here: 124 us
  waiting for transfers between devices  69.2 us (55%)
  starting transfers between devices  33.4 us (27%)
  Pallas kernels  17.5 us (14%)
  local copies, waits for them, and re-layouts  1.93 us (2%)
  other arithmetic  1.26 us (1%)
    ppermute x27, waiting for transfers between devices, swap(): lax.ppermute(value, axis, [(i, i ^ 1 << bit) for i in range(lax.axis_size...  69.2 us
    ppermute x27, starting transfers between devices, swap(): lax.ppermute(value, axis, [(i, i ^ 1 << bit) for i in range(lax.axis_size...  33.4 us
    pallas_call x2, Pallas kernels, middle(): pl.pallas_call(functools.partial(middle_kernel, chunk, level), in_specs=[...  5.16 us
    pallas_call x1, Pallas kernels, first_sums(): pl.pallas_call(functools.partial(first_kernel, level), in_specs=[SMEM] +...  4.52 us
    pallas_call x2, Pallas kernels, last(): pl.pallas_call(functools.partial(last_kernel, chunk, level), in_specs=[SM...  3.87 us
  transfers between devices with their start and end apart: 27, of which 19 were waited for; matrix products, arithmetic and copies ran while one was open for 1% of the time, Pallas kernels for 9%

profile of v4, /device:TPU:0, one launch (start us, length us, event | category | flops | bytes accessed | tf_op | source)
XLA Modules:
  0.0 123.9 jit_solution(10470108697105108455)
XLA Ops:
  0.0 1.6 %copy-done.4 = f32[1024,512]{1,0:T(8,128)S(1)} copy-done((f32[1024,512]{1,0:T(8,128)S(1)}, f32[1024,512]{1,0:T(8,128)}, u32[]{:S(2)}) %copy-start.4) | copy-done | bytes 2097176
  1.6 4.5 %shard_map.73 = (f32[640,256]{1,0:T(8,128)S(1)}, f32[640,256]{1,0:T(8,128)S(1)}) custom-call(s32[1]{0:T(128)} %bitcast.1.where_ref, f32[1024,512]{1,0:T(8,128)S(1)} %copy-done.4, f32[4,1024,256]{2,1,0:T(8,128)} %u_ref.4, f32[4,1024,256]{2,1,0:T(8,128)} %v_ref.2), custom_call_target="tpu_custom_call" | custom-call | flops 2013265920 | bytes 5242880 | tf_op jit(solution)/shard_map/pallas_call | solution.py:146
  6.1 0.5 collective-permute-start
  6.7 1.6 %collective-permute-done = f32[640,256]{1,0:T(8,128)S(1)} collective-permute-done((f32[640,256]{1,0:T(8,128)S(1)}, f32[640,256]{1,0:T(8,128)S(1)}, u32[]{:S(2)}, u32[]{:S(2)}) %collective-permute-start) | collective-permute-done | bytes 655392 | tf_op jit(solution)/shard_map/ppermute | solution.py:29
  8.5 4.0 %collective-permute-start.2 = (f32[224,256]{1,0:T(8,128)S(1)}, f32[224,256]{1,0:T(8,128)S(1)}, u32[]{:S(2)}, u32[]{:S(2)}) collective-permute-start(f32[224,256]{1,0:T(8,128)S(1)} %pad_maximum_fusion.5), channel_id=1, source_target_pairs={{0,2},{1,3},{2,0},{3,1},{4,6},{5,7},{6,4},{7,5},{8,10},{9,11},{10,... | collective-permute-start | bytes 688136 | tf_op jit(solution)/shard_map/ppermute | solution.py:29
  12.6 1.6 %collective-permute-start.1 = (f32[2,2,64,256]{3,2,1,0:T(8,128)S(1)}, f32[2,2,64,256]{3,2,1,0:T(8,128)S(1)}, u32[]{:S(2)}, u32[]{:S(2)}) collective-permute-start(f32[2,2,64,256]{3,2,1,0:T(8,128)S(1)} %slice_select_fusion.8), channel_id=1, source_target_pairs={{0,1},{1,0},{2,3},{3,2},{4,5},{5,4},{6,7},{7,6},{8,9},{9,8},{10,11... | collective-permute-start | bytes 786440 | tf_op jit(solution)/shard_map/ppermute | solution.py:29
  14.2 9.3 %collective-permute-done.2 = f32[224,256]{1,0:T(8,128)S(1)} collective-permute-done((f32[224,256]{1,0:T(8,128)S(1)}, f32[224,256]{1,0:T(8,128)S(1)}, u32[]{:S(2)}, u32[]{:S(2)}) %collective-permute-start.2) | collective-permute-done | bytes 229408 | tf_op jit(solution)/shard_map/ppermute | solution.py:29
  23.6 0.9 collective-permute-done.1
  24.6 1.3 %collective-permute-start.3 = (f32[2,2,32,256]{3,2,1,0:T(8,128)S(1)}, f32[2,2,32,256]{3,2,1,0:T(8,128)S(1)}, u32[]{:S(2)}, u32[]{:S(2)}) collective-permute-start(f32[2,2,32,256]{3,2,1,0:T(8,128)S(1)} %slice_select_fusion.9), channel_id=1, source_target_pairs={{0,2},{1,3},{2,0},{3,1},{4,6},{5,7},{6,4},{7,5},{8,10},{9,11},{10,... | collective-permute-start | bytes 393224 | tf_op jit(solution)/shard_map/ppermute | solution.py:29
  26.0 2.0 %collective-permute-start.4 = (f32[320,256]{1,0:T(8,128)S(1)}, f32[320,256]{1,0:T(8,128)S(1)}, u32[]{:S(2)}, u32[]{:S(2)}) collective-permute-start(f32[320,256]{1,0:T(8,128)S(1)} %pad_maximum_fusion.2), channel_id=1, source_target_pairs={{0,1},{1,0},{2,3},{3,2},{4,5},{5,4},{6,7},{7,6},{8,9},{9,8},{10,11... | collective-permute-start | bytes 983048 | tf_op jit(solution)/shard_map/ppermute | solution.py:29
  27.9 4.2 %collective-permute-done.3 = f32[2,2,32,256]{3,2,1,0:T(8,128)S(1)} collective-permute-done((f32[2,2,32,256]{3,2,1,0:T(8,128)S(1)}, f32[2,2,32,256]{3,2,1,0:T(8,128)S(1)}, u32[]{:S(2)}, u32[]{:S(2)}) %collective-permute-start.3) | collective-permute-done | bytes 131104 | tf_op jit(solution)/shard_map/ppermute | solution.py:29
  32.2 4.7 %collective-permute-done.4 = f32[320,256]{1,0:T(8,128)S(1)} collective-permute-done((f32[320,256]{1,0:T(8,128)S(1)}, f32[320,256]{1,0:T(8,128)S(1)}, u32[]{:S(2)}, u32[]{:S(2)}) %collective-permute-start.4) | collective-permute-done | bytes 327712 | tf_op jit(solution)/shard_map/ppermute | solution.py:29
  37.0 1.5 %collective-permute-start.5 = (f32[384,256]{1,0:T(8,128)S(1)}, f32[384,256]{1,0:T(8,128)S(1)}, u32[]{:S(2)}, u32[]{:S(2)}) collective-permute-start(f32[384,256]{1,0:T(8,128)S(1)} %pad_maximum_fusion.1), channel_id=1, source_target_pairs={{0,8},{4,12},{8,0},{12,4},{16,24},{20,28},{24,16},{28,20},{1,9},{5... | collective-permute-start | bytes 1179656 | tf_op jit(solution)/shard_map/ppermute | solution.py:29
  38.6 0.6 shard_map.75
  39.2 1.1 collective-permute-start.9
  40.3 2.6 %collective-permute-start.10 = (f32[128,256]{1,0:T(8,128)S(1)}, f32[128,256]{1,0:T(8,128)S(1)}, u32[]{:S(2)}, u32[]{:S(2)}) collective-permute-start(f32[128,256]{1,0:T(8,128)S(1)} %bitcast.131), channel_id=1, source_target_pairs={{0,2},{1,3},{2,0},{3,1},{4,6},{5,7},{6,4},{7,5},{8,10},{9,11},{10,... | collective-permute-start | bytes 393224 | tf_op jit(solution)/shard_map/ppermute | solution.py:29
  42.9 4.3 %collective-permute-done.5 = f32[384,256]{1,0:T(8,128)S(1)} collective-permute-done((f32[384,256]{1,0:T(8,128)S(1)}, f32[384,256]{1,0:T(8,128)S(1)}, u32[]{:S(2)}, u32[]{:S(2)}) %collective-permute-start.5) | collective-permute-done | bytes 393248 | tf_op jit(solution)/shard_map/ppermute | solution.py:29
  47.4 0.5 collective-permute-done.10
  48.0 1.6 %collective-permute-start.6 = (f32[2,32,256]{2,1,0:T(8,128)S(1)}, f32[2,32,256]{2,1,0:T(8,128)S(1)}, u32[]{:S(2)}, u32[]{:S(2)}) collective-permute-start(f32[2,32,256]{2,1,0:T(8,128)S(1)} %bitcast_add_fusion), channel_id=1, source_target_pairs={{0,16},{4,20},{8,24},{12,28},{16,0},{20,4},{24,8},{28,12},{1,17},{... | collective-permute-start | bytes 196616 | tf_op jit(solution)/shard_map/ppermute | solution.py:29
  49.6 2.3 %collective-permute-start.11 = (f32[256,256]{1,0:T(8,128)S(1)}, f32[256,256]{1,0:T(8,128)S(1)}, u32[]{:S(2)}, u32[]{:S(2)}) collective-permute-start(f32[256,256]{1,0:T(8,128)S(1)} %bitcast.117), channel_id=1, source_target_pairs={{0,1},{1,0},{2,3},{3,2},{4,5},{5,4},{6,7},{7,6},{8,9},{9,8},{10,11... | collective-permute-start | bytes 786440 | tf_op jit(solution)/shard_map/ppermute | solution.py:29
  52.4 1.2 shard_map.74
  53.6 3.4 %collective-permute-start.8 = (f32[2,2,32,256]{3,2,1,0:T(8,128)S(1)}, f32[2,2,32,256]{3,2,1,0:T(8,128)S(1)}, u32[]{:S(2)}, u32[]{:S(2)}) collective-permute-start(f32[2,2,32,256]{3,2,1,0:T(8,128)S(1)} %shard_map.74), channel_id=1, source_target_pairs={{0,2},{1,3},{2,0},{3,1},{4,6},{5,7},{6,4},{7,5},{8,10},{9,11},{10,... | collective-permute-start | bytes 393224 | tf_op jit(solution)/shard_map/ppermute | solution.py:29
  57.0 4.9 %collective-permute-done.8 = f32[2,2,32,256]{3,2,1,0:T(8,128)S(1)} collective-permute-done((f32[2,2,32,256]{3,2,1,0:T(8,128)S(1)}, f32[2,2,32,256]{3,2,1,0:T(8,128)S(1)}, u32[]{:S(2)}, u32[]{:S(2)}) %collective-permute-start.8) | collective-permute-done | bytes 131104 | tf_op jit(solution)/shard_map/ppermute | solution.py:29
  62.4 1.7 %collective-permute-start.12 = (f32[2,64,256]{2,1,0:T(8,128)S(1)}, f32[2,64,256]{2,1,0:T(8,128)S(1)}, u32[]{:S(2)}, u32[]{:S(2)}) collective-permute-start(f32[2,64,256]{2,1,0:T(8,128)S(1)} %get-tuple-element.104), channel_id=1, source_target_pairs={{0,1},{1,0},{2,3},{3,2},{4,5},{5,4},{6,7},{7,6},{8,9},{9,8},{10,11... | collective-permute-start | bytes 393224 | tf_op jit(solution)/shard_map/ppermute | solution.py:29
  64.1 2.9 %collective-permute-done.16 = f32[2,64,256]{2,1,0:T(8,128)S(1)} collective-permute-done((f32[2,64,256]{2,1,0:T(8,128)S(1)}, f32[2,64,256]{2,1,0:T(8,128)S(1)}, u32[]{:S(2)}, u32[]{:S(2)}) %collective-permute-start.16) | collective-permute-done | bytes 131104 | tf_op jit(solution)/shard_map/ppermute | solution.py:29
  67.2 1.3 %collective-permute-done.12 = f32[2,64,256]{2,1,0:T(8,128)S(1)} collective-permute-done((f32[2,64,256]{2,1,0:T(8,128)S(1)}, f32[2,64,256]{2,1,0:T(8,128)S(1)}, u32[]{:S(2)}, u32[]{:S(2)}) %collective-permute-start.12) | collective-permute-done | bytes 131104 | tf_op jit(solution)/shard_map/ppermute | solution.py:29
  68.7 2.6 %shard_map.77 = (f32[1024,256]{1,0:T(8,128)S(1)}, f32[256,256]{1,0:T(8,128)S(1)}, f32[256,256]{1,0:T(8,128)S(1)}) custom-call(s32[2]{0:T(128)S(1)} %pad_add_fusion.where_ref, f32[1024,512]{1,0:T(8,128)S(1)} %copy-done.5, f32[2,128,256]{2,1,0:T(8,128)S(1)} %maximum_select_fusion.11.own_ref, f32[2,128,256]{2,1,0:T(8,128)S(1)} %collective-permute-done.17.partner_ref, ...), custom_call_target="tpu_custom_call" | custom-call | flops 1610612736 | bytes 4194304 | tf_op jit(solution)/shard_map/pallas_call | solution.py:200
  71.3 0.7 collective-permute-start.18
  72.0 2.6 %shard_map.76 = (f32[1024,256]{1,0:T(8,128)S(1)}, f32[256,256]{1,0:T(8,128)S(1)}, f32[256,256]{1,0:T(8,128)S(1)}) custom-call(s32[2]{0:T(128)S(1)} %pad_add_fusion.where_ref, f32[1024,512]{1,0:T(8,128)S(1)} %copy-done.5, f32[2,128,256]{2,1,0:T(8,128)S(1)} %maximum_select_fusion.10.own_ref, f32[2,128,256]{2,1,0:T(8,128)S(1)} %collective-permute-done.13.partner_ref, ...), custom_call_target="tpu_custom_call" | custom-call | flops 1610612736 | bytes 4194304 | tf_op jit(solution)/shard_map/pallas_call | solution.py:200
  74.5 1.5 %collective-permute-start.14 = (f32[256,256]{1,0:T(8,128)S(1)}, f32[256,256]{1,0:T(8,128)S(1)}, u32[]{:S(2)}, u32[]{:S(2)}) collective-permute-start(f32[256,256]{1,0:T(8,128)S(1)} %get-tuple-element.64), channel_id=1, source_target_pairs={{0,1},{1,0},{2,3},{3,2},{4,5},{5,4},{6,7},{7,6},{8,9},{9,8},{10,11... | collective-permute-start | bytes 786440 | tf_op jit(solution)/shard_map/ppermute | solution.py:29
  76.1 4.4 %collective-permute-done.18 = f32[256,256]{1,0:T(8,128)S(1)} collective-permute-done((f32[256,256]{1,0:T(8,128)S(1)}, f32[256,256]{1,0:T(8,128)S(1)}, u32[]{:S(2)}, u32[]{:S(2)}) %collective-permute-start.18) | collective-permute-done | bytes 262176 | tf_op jit(solution)/shard_map/ppermute | solution.py:29
  80.5 1.5 %collective-permute-start.19 = (f32[128,256]{1,0:T(8,128)S(1)}, f32[128,256]{1,0:T(8,128)S(1)}, u32[]{:S(2)}, u32[]{:S(2)}) collective-permute-start(f32[128,256]{1,0:T(8,128)S(1)} %slice.117), channel_id=1, source_target_pairs={{0,2},{1,3},{2,0},{3,1},{4,6},{5,7},{6,4},{7,5},{8,10},{9,11},{10,... | collective-permute-start | bytes 393224 | tf_op jit(solution)/shard_map/ppermute | solution.py:29
  82.0 1.5 %collective-permute-start.24 = (f32[256,256]{1,0:T(8,128)S(1)}, f32[256,256]{1,0:T(8,128)S(1)}, u32[]{:S(2)}, u32[]{:S(2)}) collective-permute-start(f32[256,256]{1,0:T(8,128)S(1)} %bitcast.120), channel_id=1, source_target_pairs={{0,1},{1,0},{2,3},{3,2},{4,5},{5,4},{6,7},{7,6},{8,9},{9,8},{10,11... | collective-permute-start | bytes 786440 | tf_op jit(solution)/shard_map/ppermute | solution.py:29
  83.6 5.3 %collective-permute-done.14 = f32[256,256]{1,0:T(8,128)S(1)} collective-permute-done((f32[256,256]{1,0:T(8,128)S(1)}, f32[256,256]{1,0:T(8,128)S(1)}, u32[]{:S(2)}, u32[]{:S(2)}) %collective-permute-start.14) | collective-permute-done | bytes 262176 | tf_op jit(solution)/shard_map/ppermute | solution.py:29
  89.3 1.2 collective-permute-done.20.upper_other
  90.5 0.6 shard_map.78
  91.1 4.1 %collective-permute-done.15 = f32[128,256]{1,0:T(8,128)S(1)} collective-permute-done((f32[128,256]{1,0:T(8,128)S(1)}, f32[128,256]{1,0:T(8,128)S(1)}, u32[]{:S(2)}, u32[]{:S(2)}) %collective-permute-start.15) | collective-permute-done | bytes 131104 | tf_op jit(solution)/shard_map/ppermute | solution.py:29
  95.3 1.6 %collective-permute-done.24 = f32[256,256]{1,0:T(8,128)S(1)} collective-permute-done((f32[256,256]{1,0:T(8,128)S(1)}, f32[256,256]{1,0:T(8,128)S(1)}, u32[]{:S(2)}, u32[]{:S(2)}) %collective-permute-start.24) | collective-permute-done | bytes 262176 | tf_op jit(solution)/shard_map/ppermute | solution.py:29
  96.9 1.8 %collective-permute-start.23 = (f32[128,256]{1,0:T(8,128)S(1)}, f32[128,256]{1,0:T(8,128)S(1)}, u32[]{:S(2)}, u32[]{:S(2)}) collective-permute-start(f32[128,256]{1,0:T(8,128)S(1)} %get-tuple-element.70.own), channel_id=1, source_target_pairs={{0,2},{1,3},{2,0},{3,1},{4,6},{5,7},{6,4},{7,5},{8,10},{9,11},{10,... | collective-permute-start | bytes 393224 | tf_op jit(solution)/shard_map/ppermute | solution.py:29
  98.7 0.6 shard_map.79
  99.4 1.3 %collective-permute-start.22 = (f32[128,256]{1,0:T(8,128)S(1)}, f32[128,256]{1,0:T(8,128)S(1)}, u32[]{:S(2)}, u32[]{:S(2)}) collective-permute-start(f32[128,256]{1,0:T(8,128)S(1)} %get-tuple-element.73.own), channel_id=1, source_target_pairs={{0,2},{1,3},{2,0},{3,1},{4,6},{5,7},{6,4},{7,5},{8,10},{9,11},{10,... | collective-permute-start | bytes 393224 | tf_op jit(solution)/shard_map/ppermute | solution.py:29
  100.7 8.8 %collective-permute-done.23.sibling = f32[128,256]{1,0:T(8,128)S(1)} collective-permute-done((f32[128,256]{1,0:T(8,128)S(1)}, f32[128,256]{1,0:T(8,128)S(1)}, u32[]{:S(2)}, u32[]{:S(2)}) %collective-permute-start.23) | collective-permute-done | bytes 131104 | tf_op jit(solution)/shard_map/ppermute | solution.py:29
  110.0 1.5 %collective-permute-done.22.sibling = f32[128,256]{1,0:T(8,128)S(1)} collective-permute-done((f32[128,256]{1,0:T(8,128)S(1)}, f32[128,256]{1,0:T(8,128)S(1)}, u32[]{:S(2)}, u32[]{:S(2)}) %collective-permute-start.22) | collective-permute-done | bytes 131104 | tf_op jit(solution)/shard_map/ppermute | solution.py:29
  111.9 0.6 collective-permute-start.25
  112.5 6.4 %collective-permute-done.26.partner_ref = f32[2,128,256]{2,1,0:T(8,128)S(1)} collective-permute-done((f32[2,128,256]{2,1,0:T(8,128)S(1)}, f32[2,128,256]{2,1,0:T(8,128)S(1)}, u32[]{:S(2)}, u32[]{:S(2)}) %collective-permute-start.26) | collective-permute-done | bytes 262176 | tf_op jit(solution)/shard_map/ppermute | solution.py:29
  118.9 1.9 %shard_map.82.refs_0_ = f32[1024,512]{1,0:T(8,128)} custom-call(s32[1]{0:T(128)} %bitcast.where_ref, f32[1024,256]{1,0:T(8,128)S(1)} %get-tuple-element.75.x_ref, f32[2,128,256]{2,1,0:T(8,128)S(1)} %shard_map.80.own_ref, f32[2,128,256]{2,1,0:T(8,128)S(1)} %collective-permute-done.26.partner_ref, f32[4,1024,256]{2,1,0:T(8,128)S(1)} %copy-done.1), custom_call_target="tpu_custom_call" | custom-call | flops 805306368 | bytes 3145728 | tf_op jit(solution)/shard_map/pallas_call | solution.py:232
  120.8 1.1 collective-permute-done.25.partner_ref
  122.0 1.9 %shard_map.83 = f32[1024,512]{1,0:T(8,128)} custom-call(s32[1]{0:T(128)} %bitcast.where_ref, f32[1024,256]{1,0:T(8,128)S(1)} %get-tuple-element.62.x_ref, f32[2,128,256]{2,1,0:T(8,128)S(1)} %shard_map.81.own_ref, f32[2,128,256]{2,1,0:T(8,128)S(1)} %collective-permute-done.25.partner_ref, ...), custom_call_target="tpu_custom_call", output_to_operand_aliasing={{}: (5, {})} | custom-call | flops 805306368 | bytes 3145728 | tf_op jit(solution)/shard_map/pallas_call | solution.py:232
  (98 shorter events, 3.3 us)
Async XLA Ops:
  0.0 1.6 %copy-start.4 = (f32[1024,512]{1,0:T(8,128)S(1)}, f32[1024,512]{1,0:T(8,128)}, u32[]{:S(2)}) copy-start(f32[1024,512]{1,0:T(8,128)} %old_ref.1) | copy-start | bytes 6291460
  1.6 5.0 %copy-start.9 = (f32[16,512]{1,0:T(8,128)S(1)}, f32[16,512]{1,0:T(8,128)}, u32[]{:S(2)}) copy-start(f32[16,512]{1,0:T(8,128)} %param.10) | copy-start | bytes 98308
  1.6 5.1 %copy-start.8 = (f32[32,512]{1,0:T(8,128)S(1)}, f32[32,512]{1,0:T(8,128)}, u32[]{:S(2)}) copy-start(f32[32,512]{1,0:T(8,128)} %param.11) | copy-start | bytes 196612
  1.6 5.1 %copy-start.7 = (f32[64,512]{1,0:T(8,128)S(1)}, f32[64,512]{1,0:T(8,128)}, u32[]{:S(2)}) copy-start(f32[64,512]{1,0:T(8,128)} %param.12) | copy-start | bytes 393220
  6.1 2.2 %collective-permute-start = (f32[640,256]{1,0:T(8,128)S(1)}, f32[640,256]{1,0:T(8,128)S(1)}, u32[]{:S(2)}, u32[]{:S(2)}) collective-permute-start(f32[640,256]{1,0:T(8,128)S(1)} %get-tuple-element.41), channel_id=1, source_target_pairs={{0,4},{4,0},{8,12},{12,8},{16,20},{20,16},{24,28},{28,24},{1,5},{5... | collective-permute-start | bytes 1966088 | tf_op jit(solution)/shard_map/ppermute | solution.py:29
  8.4 30.1 %copy-start.2 = (f32[4,1024,256]{2,1,0:T(8,128)S(1)}, f32[4,1024,256]{2,1,0:T(8,128)}, u32[]{:S(2)}) copy-start(f32[4,1024,256]{2,1,0:T(8,128)} %v_ref.2) | copy-start | bytes 12582916
  8.5 15.0 %collective-permute-start.2 = (f32[224,256]{1,0:T(8,128)S(1)}, f32[224,256]{1,0:T(8,128)S(1)}, u32[]{:S(2)}, u32[]{:S(2)}) collective-permute-start(f32[224,256]{1,0:T(8,128)S(1)} %pad_maximum_fusion.5), channel_id=1, source_target_pairs={{0,2},{1,3},{2,0},{3,1},{4,6},{5,7},{6,4},{7,5},{8,10},{9,11},{10,... | collective-permute-start | bytes 688136 | tf_op jit(solution)/shard_map/ppermute | solution.py:29
  12.6 11.9 %collective-permute-start.1 = (f32[2,2,64,256]{3,2,1,0:T(8,128)S(1)}, f32[2,2,64,256]{3,2,1,0:T(8,128)S(1)}, u32[]{:S(2)}, u32[]{:S(2)}) collective-permute-start(f32[2,2,64,256]{3,2,1,0:T(8,128)S(1)} %slice_select_fusion.8), channel_id=1, source_target_pairs={{0,1},{1,0},{2,3},{3,2},{4,5},{5,4},{6,7},{7,6},{8,9},{9,8},{10,11... | collective-permute-start | bytes 786440 | tf_op jit(solution)/shard_map/ppermute | solution.py:29
  24.5 14.1 %copy-start = (f32[4,1024,256]{2,1,0:T(8,128)S(1)}, f32[4,1024,256]{2,1,0:T(8,128)}, u32[]{:S(2)}) copy-start(f32[4,1024,256]{2,1,0:T(8,128)} %u_ref.4) | copy-start | bytes 12582916
  24.6 7.6 %collective-permute-start.3 = (f32[2,2,32,256]{3,2,1,0:T(8,128)S(1)}, f32[2,2,32,256]{3,2,1,0:T(8,128)S(1)}, u32[]{:S(2)}, u32[]{:S(2)}) collective-permute-start(f32[2,2,32,256]{3,2,1,0:T(8,128)S(1)} %slice_select_fusion.9), channel_id=1, source_target_pairs={{0,2},{1,3},{2,0},{3,1},{4,6},{5,7},{6,4},{7,5},{8,10},{9,11},{10,... | collective-permute-start | bytes 393224 | tf_op jit(solution)/shard_map/ppermute | solution.py:29
  26.0 10.9 %collective-permute-start.4 = (f32[320,256]{1,0:T(8,128)S(1)}, f32[320,256]{1,0:T(8,128)S(1)}, u32[]{:S(2)}, u32[]{:S(2)}) collective-permute-start(f32[320,256]{1,0:T(8,128)S(1)} %pad_maximum_fusion.2), channel_id=1, source_target_pairs={{0,1},{1,0},{2,3},{3,2},{4,5},{5,4},{6,7},{7,6},{8,9},{9,8},{10,11... | collective-permute-start | bytes 983048 | tf_op jit(solution)/shard_map/ppermute | solution.py:29
  37.0 10.1 %collective-permute-start.5 = (f32[384,256]{1,0:T(8,128)S(1)}, f32[384,256]{1,0:T(8,128)S(1)}, u32[]{:S(2)}, u32[]{:S(2)}) collective-permute-start(f32[384,256]{1,0:T(8,128)S(1)} %pad_maximum_fusion.1), channel_id=1, source_target_pairs={{0,8},{4,12},{8,0},{12,4},{16,24},{20,28},{24,16},{28,20},{1,9},{5... | collective-permute-start | bytes 1179656 | tf_op jit(solution)/shard_map/ppermute | solution.py:29
  39.2 22.8 %collective-permute-start.9 = (f32[256,256]{1,0:T(8,128)S(1)}, f32[256,256]{1,0:T(8,128)S(1)}, u32[]{:S(2)}, u32[]{:S(2)}) collective-permute-start(f32[256,256]{1,0:T(8,128)S(1)} %shard_map.75), channel_id=1, source_target_pairs={{0,1},{1,0},{2,3},{3,2},{4,5},{5,4},{6,7},{7,6},{8,9},{9,8},{10,11... | collective-permute-start | bytes 786440 | tf_op jit(solution)/shard_map/ppermute | solution.py:29
  40.3 7.6 %collective-permute-start.10 = (f32[128,256]{1,0:T(8,128)S(1)}, f32[128,256]{1,0:T(8,128)S(1)}, u32[]{:S(2)}, u32[]{:S(2)}) collective-permute-start(f32[128,256]{1,0:T(8,128)S(1)} %bitcast.131), channel_id=1, source_target_pairs={{0,2},{1,3},{2,0},{3,1},{4,6},{5,7},{6,4},{7,5},{8,10},{9,11},{10,... | collective-permute-start | bytes 393224 | tf_op jit(solution)/shard_map/ppermute | solution.py:29
  47.3 4.6 %collective-permute-start.7 = (f32[768,256]{1,0:T(8,128)S(1)}, f32[768,256]{1,0:T(8,128)S(1)}, u32[]{:S(2)}, u32[]{:S(2)}) collective-permute-start(f32[768,256]{1,0:T(8,128)S(1)} %pad_maximum_fusion), channel_id=1, source_target_pairs={{0,4},{4,0},{8,12},{12,8},{16,20},{20,16},{24,28},{28,24},{1,5},{5... | collective-permute-start | bytes 2359304 | tf_op jit(solution)/shard_map/ppermute | solution.py:29
  48.0 4.3 %collective-permute-start.6 = (f32[2,32,256]{2,1,0:T(8,128)S(1)}, f32[2,32,256]{2,1,0:T(8,128)S(1)}, u32[]{:S(2)}, u32[]{:S(2)}) collective-permute-start(f32[2,32,256]{2,1,0:T(8,128)S(1)} %bitcast_add_fusion), channel_id=1, source_target_pairs={{0,16},{4,20},{8,24},{12,28},{16,0},{20,4},{24,8},{28,12},{1,17},{... | collective-permute-start | bytes 196616 | tf_op jit(solution)/shard_map/ppermute | solution.py:29
  49.6 12.4 %collective-permute-start.11 = (f32[256,256]{1,0:T(8,128)S(1)}, f32[256,256]{1,0:T(8,128)S(1)}, u32[]{:S(2)}, u32[]{:S(2)}) collective-permute-start(f32[256,256]{1,0:T(8,128)S(1)} %bitcast.117), channel_id=1, source_target_pairs={{0,1},{1,0},{2,3},{3,2},{4,5},{5,4},{6,7},{7,6},{8,9},{9,8},{10,11... | collective-permute-start | bytes 786440 | tf_op jit(solution)/shard_map/ppermute | solution.py:29
  51.9 16.7 %copy-start.5 = (f32[1024,512]{1,0:T(8,128)S(1)}, f32[1024,512]{1,0:T(8,128)}, u32[]{:S(2)}) copy-start(f32[1024,512]{1,0:T(8,128)} %old_ref.1) | copy-start | bytes 6291460
  52.1 16.6 %copy-start.3 = (f32[4,1024,256]{2,1,0:T(8,128)S(1)}, f32[4,1024,256]{2,1,0:T(8,128)}, u32[]{:S(2)}) copy-start(f32[4,1024,256]{2,1,0:T(8,128)} %v_ref.2) | copy-start | bytes 12582916
  52.3 16.4 %copy-start.1 = (f32[4,1024,256]{2,1,0:T(8,128)S(1)}, f32[4,1024,256]{2,1,0:T(8,128)}, u32[]{:S(2)}) copy-start(f32[4,1024,256]{2,1,0:T(8,128)} %u_ref.4) | copy-start | bytes 12582916
  53.6 8.4 %collective-permute-start.8 = (f32[2,2,32,256]{3,2,1,0:T(8,128)S(1)}, f32[2,2,32,256]{3,2,1,0:T(8,128)S(1)}, u32[]{:S(2)}, u32[]{:S(2)}) collective-permute-start(f32[2,2,32,256]{3,2,1,0:T(8,128)S(1)} %shard_map.74), channel_id=1, source_target_pairs={{0,2},{1,3},{2,0},{3,1},{4,6},{5,7},{6,4},{7,5},{8,10},{9,11},{10,... | collective-permute-start | bytes 393224 | tf_op jit(solution)/shard_map/ppermute | solution.py:29
  62.0 5.0 %collective-permute-start.16 = (f32[2,64,256]{2,1,0:T(8,128)S(1)}, f32[2,64,256]{2,1,0:T(8,128)S(1)}, u32[]{:S(2)}, u32[]{:S(2)}) collective-permute-start(f32[2,64,256]{2,1,0:T(8,128)S(1)} %get-tuple-element.103), channel_id=1, source_target_pairs={{0,1},{1,0},{2,3},{3,2},{4,5},{5,4},{6,7},{7,6},{8,9},{9,8},{10,11... | collective-permute-start | bytes 393224 | tf_op jit(solution)/shard_map/ppermute | solution.py:29
  62.4 6.1 %collective-permute-start.12 = (f32[2,64,256]{2,1,0:T(8,128)S(1)}, f32[2,64,256]{2,1,0:T(8,128)S(1)}, u32[]{:S(2)}, u32[]{:S(2)}) collective-permute-start(f32[2,64,256]{2,1,0:T(8,128)S(1)} %get-tuple-element.104), channel_id=1, source_target_pairs={{0,1},{1,0},{2,3},{3,2},{4,5},{5,4},{6,7},{7,6},{8,9},{9,8},{10,11... | collective-permute-start | bytes 393224 | tf_op jit(solution)/shard_map/ppermute | solution.py:29
  67.1 1.6 %collective-permute-start.17 = (f32[2,128,256]{2,1,0:T(8,128)S(1)}, f32[2,128,256]{2,1,0:T(8,128)S(1)}, u32[]{:S(2)}, u32[]{:S(2)}) collective-permute-start(f32[2,128,256]{2,1,0:T(8,128)S(1)} %maximum_select_fusion.11.own_ref), channel_id=1, source_target_pairs={{0,4},{4,0},{8,12},{12,8},{16,20},{20,16},{24,28},{28,24},{1,5},{5... | collective-permute-start | bytes 786440 | tf_op jit(solution)/shard_map/ppermute | solution.py:29
  68.5 3.5 %collective-permute-start.13 = (f32[2,128,256]{2,1,0:T(8,128)S(1)}, f32[2,128,256]{2,1,0:T(8,128)S(1)}, u32[]{:S(2)}, u32[]{:S(2)}) collective-permute-start(f32[2,128,256]{2,1,0:T(8,128)S(1)} %maximum_select_fusion.10.own_ref), channel_id=1, source_target_pairs={{0,4},{4,0},{8,12},{12,8},{16,20},{20,16},{24,28},{28,24},{1,5},{5... | collective-permute-start | bytes 786440 | tf_op jit(solution)/shard_map/ppermute | solution.py:29
  71.3 4.8 %copy-start.6 = (f32[128,512]{1,0:T(8,128)S(1)}, f32[128,512]{1,0:T(8,128)}, u32[]{:S(2)}) copy-start(f32[128,512]{1,0:T(8,128)} %param.13) | copy-start | bytes 786436
  71.3 9.2 %collective-permute-start.18 = (f32[256,256]{1,0:T(8,128)S(1)}, f32[256,256]{1,0:T(8,128)S(1)}, u32[]{:S(2)}, u32[]{:S(2)}) collective-permute-start(f32[256,256]{1,0:T(8,128)S(1)} %get-tuple-element.66), channel_id=1, source_target_pairs={{0,1},{1,0},{2,3},{3,2},{4,5},{5,4},{6,7},{7,6},{8,9},{9,8},{10,11... | collective-permute-start | bytes 786440 | tf_op jit(solution)/shard_map/ppermute | solution.py:29
  74.5 14.4 %collective-permute-start.14 = (f32[256,256]{1,0:T(8,128)S(1)}, f32[256,256]{1,0:T(8,128)S(1)}, u32[]{:S(2)}, u32[]{:S(2)}) collective-permute-start(f32[256,256]{1,0:T(8,128)S(1)} %get-tuple-element.64), channel_id=1, source_target_pairs={{0,1},{1,0},{2,3},{3,2},{4,5},{5,4},{6,7},{7,6},{8,9},{9,8},{10,11... | collective-permute-start | bytes 786440 | tf_op jit(solution)/shard_map/ppermute | solution.py:29
  80.5 8.5 %collective-permute-start.19 = (f32[128,256]{1,0:T(8,128)S(1)}, f32[128,256]{1,0:T(8,128)S(1)}, u32[]{:S(2)}, u32[]{:S(2)}) collective-permute-start(f32[128,256]{1,0:T(8,128)S(1)} %slice.117), channel_id=1, source_target_pairs={{0,2},{1,3},{2,0},{3,1},{4,6},{5,7},{6,4},{7,5},{8,10},{9,11},{10,... | collective-permute-start | bytes 393224 | tf_op jit(solution)/shard_map/ppermute | solution.py:29
  82.0 14.9 %collective-permute-start.24 = (f32[256,256]{1,0:T(8,128)S(1)}, f32[256,256]{1,0:T(8,128)S(1)}, u32[]{:S(2)}, u32[]{:S(2)}) collective-permute-start(f32[256,256]{1,0:T(8,128)S(1)} %bitcast.120), channel_id=1, source_target_pairs={{0,1},{1,0},{2,3},{3,2},{4,5},{5,4},{6,7},{7,6},{8,9},{9,8},{10,11... | collective-permute-start | bytes 786440 | tf_op jit(solution)/shard_map/ppermute | solution.py:29
  89.0 6.2 %collective-permute-start.15 = (f32[128,256]{1,0:T(8,128)S(1)}, f32[128,256]{1,0:T(8,128)S(1)}, u32[]{:S(2)}, u32[]{:S(2)}) collective-permute-start(f32[128,256]{1,0:T(8,128)S(1)} %slice.116), channel_id=1, source_target_pairs={{0,2},{1,3},{2,0},{3,1},{4,6},{5,7},{6,4},{7,5},{8,10},{9,11},{10,... | collective-permute-start | bytes 393224 | tf_op jit(solution)/shard_map/ppermute | solution.py:29
  89.1 1.4 %collective-permute-start.20 = (f32[128,256]{1,0:T(8,128)S(1)}, f32[128,256]{1,0:T(8,128)S(1)}, u32[]{:S(2)}, u32[]{:S(2)}) collective-permute-start(f32[128,256]{1,0:T(8,128)S(1)} %get-tuple-element.102.upper), channel_id=1, source_target_pairs={{0,4},{4,0},{8,12},{12,8},{16,20},{20,16},{24,28},{28,24},{1,5},{5... | collective-permute-start | bytes 393224 | tf_op jit(solution)/shard_map/ppermute | solution.py:29
  95.2 3.5 %collective-permute-start.21 = (f32[128,256]{1,0:T(8,128)S(1)}, f32[128,256]{1,0:T(8,128)S(1)}, u32[]{:S(2)}, u32[]{:S(2)}) collective-permute-start(f32[128,256]{1,0:T(8,128)S(1)} %get-tuple-element.100.upper), channel_id=1, source_target_pairs={{0,4},{4,0},{8,12},{12,8},{16,20},{20,16},{24,28},{28,24},{1,5},{5... | collective-permute-start | bytes 393224 | tf_op jit(solution)/shard_map/ppermute | solution.py:29
  96.9 12.6 %collective-permute-start.23 = (f32[128,256]{1,0:T(8,128)S(1)}, f32[128,256]{1,0:T(8,128)S(1)}, u32[]{:S(2)}, u32[]{:S(2)}) collective-permute-start(f32[128,256]{1,0:T(8,128)S(1)} %get-tuple-element.70.own), channel_id=1, source_target_pairs={{0,2},{1,3},{2,0},{3,1},{4,6},{5,7},{6,4},{7,5},{8,10},{9,11},{10,... | collective-permute-start | bytes 393224 | tf_op jit(solution)/shard_map/ppermute | solution.py:29
  99.4 12.1 %collective-permute-start.22 = (f32[128,256]{1,0:T(8,128)S(1)}, f32[128,256]{1,0:T(8,128)S(1)}, u32[]{:S(2)}, u32[]{:S(2)}) collective-permute-start(f32[128,256]{1,0:T(8,128)S(1)} %get-tuple-element.73.own), channel_id=1, source_target_pairs={{0,2},{1,3},{2,0},{3,1},{4,6},{5,7},{6,4},{7,5},{8,10},{9,11},{10,... | collective-permute-start | bytes 393224 | tf_op jit(solution)/shard_map/ppermute | solution.py:29
  109.9 9.0 %collective-permute-start.26 = (f32[2,128,256]{2,1,0:T(8,128)S(1)}, f32[2,128,256]{2,1,0:T(8,128)S(1)}, u32[]{:S(2)}, u32[]{:S(2)}) collective-permute-start(f32[2,128,256]{2,1,0:T(8,128)S(1)} %shard_map.80.own_ref), channel_id=1, source_target_pairs={{0,1},{1,0},{2,3},{3,2},{4,5},{5,4},{6,7},{7,6},{8,9},{9,8},{10,11... | collective-permute-start | bytes 786440 | tf_op jit(solution)/shard_map/ppermute | solution.py:29
  111.9 10.1 %collective-permute-start.25 = (f32[2,128,256]{2,1,0:T(8,128)S(1)}, f32[2,128,256]{2,1,0:T(8,128)S(1)}, u32[]{:S(2)}, u32[]{:S(2)}) collective-permute-start(f32[2,128,256]{2,1,0:T(8,128)S(1)} %shard_map.81.own_ref), channel_id=1, source_target_pairs={{0,1},{1,0},{2,3},{3,2},{4,5},{5,4},{6,7},{7,6},{8,9},{9,8},{10,11... | collective-permute-start | bytes 786440 | tf_op jit(solution)/shard_map/ppermute | solution.py:29

commit v5 on v4

--- a/solution.py
+++ b/solution.py
@@ -13,7 +13,7 @@
 LOW = -1
 HOLD = True
 FIRST = 50
-FIRST_STEPS = 4
+FIRST_STEPS = 2
 LAST_STEPS = 4
 MID = 24
 LAST = 24

time: 125 us -> 124 us (level)
  no operation moved by 1% of the time
where the time goes in v5:
time: 124 us
  waiting for transfers between devices  69.2 us (56%)
  starting transfers between devices  33.4 us (27%)
  Pallas kernels  17.3 us (14%)
  local copies, waits for them, and re-layouts  1.93 us (2%)
  other arithmetic  1.26 us (1%)
    ppermute x27, waiting for transfers between devices, swap(): lax.ppermute(value, axis, [(i, i ^ 1 << bit) for i in range(lax.axis_size...  69.2 us
    ppermute x27, starting transfers between devices, swap(): lax.ppermute(value, axis, [(i, i ^ 1 << bit) for i in range(lax.axis_size...  33.4 us
    pallas_call x2, Pallas kernels, middle(): pl.pallas_call(functools.partial(middle_kernel, chunk, level), in_specs=[...  5.16 us
    pallas_call x1, Pallas kernels, first_sums(): pl.pallas_call(functools.partial(first_kernel, level), in_specs=[SMEM] +...  4.31 us
    pallas_call x2, Pallas kernels, last(): pl.pallas_call(functools.partial(last_kernel, chunk, level), in_specs=[SM...  3.86 us
  transfers between devices with their start and end apart: 27, of which 19 were waited for; matrix products, arithmetic and copies ran while one was open for 1% of the time, Pallas kernels for 9%

profile of v5, /device:TPU:0, one launch (start us, length us, event | category | flops | bytes accessed | tf_op | source)
XLA Modules:
  0.0 123.7 jit_solution(2224681926235612511)
XLA Ops:
  0.0 1.6 %copy-done.4 = f32[1024,512]{1,0:T(8,128)S(1)} copy-done((f32[1024,512]{1,0:T(8,128)S(1)}, f32[1024,512]{1,0:T(8,128)}, u32[]{:S(2)}) %copy-start.4) | copy-done | bytes 2097176
  1.6 4.3 %shard_map.73 = (f32[640,256]{1,0:T(8,128)S(1)}, f32[640,256]{1,0:T(8,128)S(1)}) custom-call(s32[1]{0:T(128)} %bitcast.1.where_ref, f32[1024,512]{1,0:T(8,128)S(1)} %copy-done.4, f32[4,1024,256]{2,1,0:T(8,128)} %u_ref.4, f32[4,1024,256]{2,1,0:T(8,128)} %v_ref.2), custom_call_target="tpu_custom_call" | custom-call | flops 2013265920 | bytes 5242880 | tf_op jit(solution)/shard_map/pallas_call | solution.py:146
  5.9 0.5 collective-permute-start
  6.5 1.6 %collective-permute-done = f32[640,256]{1,0:T(8,128)S(1)} collective-permute-done((f32[640,256]{1,0:T(8,128)S(1)}, f32[640,256]{1,0:T(8,128)S(1)}, u32[]{:S(2)}, u32[]{:S(2)}) %collective-permute-start) | collective-permute-done | bytes 655392 | tf_op jit(solution)/shard_map/ppermute | solution.py:29
  8.3 4.0 %collective-permute-start.2 = (f32[224,256]{1,0:T(8,128)S(1)}, f32[224,256]{1,0:T(8,128)S(1)}, u32[]{:S(2)}, u32[]{:S(2)}) collective-permute-start(f32[224,256]{1,0:T(8,128)S(1)} %pad_maximum_fusion.5), channel_id=1, source_target_pairs={{0,2},{1,3},{2,0},{3,1},{4,6},{5,7},{6,4},{7,5},{8,10},{9,11},{10,... | collective-permute-start | bytes 688136 | tf_op jit(solution)/shard_map/ppermute | solution.py:29
  12.4 1.6 %collective-permute-start.1 = (f32[2,2,64,256]{3,2,1,0:T(8,128)S(1)}, f32[2,2,64,256]{3,2,1,0:T(8,128)S(1)}, u32[]{:S(2)}, u32[]{:S(2)}) collective-permute-start(f32[2,2,64,256]{3,2,1,0:T(8,128)S(1)} %slice_select_fusion.8), channel_id=1, source_target_pairs={{0,1},{1,0},{2,3},{3,2},{4,5},{5,4},{6,7},{7,6},{8,9},{9,8},{10,11... | collective-permute-start | bytes 786440 | tf_op jit(solution)/shard_map/ppermute | solution.py:29
  14.0 9.2 %collective-permute-done.2 = f32[224,256]{1,0:T(8,128)S(1)} collective-permute-done((f32[224,256]{1,0:T(8,128)S(1)}, f32[224,256]{1,0:T(8,128)S(1)}, u32[]{:S(2)}, u32[]{:S(2)}) %collective-permute-start.2) | collective-permute-done | bytes 229408 | tf_op jit(solution)/shard_map/ppermute | solution.py:29
  23.4 0.9 collective-permute-done.1
  24.4 1.3 %collective-permute-start.3 = (f32[2,2,32,256]{3,2,1,0:T(8,128)S(1)}, f32[2,2,32,256]{3,2,1,0:T(8,128)S(1)}, u32[]{:S(2)}, u32[]{:S(2)}) collective-permute-start(f32[2,2,32,256]{3,2,1,0:T(8,128)S(1)} %slice_select_fusion.9), channel_id=1, source_target_pairs={{0,2},{1,3},{2,0},{3,1},{4,6},{5,7},{6,4},{7,5},{8,10},{9,11},{10,... | collective-permute-start | bytes 393224 | tf_op jit(solution)/shard_map/ppermute | solution.py:29
  25.7 2.0 %collective-permute-start.4 = (f32[320,256]{1,0:T(8,128)S(1)}, f32[320,256]{1,0:T(8,128)S(1)}, u32[]{:S(2)}, u32[]{:S(2)}) collective-permute-start(f32[320,256]{1,0:T(8,128)S(1)} %pad_maximum_fusion.2), channel_id=1, source_target_pairs={{0,1},{1,0},{2,3},{3,2},{4,5},{5,4},{6,7},{7,6},{8,9},{9,8},{10,11... | collective-permute-start | bytes 983048 | tf_op jit(solution)/shard_map/ppermute | solution.py:29
  27.7 4.2 %collective-permute-done.3 = f32[2,2,32,256]{3,2,1,0:T(8,128)S(1)} collective-permute-done((f32[2,2,32,256]{3,2,1,0:T(8,128)S(1)}, f32[2,2,32,256]{3,2,1,0:T(8,128)S(1)}, u32[]{:S(2)}, u32[]{:S(2)}) %collective-permute-start.3) | collective-permute-done | bytes 131104 | tf_op jit(solution)/shard_map/ppermute | solution.py:29
  32.0 4.7 %collective-permute-done.4 = f32[320,256]{1,0:T(8,128)S(1)} collective-permute-done((f32[320,256]{1,0:T(8,128)S(1)}, f32[320,256]{1,0:T(8,128)S(1)}, u32[]{:S(2)}, u32[]{:S(2)}) %collective-permute-start.4) | collective-permute-done | bytes 327712 | tf_op jit(solution)/shard_map/ppermute | solution.py:29
  36.8 1.6 %collective-permute-start.5 = (f32[384,256]{1,0:T(8,128)S(1)}, f32[384,256]{1,0:T(8,128)S(1)}, u32[]{:S(2)}, u32[]{:S(2)}) collective-permute-start(f32[384,256]{1,0:T(8,128)S(1)} %pad_maximum_fusion.1), channel_id=1, source_target_pairs={{0,8},{4,12},{8,0},{12,4},{16,24},{20,28},{24,16},{28,20},{1,9},{5... | collective-permute-start | bytes 1179656 | tf_op jit(solution)/shard_map/ppermute | solution.py:29
  38.4 0.6 shard_map.75
  39.0 1.1 collective-permute-start.9
  40.1 2.6 %collective-permute-start.10 = (f32[128,256]{1,0:T(8,128)S(1)}, f32[128,256]{1,0:T(8,128)S(1)}, u32[]{:S(2)}, u32[]{:S(2)}) collective-permute-start(f32[128,256]{1,0:T(8,128)S(1)} %bitcast.131), channel_id=1, source_target_pairs={{0,2},{1,3},{2,0},{3,1},{4,6},{5,7},{6,4},{7,5},{8,10},{9,11},{10,... | collective-permute-start | bytes 393224 | tf_op jit(solution)/shard_map/ppermute | solution.py:29
  42.7 4.3 %collective-permute-done.5 = f32[384,256]{1,0:T(8,128)S(1)} collective-permute-done((f32[384,256]{1,0:T(8,128)S(1)}, f32[384,256]{1,0:T(8,128)S(1)}, u32[]{:S(2)}, u32[]{:S(2)}) %collective-permute-start.5) | collective-permute-done | bytes 393248 | tf_op jit(solution)/shard_map/ppermute | solution.py:29
  47.2 0.6 collective-permute-done.10
  47.8 1.6 %collective-permute-start.6 = (f32[2,32,256]{2,1,0:T(8,128)S(1)}, f32[2,32,256]{2,1,0:T(8,128)S(1)}, u32[]{:S(2)}, u32[]{:S(2)}) collective-permute-start(f32[2,32,256]{2,1,0:T(8,128)S(1)} %bitcast_add_fusion), channel_id=1, source_target_pairs={{0,16},{4,20},{8,24},{12,28},{16,0},{20,4},{24,8},{28,12},{1,17},{... | collective-permute-start | bytes 196616 | tf_op jit(solution)/shard_map/ppermute | solution.py:29
  49.4 2.3 %collective-permute-start.11 = (f32[256,256]{1,0:T(8,128)S(1)}, f32[256,256]{1,0:T(8,128)S(1)}, u32[]{:S(2)}, u32[]{:S(2)}) collective-permute-start(f32[256,256]{1,0:T(8,128)S(1)} %bitcast.117), channel_id=1, source_target_pairs={{0,1},{1,0},{2,3},{3,2},{4,5},{5,4},{6,7},{7,6},{8,9},{9,8},{10,11... | collective-permute-start | bytes 786440 | tf_op jit(solution)/shard_map/ppermute | solution.py:29
  52.1 1.2 shard_map.74
  53.4 3.4 %collective-permute-start.8 = (f32[2,2,32,256]{3,2,1,0:T(8,128)S(1)}, f32[2,2,32,256]{3,2,1,0:T(8,128)S(1)}, u32[]{:S(2)}, u32[]{:S(2)}) collective-permute-start(f32[2,2,32,256]{3,2,1,0:T(8,128)S(1)} %shard_map.74), channel_id=1, source_target_pairs={{0,2},{1,3},{2,0},{3,1},{4,6},{5,7},{6,4},{7,5},{8,10},{9,11},{10,... | collective-permute-start | bytes 393224 | tf_op jit(solution)/shard_map/ppermute | solution.py:29
  56.8 4.9 %collective-permute-done.8 = f32[2,2,32,256]{3,2,1,0:T(8,128)S(1)} collective-permute-done((f32[2,2,32,256]{3,2,1,0:T(8,128)S(1)}, f32[2,2,32,256]{3,2,1,0:T(8,128)S(1)}, u32[]{:S(2)}, u32[]{:S(2)}) %collective-permute-start.8) | collective-permute-done | bytes 131104 | tf_op jit(solution)/shard_map/ppermute | solution.py:29
  62.2 1.7 %collective-permute-start.12 = (f32[2,64,256]{2,1,0:T(8,128)S(1)}, f32[2,64,256]{2,1,0:T(8,128)S(1)}, u32[]{:S(2)}, u32[]{:S(2)}) collective-permute-start(f32[2,64,256]{2,1,0:T(8,128)S(1)} %get-tuple-element.104), channel_id=1, source_target_pairs={{0,1},{1,0},{2,3},{3,2},{4,5},{5,4},{6,7},{7,6},{8,9},{9,8},{10,11... | collective-permute-start | bytes 393224 | tf_op jit(solution)/shard_map/ppermute | solution.py:29
  63.9 2.9 %collective-permute-done.16 = f32[2,64,256]{2,1,0:T(8,128)S(1)} collective-permute-done((f32[2,64,256]{2,1,0:T(8,128)S(1)}, f32[2,64,256]{2,1,0:T(8,128)S(1)}, u32[]{:S(2)}, u32[]{:S(2)}) %collective-permute-start.16) | collective-permute-done | bytes 131104 | tf_op jit(solution)/shard_map/ppermute | solution.py:29
  66.9 1.3 %collective-permute-done.12 = f32[2,64,256]{2,1,0:T(8,128)S(1)} collective-permute-done((f32[2,64,256]{2,1,0:T(8,128)S(1)}, f32[2,64,256]{2,1,0:T(8,128)S(1)}, u32[]{:S(2)}, u32[]{:S(2)}) %collective-permute-start.12) | collective-permute-done | bytes 131104 | tf_op jit(solution)/shard_map/ppermute | solution.py:29
  68.5 2.6 %shard_map.77 = (f32[1024,256]{1,0:T(8,128)S(1)}, f32[256,256]{1,0:T(8,128)S(1)}, f32[256,256]{1,0:T(8,128)S(1)}) custom-call(s32[2]{0:T(128)S(1)} %pad_add_fusion.where_ref, f32[1024,512]{1,0:T(8,128)S(1)} %copy-done.5, f32[2,128,256]{2,1,0:T(8,128)S(1)} %maximum_select_fusion.11.own_ref, f32[2,128,256]{2,1,0:T(8,128)S(1)} %collective-permute-done.17.partner_ref, ...), custom_call_target="tpu_custom_call" | custom-call | flops 1610612736 | bytes 4194304 | tf_op jit(solution)/shard_map/pallas_call | solution.py:200
  71.1 0.7 collective-permute-start.18
  71.7 2.6 %shard_map.76 = (f32[1024,256]{1,0:T(8,128)S(1)}, f32[256,256]{1,0:T(8,128)S(1)}, f32[256,256]{1,0:T(8,128)S(1)}) custom-call(s32[2]{0:T(128)S(1)} %pad_add_fusion.where_ref, f32[1024,512]{1,0:T(8,128)S(1)} %copy-done.5, f32[2,128,256]{2,1,0:T(8,128)S(1)} %maximum_select_fusion.10.own_ref, f32[2,128,256]{2,1,0:T(8,128)S(1)} %collective-permute-done.13.partner_ref, ...), custom_call_target="tpu_custom_call" | custom-call | flops 1610612736 | bytes 4194304 | tf_op jit(solution)/shard_map/pallas_call | solution.py:200
  74.3 1.5 %collective-permute-start.14 = (f32[256,256]{1,0:T(8,128)S(1)}, f32[256,256]{1,0:T(8,128)S(1)}, u32[]{:S(2)}, u32[]{:S(2)}) collective-permute-start(f32[256,256]{1,0:T(8,128)S(1)} %get-tuple-element.64), channel_id=1, source_target_pairs={{0,1},{1,0},{2,3},{3,2},{4,5},{5,4},{6,7},{7,6},{8,9},{9,8},{10,11... | collective-permute-start | bytes 786440 | tf_op jit(solution)/shard_map/ppermute | solution.py:29
  75.9 4.4 %collective-permute-done.18 = f32[256,256]{1,0:T(8,128)S(1)} collective-permute-done((f32[256,256]{1,0:T(8,128)S(1)}, f32[256,256]{1,0:T(8,128)S(1)}, u32[]{:S(2)}, u32[]{:S(2)}) %collective-permute-start.18) | collective-permute-done | bytes 262176 | tf_op jit(solution)/shard_map/ppermute | solution.py:29
  80.3 1.5 %collective-permute-start.19 = (f32[128,256]{1,0:T(8,128)S(1)}, f32[128,256]{1,0:T(8,128)S(1)}, u32[]{:S(2)}, u32[]{:S(2)}) collective-permute-start(f32[128,256]{1,0:T(8,128)S(1)} %slice.117), channel_id=1, source_target_pairs={{0,2},{1,3},{2,0},{3,1},{4,6},{5,7},{6,4},{7,5},{8,10},{9,11},{10,... | collective-permute-start | bytes 393224 | tf_op jit(solution)/shard_map/ppermute | solution.py:29
  81.8 1.5 %collective-permute-start.24 = (f32[256,256]{1,0:T(8,128)S(1)}, f32[256,256]{1,0:T(8,128)S(1)}, u32[]{:S(2)}, u32[]{:S(2)}) collective-permute-start(f32[256,256]{1,0:T(8,128)S(1)} %bitcast.120), channel_id=1, source_target_pairs={{0,1},{1,0},{2,3},{3,2},{4,5},{5,4},{6,7},{7,6},{8,9},{9,8},{10,11... | collective-permute-start | bytes 786440 | tf_op jit(solution)/shard_map/ppermute | solution.py:29
  83.4 5.3 %collective-permute-done.14 = f32[256,256]{1,0:T(8,128)S(1)} collective-permute-done((f32[256,256]{1,0:T(8,128)S(1)}, f32[256,256]{1,0:T(8,128)S(1)}, u32[]{:S(2)}, u32[]{:S(2)}) %collective-permute-start.14) | collective-permute-done | bytes 262176 | tf_op jit(solution)/shard_map/ppermute | solution.py:29
  89.1 1.2 collective-permute-done.20.upper_other
  90.3 0.6 shard_map.78
  90.9 4.1 %collective-permute-done.15 = f32[128,256]{1,0:T(8,128)S(1)} collective-permute-done((f32[128,256]{1,0:T(8,128)S(1)}, f32[128,256]{1,0:T(8,128)S(1)}, u32[]{:S(2)}, u32[]{:S(2)}) %collective-permute-start.15) | collective-permute-done | bytes 131104 | tf_op jit(solution)/shard_map/ppermute | solution.py:29
  95.1 1.6 %collective-permute-done.24 = f32[256,256]{1,0:T(8,128)S(1)} collective-permute-done((f32[256,256]{1,0:T(8,128)S(1)}, f32[256,256]{1,0:T(8,128)S(1)}, u32[]{:S(2)}, u32[]{:S(2)}) %collective-permute-start.24) | collective-permute-done | bytes 262176 | tf_op jit(solution)/shard_map/ppermute | solution.py:29
  96.7 1.8 %collective-permute-start.23 = (f32[128,256]{1,0:T(8,128)S(1)}, f32[128,256]{1,0:T(8,128)S(1)}, u32[]{:S(2)}, u32[]{:S(2)}) collective-permute-start(f32[128,256]{1,0:T(8,128)S(1)} %get-tuple-element.70.own), channel_id=1, source_target_pairs={{0,2},{1,3},{2,0},{3,1},{4,6},{5,7},{6,4},{7,5},{8,10},{9,11},{10,... | collective-permute-start | bytes 393224 | tf_op jit(solution)/shard_map/ppermute | solution.py:29
  98.5 0.6 shard_map.79
  99.2 1.3 %collective-permute-start.22 = (f32[128,256]{1,0:T(8,128)S(1)}, f32[128,256]{1,0:T(8,128)S(1)}, u32[]{:S(2)}, u32[]{:S(2)}) collective-permute-start(f32[128,256]{1,0:T(8,128)S(1)} %get-tuple-element.73.own), channel_id=1, source_target_pairs={{0,2},{1,3},{2,0},{3,1},{4,6},{5,7},{6,4},{7,5},{8,10},{9,11},{10,... | collective-permute-start | bytes 393224 | tf_op jit(solution)/shard_map/ppermute | solution.py:29
  100.5 8.8 %collective-permute-done.23.sibling = f32[128,256]{1,0:T(8,128)S(1)} collective-permute-done((f32[128,256]{1,0:T(8,128)S(1)}, f32[128,256]{1,0:T(8,128)S(1)}, u32[]{:S(2)}, u32[]{:S(2)}) %collective-permute-start.23) | collective-permute-done | bytes 131104 | tf_op jit(solution)/shard_map/ppermute | solution.py:29
  109.8 1.5 %collective-permute-done.22.sibling = f32[128,256]{1,0:T(8,128)S(1)} collective-permute-done((f32[128,256]{1,0:T(8,128)S(1)}, f32[128,256]{1,0:T(8,128)S(1)}, u32[]{:S(2)}, u32[]{:S(2)}) %collective-permute-start.22) | collective-permute-done | bytes 131104 | tf_op jit(solution)/shard_map/ppermute | solution.py:29
  111.7 0.6 collective-permute-start.25
  112.3 6.5 %collective-permute-done.26.partner_ref = f32[2,128,256]{2,1,0:T(8,128)S(1)} collective-permute-done((f32[2,128,256]{2,1,0:T(8,128)S(1)}, f32[2,128,256]{2,1,0:T(8,128)S(1)}, u32[]{:S(2)}, u32[]{:S(2)}) %collective-permute-start.26) | collective-permute-done | bytes 262176 | tf_op jit(solution)/shard_map/ppermute | solution.py:29
  118.7 1.9 %shard_map.82.refs_0_ = f32[1024,512]{1,0:T(8,128)} custom-call(s32[1]{0:T(128)} %bitcast.where_ref, f32[1024,256]{1,0:T(8,128)S(1)} %get-tuple-element.75.x_ref, f32[2,128,256]{2,1,0:T(8,128)S(1)} %shard_map.80.own_ref, f32[2,128,256]{2,1,0:T(8,128)S(1)} %collective-permute-done.26.partner_ref, f32[4,1024,256]{2,1,0:T(8,128)S(1)} %copy-done.1), custom_call_target="tpu_custom_call" | custom-call | flops 805306368 | bytes 3145728 | tf_op jit(solution)/shard_map/pallas_call | solution.py:232
  120.7 1.1 collective-permute-done.25.partner_ref
  121.8 1.9 %shard_map.83 = f32[1024,512]{1,0:T(8,128)} custom-call(s32[1]{0:T(128)} %bitcast.where_ref, f32[1024,256]{1,0:T(8,128)S(1)} %get-tuple-element.62.x_ref, f32[2,128,256]{2,1,0:T(8,128)S(1)} %shard_map.81.own_ref, f32[2,128,256]{2,1,0:T(8,128)S(1)} %collective-permute-done.25.partner_ref, ...), custom_call_target="tpu_custom_call", output_to_operand_aliasing={{}: (5, {})} | custom-call | flops 805306368 | bytes 3145728 | tf_op jit(solution)/shard_map/pallas_call | solution.py:232
  (98 shorter events, 3.3 us)
Async XLA Ops:
  0.0 1.6 %copy-start.4 = (f32[1024,512]{1,0:T(8,128)S(1)}, f32[1024,512]{1,0:T(8,128)}, u32[]{:S(2)}) copy-start(f32[1024,512]{1,0:T(8,128)} %old_ref.1) | copy-start | bytes 6291460
  1.6 4.8 %copy-start.9 = (f32[16,512]{1,0:T(8,128)S(1)}, f32[16,512]{1,0:T(8,128)}, u32[]{:S(2)}) copy-start(f32[16,512]{1,0:T(8,128)} %param.10) | copy-start | bytes 98308
  1.6 4.9 %copy-start.8 = (f32[32,512]{1,0:T(8,128)S(1)}, f32[32,512]{1,0:T(8,128)}, u32[]{:S(2)}) copy-start(f32[32,512]{1,0:T(8,128)} %param.11) | copy-start | bytes 196612
  1.6 4.9 %copy-start.7 = (f32[64,512]{1,0:T(8,128)S(1)}, f32[64,512]{1,0:T(8,128)}, u32[]{:S(2)}) copy-start(f32[64,512]{1,0:T(8,128)} %param.12) | copy-start | bytes 393220
  5.9 2.2 %collective-permute-start = (f32[640,256]{1,0:T(8,128)S(1)}, f32[640,256]{1,0:T(8,128)S(1)}, u32[]{:S(2)}, u32[]{:S(2)}) collective-permute-start(f32[640,256]{1,0:T(8,128)S(1)} %get-tuple-element.41), channel_id=1, source_target_pairs={{0,4},{4,0},{8,12},{12,8},{16,20},{20,16},{24,28},{28,24},{1,5},{5... | collective-permute-start | bytes 1966088 | tf_op jit(solution)/shard_map/ppermute | solution.py:29
  8.2 30.1 %copy-start.2 = (f32[4,1024,256]{2,1,0:T(8,128)S(1)}, f32[4,1024,256]{2,1,0:T(8,128)}, u32[]{:S(2)}) copy-start(f32[4,1024,256]{2,1,0:T(8,128)} %v_ref.2) | copy-start | bytes 12582916
  8.3 14.9 %collective-permute-start.2 = (f32[224,256]{1,0:T(8,128)S(1)}, f32[224,256]{1,0:T(8,128)S(1)}, u32[]{:S(2)}, u32[]{:S(2)}) collective-permute-start(f32[224,256]{1,0:T(8,128)S(1)} %pad_maximum_fusion.5), channel_id=1, source_target_pairs={{0,2},{1,3},{2,0},{3,1},{4,6},{5,7},{6,4},{7,5},{8,10},{9,11},{10,... | collective-permute-start | bytes 688136 | tf_op jit(solution)/shard_map/ppermute | solution.py:29
  12.4 11.9 %collective-permute-start.1 = (f32[2,2,64,256]{3,2,1,0:T(8,128)S(1)}, f32[2,2,64,256]{3,2,1,0:T(8,128)S(1)}, u32[]{:S(2)}, u32[]{:S(2)}) collective-permute-start(f32[2,2,64,256]{3,2,1,0:T(8,128)S(1)} %slice_select_fusion.8), channel_id=1, source_target_pairs={{0,1},{1,0},{2,3},{3,2},{4,5},{5,4},{6,7},{7,6},{8,9},{9,8},{10,11... | collective-permute-start | bytes 786440 | tf_op jit(solution)/shard_map/ppermute | solution.py:29
  24.3 14.1 %copy-start = (f32[4,1024,256]{2,1,0:T(8,128)S(1)}, f32[4,1024,256]{2,1,0:T(8,128)}, u32[]{:S(2)}) copy-start(f32[4,1024,256]{2,1,0:T(8,128)} %u_ref.4) | copy-start | bytes 12582916
  24.4 7.6 %collective-permute-start.3 = (f32[2,2,32,256]{3,2,1,0:T(8,128)S(1)}, f32[2,2,32,256]{3,2,1,0:T(8,128)S(1)}, u32[]{:S(2)}, u32[]{:S(2)}) collective-permute-start(f32[2,2,32,256]{3,2,1,0:T(8,128)S(1)} %slice_select_fusion.9), channel_id=1, source_target_pairs={{0,2},{1,3},{2,0},{3,1},{4,6},{5,7},{6,4},{7,5},{8,10},{9,11},{10,... | collective-permute-start | bytes 393224 | tf_op jit(solution)/shard_map/ppermute | solution.py:29
  25.7 10.9 %collective-permute-start.4 = (f32[320,256]{1,0:T(8,128)S(1)}, f32[320,256]{1,0:T(8,128)S(1)}, u32[]{:S(2)}, u32[]{:S(2)}) collective-permute-start(f32[320,256]{1,0:T(8,128)S(1)} %pad_maximum_fusion.2), channel_id=1, source_target_pairs={{0,1},{1,0},{2,3},{3,2},{4,5},{5,4},{6,7},{7,6},{8,9},{9,8},{10,11... | collective-permute-start | bytes 983048 | tf_op jit(solution)/shard_map/ppermute | solution.py:29
  36.8 10.1 %collective-permute-start.5 = (f32[384,256]{1,0:T(8,128)S(1)}, f32[384,256]{1,0:T(8,128)S(1)}, u32[]{:S(2)}, u32[]{:S(2)}) collective-permute-start(f32[384,256]{1,0:T(8,128)S(1)} %pad_maximum_fusion.1), channel_id=1, source_target_pairs={{0,8},{4,12},{8,0},{12,4},{16,24},{20,28},{24,16},{28,20},{1,9},{5... | collective-permute-start | bytes 1179656 | tf_op jit(solution)/shard_map/ppermute | solution.py:29
  39.0 22.8 %collective-permute-start.9 = (f32[256,256]{1,0:T(8,128)S(1)}, f32[256,256]{1,0:T(8,128)S(1)}, u32[]{:S(2)}, u32[]{:S(2)}) collective-permute-start(f32[256,256]{1,0:T(8,128)S(1)} %shard_map.75), channel_id=1, source_target_pairs={{0,1},{1,0},{2,3},{3,2},{4,5},{5,4},{6,7},{7,6},{8,9},{9,8},{10,11... | collective-permute-start | bytes 786440 | tf_op jit(solution)/shard_map/ppermute | solution.py:29
  40.1 7.7 %collective-permute-start.10 = (f32[128,256]{1,0:T(8,128)S(1)}, f32[128,256]{1,0:T(8,128)S(1)}, u32[]{:S(2)}, u32[]{:S(2)}) collective-permute-start(f32[128,256]{1,0:T(8,128)S(1)} %bitcast.131), channel_id=1, source_target_pairs={{0,2},{1,3},{2,0},{3,1},{4,6},{5,7},{6,4},{7,5},{8,10},{9,11},{10,... | collective-permute-start | bytes 393224 | tf_op jit(solution)/shard_map/ppermute | solution.py:29
  47.1 4.7 %collective-permute-start.7 = (f32[768,256]{1,0:T(8,128)S(1)}, f32[768,256]{1,0:T(8,128)S(1)}, u32[]{:S(2)}, u32[]{:S(2)}) collective-permute-start(f32[768,256]{1,0:T(8,128)S(1)} %pad_maximum_fusion), channel_id=1, source_target_pairs={{0,4},{4,0},{8,12},{12,8},{16,20},{20,16},{24,28},{28,24},{1,5},{5... | collective-permute-start | bytes 2359304 | tf_op jit(solution)/shard_map/ppermute | solution.py:29
  47.8 4.3 %collective-permute-start.6 = (f32[2,32,256]{2,1,0:T(8,128)S(1)}, f32[2,32,256]{2,1,0:T(8,128)S(1)}, u32[]{:S(2)}, u32[]{:S(2)}) collective-permute-start(f32[2,32,256]{2,1,0:T(8,128)S(1)} %bitcast_add_fusion), channel_id=1, source_target_pairs={{0,16},{4,20},{8,24},{12,28},{16,0},{20,4},{24,8},{28,12},{1,17},{... | collective-permute-start | bytes 196616 | tf_op jit(solution)/shard_map/ppermute | solution.py:29
  49.4 12.4 %collective-permute-start.11 = (f32[256,256]{1,0:T(8,128)S(1)}, f32[256,256]{1,0:T(8,128)S(1)}, u32[]{:S(2)}, u32[]{:S(2)}) collective-permute-start(f32[256,256]{1,0:T(8,128)S(1)} %bitcast.117), channel_id=1, source_target_pairs={{0,1},{1,0},{2,3},{3,2},{4,5},{5,4},{6,7},{7,6},{8,9},{9,8},{10,11... | collective-permute-start | bytes 786440 | tf_op jit(solution)/shard_map/ppermute | solution.py:29
  51.7 16.7 %copy-start.5 = (f32[1024,512]{1,0:T(8,128)S(1)}, f32[1024,512]{1,0:T(8,128)}, u32[]{:S(2)}) copy-start(f32[1024,512]{1,0:T(8,128)} %old_ref.1) | copy-start | bytes 6291460
  51.9 16.6 %copy-start.3 = (f32[4,1024,256]{2,1,0:T(8,128)S(1)}, f32[4,1024,256]{2,1,0:T(8,128)}, u32[]{:S(2)}) copy-start(f32[4,1024,256]{2,1,0:T(8,128)} %v_ref.2) | copy-start | bytes 12582916
  52.1 16.4 %copy-start.1 = (f32[4,1024,256]{2,1,0:T(8,128)S(1)}, f32[4,1024,256]{2,1,0:T(8,128)}, u32[]{:S(2)}) copy-start(f32[4,1024,256]{2,1,0:T(8,128)} %u_ref.4) | copy-start | bytes 12582916
  53.4 8.4 %collective-permute-start.8 = (f32[2,2,32,256]{3,2,1,0:T(8,128)S(1)}, f32[2,2,32,256]{3,2,1,0:T(8,128)S(1)}, u32[]{:S(2)}, u32[]{:S(2)}) collective-permute-start(f32[2,2,32,256]{3,2,1,0:T(8,128)S(1)} %shard_map.74), channel_id=1, source_target_pairs={{0,2},{1,3},{2,0},{3,1},{4,6},{5,7},{6,4},{7,5},{8,10},{9,11},{10,... | collective-permute-start | bytes 393224 | tf_op jit(solution)/shard_map/ppermute | solution.py:29
  61.8 5.0 %collective-permute-start.16 = (f32[2,64,256]{2,1,0:T(8,128)S(1)}, f32[2,64,256]{2,1,0:T(8,128)S(1)}, u32[]{:S(2)}, u32[]{:S(2)}) collective-permute-start(f32[2,64,256]{2,1,0:T(8,128)S(1)} %get-tuple-element.103), channel_id=1, source_target_pairs={{0,1},{1,0},{2,3},{3,2},{4,5},{5,4},{6,7},{7,6},{8,9},{9,8},{10,11... | collective-permute-start | bytes 393224 | tf_op jit(solution)/shard_map/ppermute | solution.py:29
  62.2 6.1 %collective-permute-start.12 = (f32[2,64,256]{2,1,0:T(8,128)S(1)}, f32[2,64,256]{2,1,0:T(8,128)S(1)}, u32[]{:S(2)}, u32[]{:S(2)}) collective-permute-start(f32[2,64,256]{2,1,0:T(8,128)S(1)} %get-tuple-element.104), channel_id=1, source_target_pairs={{0,1},{1,0},{2,3},{3,2},{4,5},{5,4},{6,7},{7,6},{8,9},{9,8},{10,11... | collective-permute-start | bytes 393224 | tf_op jit(solution)/shard_map/ppermute | solution.py:29
  66.9 1.6 %collective-permute-start.17 = (f32[2,128,256]{2,1,0:T(8,128)S(1)}, f32[2,128,256]{2,1,0:T(8,128)S(1)}, u32[]{:S(2)}, u32[]{:S(2)}) collective-permute-start(f32[2,128,256]{2,1,0:T(8,128)S(1)} %maximum_select_fusion.11.own_ref), channel_id=1, source_target_pairs={{0,4},{4,0},{8,12},{12,8},{16,20},{20,16},{24,28},{28,24},{1,5},{5... | collective-permute-start | bytes 786440 | tf_op jit(solution)/shard_map/ppermute | solution.py:29
  68.3 3.5 %collective-permute-start.13 = (f32[2,128,256]{2,1,0:T(8,128)S(1)}, f32[2,128,256]{2,1,0:T(8,128)S(1)}, u32[]{:S(2)}, u32[]{:S(2)}) collective-permute-start(f32[2,128,256]{2,1,0:T(8,128)S(1)} %maximum_select_fusion.10.own_ref), channel_id=1, source_target_pairs={{0,4},{4,0},{8,12},{12,8},{16,20},{20,16},{24,28},{28,24},{1,5},{5... | collective-permute-start | bytes 786440 | tf_op jit(solution)/shard_map/ppermute | solution.py:29
  71.1 4.8 %copy-start.6 = (f32[128,512]{1,0:T(8,128)S(1)}, f32[128,512]{1,0:T(8,128)}, u32[]{:S(2)}) copy-start(f32[128,512]{1,0:T(8,128)} %param.13) | copy-start | bytes 786436
  71.1 9.2 %collective-permute-start.18 = (f32[256,256]{1,0:T(8,128)S(1)}, f32[256,256]{1,0:T(8,128)S(1)}, u32[]{:S(2)}, u32[]{:S(2)}) collective-permute-start(f32[256,256]{1,0:T(8,128)S(1)} %get-tuple-element.66), channel_id=1, source_target_pairs={{0,1},{1,0},{2,3},{3,2},{4,5},{5,4},{6,7},{7,6},{8,9},{9,8},{10,11... | collective-permute-start | bytes 786440 | tf_op jit(solution)/shard_map/ppermute | solution.py:29
  74.3 14.4 %collective-permute-start.14 = (f32[256,256]{1,0:T(8,128)S(1)}, f32[256,256]{1,0:T(8,128)S(1)}, u32[]{:S(2)}, u32[]{:S(2)}) collective-permute-start(f32[256,256]{1,0:T(8,128)S(1)} %get-tuple-element.64), channel_id=1, source_target_pairs={{0,1},{1,0},{2,3},{3,2},{4,5},{5,4},{6,7},{7,6},{8,9},{9,8},{10,11... | collective-permute-start | bytes 786440 | tf_op jit(solution)/shard_map/ppermute | solution.py:29
  80.3 8.5 %collective-permute-start.19 = (f32[128,256]{1,0:T(8,128)S(1)}, f32[128,256]{1,0:T(8,128)S(1)}, u32[]{:S(2)}, u32[]{:S(2)}) collective-permute-start(f32[128,256]{1,0:T(8,128)S(1)} %slice.117), channel_id=1, source_target_pairs={{0,2},{1,3},{2,0},{3,1},{4,6},{5,7},{6,4},{7,5},{8,10},{9,11},{10,... | collective-permute-start | bytes 393224 | tf_op jit(solution)/shard_map/ppermute | solution.py:29
  81.8 14.9 %collective-permute-start.24 = (f32[256,256]{1,0:T(8,128)S(1)}, f32[256,256]{1,0:T(8,128)S(1)}, u32[]{:S(2)}, u32[]{:S(2)}) collective-permute-start(f32[256,256]{1,0:T(8,128)S(1)} %bitcast.120), channel_id=1, source_target_pairs={{0,1},{1,0},{2,3},{3,2},{4,5},{5,4},{6,7},{7,6},{8,9},{9,8},{10,11... | collective-permute-start | bytes 786440 | tf_op jit(solution)/shard_map/ppermute | solution.py:29
  88.7 6.3 %collective-permute-start.15 = (f32[128,256]{1,0:T(8,128)S(1)}, f32[128,256]{1,0:T(8,128)S(1)}, u32[]{:S(2)}, u32[]{:S(2)}) collective-permute-start(f32[128,256]{1,0:T(8,128)S(1)} %slice.116), channel_id=1, source_target_pairs={{0,2},{1,3},{2,0},{3,1},{4,6},{5,7},{6,4},{7,5},{8,10},{9,11},{10,... | collective-permute-start | bytes 393224 | tf_op jit(solution)/shard_map/ppermute | solution.py:29
  88.9 1.4 %collective-permute-start.20 = (f32[128,256]{1,0:T(8,128)S(1)}, f32[128,256]{1,0:T(8,128)S(1)}, u32[]{:S(2)}, u32[]{:S(2)}) collective-permute-start(f32[128,256]{1,0:T(8,128)S(1)} %get-tuple-element.102.upper), channel_id=1, source_target_pairs={{0,4},{4,0},{8,12},{12,8},{16,20},{20,16},{24,28},{28,24},{1,5},{5... | collective-permute-start | bytes 393224 | tf_op jit(solution)/shard_map/ppermute | solution.py:29
  95.0 3.5 %collective-permute-start.21 = (f32[128,256]{1,0:T(8,128)S(1)}, f32[128,256]{1,0:T(8,128)S(1)}, u32[]{:S(2)}, u32[]{:S(2)}) collective-permute-start(f32[128,256]{1,0:T(8,128)S(1)} %get-tuple-element.100.upper), channel_id=1, source_target_pairs={{0,4},{4,0},{8,12},{12,8},{16,20},{20,16},{24,28},{28,24},{1,5},{5... | collective-permute-start | bytes 393224 | tf_op jit(solution)/shard_map/ppermute | solution.py:29
  96.7 12.6 %collective-permute-start.23 = (f32[128,256]{1,0:T(8,128)S(1)}, f32[128,256]{1,0:T(8,128)S(1)}, u32[]{:S(2)}, u32[]{:S(2)}) collective-permute-start(f32[128,256]{1,0:T(8,128)S(1)} %get-tuple-element.70.own), channel_id=1, source_target_pairs={{0,2},{1,3},{2,0},{3,1},{4,6},{5,7},{6,4},{7,5},{8,10},{9,11},{10,... | collective-permute-start | bytes 393224 | tf_op jit(solution)/shard_map/ppermute | solution.py:29
  99.2 12.1 %collective-permute-start.22 = (f32[128,256]{1,0:T(8,128)S(1)}, f32[128,256]{1,0:T(8,128)S(1)}, u32[]{:S(2)}, u32[]{:S(2)}) collective-permute-start(f32[128,256]{1,0:T(8,128)S(1)} %get-tuple-element.73.own), channel_id=1, source_target_pairs={{0,2},{1,3},{2,0},{3,1},{4,6},{5,7},{6,4},{7,5},{8,10},{9,11},{10,... | collective-permute-start | bytes 393224 | tf_op jit(solution)/shard_map/ppermute | solution.py:29
  109.7 9.0 %collective-permute-start.26 = (f32[2,128,256]{2,1,0:T(8,128)S(1)}, f32[2,128,256]{2,1,0:T(8,128)S(1)}, u32[]{:S(2)}, u32[]{:S(2)}) collective-permute-start(f32[2,128,256]{2,1,0:T(8,128)S(1)} %shard_map.80.own_ref), channel_id=1, source_target_pairs={{0,1},{1,0},{2,3},{3,2},{4,5},{5,4},{6,7},{7,6},{8,9},{9,8},{10,11... | collective-permute-start | bytes 786440 | tf_op jit(solution)/shard_map/ppermute | solution.py:29
  111.7 10.1 %collective-permute-start.25 = (f32[2,128,256]{2,1,0:T(8,128)S(1)}, f32[2,128,256]{2,1,0:T(8,128)S(1)}, u32[]{:S(2)}, u32[]{:S(2)}) collective-permute-start(f32[2,128,256]{2,1,0:T(8,128)S(1)} %shard_map.81.own_ref), channel_id=1, source_target_pairs={{0,1},{1,0},{2,3},{3,2},{4,5},{5,4},{6,7},{7,6},{8,9},{9,8},{10,11... | collective-permute-start | bytes 786440 | tf_op jit(solution)/shard_map/ppermute | solution.py:29
